TPU v7x, 32 devices: a whole 2x2x4 slice. The times are simulated.
32 devices in a mesh: dp: 8 (over y, x, core), mp: 4 (over z).
Axes of the slice: x: 2, y: 2, z: 4, core: 2. Of those that a mesh axis runs over, the one named last changes fastest.
Arguments:
- tokens: bfloat16 [24576, 768], P(('dp', 'mp'))
- out_cotangent: bfloat16 [24576, 768], P(('dp', 'mp')), may hold values from -6 to 6
- lengths: int32 [24], P('dp'), may hold values from 256 to 1024, as said below
- starts: int32 [24], P('dp'), may hold values from 0 to 1023, as said below
- ends: int32 [24], P('dp'), may hold values from 0 to 1023, as said below
- flags: int32 [24], P('dp'), may hold values 0 or 1
- qkv_master: float32 [3, 768, 768], P(None, 'dp', 'mp')
- proj_master: float32 [768, 768], P('mp', 'dp')
- up_master: float32 [768, 3072], P('dp', 'mp')
- down_master: float32 [3072, 768], P('mp', 'dp')
- vectors: float32 [12, 768], replicated
- qkv_first: float32 [3, 768, 768], P(None, 'dp', 'mp'), may hold values from -0.00024414062 to 0.00024414062
- proj_first: float32 [768, 768], P('mp', 'dp'), may hold values from -0.00024414062 to 0.00024414062
- up_first: float32 [768, 3072], P('dp', 'mp'), may hold values from -0.00024414062 to 0.00024414062
- down_first: float32 [3072, 768], P('mp', 'dp'), may hold values from -0.00024414062 to 0.00024414062
- qkv_second: float32 [3, 768, 768], P(None, 'dp', 'mp'), may hold values from 1.4128508e-10 to 5.651403e-10
- proj_second: float32 [768, 768], P('mp', 'dp'), may hold values from 1.4128508e-10 to 5.651403e-10
- up_second: float32 [768, 3072], P('dp', 'mp'), may hold values from 1.4128508e-10 to 5.651403e-10
- down_second: float32 [3072, 768], P('mp', 'dp'), may hold values from 1.4128508e-10 to 5.651403e-10
- vector_first: float32 [12, 768], P(None, ('dp', 'mp')), may hold values from -0.0008544922 to 0.0008544922
- vector_second: float32 [12, 768], P(None, ('dp', 'mp')), may hold values from 1.4128508e-09 to 5.6514033e-09
Outputs:
- block_out: bfloat16 [24576, 768], P(('dp', 'mp'))
- input_grad: float32 [24576, 768], P(('dp', 'mp'))
- grad_norm: float32 [], replicated
- qkv_grad: float32 [3, 768, 768], P(None, 'dp', 'mp')
- qkv_first_new: float32 [3, 768, 768], P(None, 'dp', 'mp')
- qkv_second_new: float32 [3, 768, 768], P(None, 'dp', 'mp')
- qkv_new: float32 [3, 768, 768], P(None, 'dp', 'mp')
- proj_grad: float32 [768, 768], P('mp', 'dp')
- proj_first_new: float32 [768, 768], P('mp', 'dp')
- proj_second_new: float32 [768, 768], P('mp', 'dp')
- proj_new: float32 [768, 768], P('mp', 'dp')
- up_grad: float32 [768, 3072], P('dp', 'mp')
- up_first_new: float32 [768, 3072], P('dp', 'mp')
- up_second_new: float32 [768, 3072], P('dp', 'mp')
- up_new: float32 [768, 3072], P('dp', 'mp')
- down_grad: float32 [3072, 768], P('mp', 'dp')
- down_first_new: float32 [3072, 768], P('mp', 'dp')
- down_second_new: float32 [3072, 768], P('mp', 'dp')
- down_new: float32 [3072, 768], P('mp', 'dp')
- vector_grad: float32 [12, 768], P(None, ('dp', 'mp'))
- vector_first_new: float32 [12, 768], P(None, ('dp', 'mp'))
- vector_second_new: float32 [12, 768], P(None, ('dp', 'mp'))
- vector_new: float32 [12, 768], P(None, ('dp', 'mp'))
Inputs may be any that keep to these rules, and one draw needn't show every extreme that they name: `lengths`: each length is at least 256; in every aligned block of 3 sequences one sequence is longer than 768; one sequence of all has length exactly 1024, and its start and end are both 1024 - 1. Each start lies below its sequence's length; the sequence of length exactly 1024 starts at 1023. Each end is at least its start, fewer than 32 positions after it, and below its sequence's length; the sequence of length exactly 1024 ends at 1023.
All inputs are finite; a program needn't handle non-finite values. No bound on the sum of `flags` on one device may be relied on, other than what follows from the above.
Results may differ from a plain program's by a relative error of at most 0.025.
Values may be sent and summed in bfloat16 or wider, within the bound.
No kernel may reach another device: no remote copies, remote signals or barrier semaphores. Data moves between devices by JAX's collectives and lax.ppermute only.
A program may use at most 192 MiB of HBM per device.

v0:
```python
from functools import partial
import math

import jax
import jax.numpy as jnp
from jax import lax
from jax.sharding import PartitionSpec as P

D = 768
HEADS = 12
HDIM = 64
FF = 3072
LEN = 1024
STEP = 10


LN_EPS = 1e-06
BETA_ONE = 0.9
BETA_TWO = 0.999
ADAM_EPS = 1e-08
WEIGHT_DECAY = 0.01
CLIP_NORM = 1.0
VECTOR_RATE = 1.0
MATRIX_RATE = 2.0
NEG_FILL = -1e30


def layer_norm(summed, gain_row, offset_row):
    average = jnp.mean(summed, -1, keepdims=True)
    centered = summed - average
    variance = jnp.mean(centered * centered, -1, keepdims=True)
    return centered * lax.rsqrt(variance + LN_EPS) * gain_row + offset_row


def contract_rows(left, right):
    return lax.dot_general(
        left, right, (((0,), (0,)), ((), ())), preferred_element_type=jnp.float32
    )


def contract_cols(left, right):
    return lax.dot_general(
        left, right, (((1,), (1,)), ((), ())), preferred_element_type=jnp.float32
    )


def adamw(weight, grad, first, second, rate, decay, clip_factor):
    clipped = grad * clip_factor
    first_new = BETA_ONE * first + (1.0 - BETA_ONE) * clipped
    second_new = BETA_TWO * second + (1.0 - BETA_TWO) * clipped * clipped
    first_hat = first_new / (1.0 - BETA_ONE**STEP)
    second_hat = second_new / (1.0 - BETA_TWO**STEP)
    updated = weight * (1.0 - rate * decay) - rate * first_hat / (jnp.sqrt(second_hat) + ADAM_EPS)
    return (clipped, first_new, second_new, updated)


def shards(
    tokens,
    out_cotangent,
    lengths,
    starts,
    ends,
    flags,
    qkv_master,
    proj_master,
    up_master,
    down_master,
    vectors,
    qkv_first,
    proj_first,
    up_first,
    down_first,
    qkv_second,
    proj_second,
    up_second,
    down_second,
    vector_first,
    vector_second,
):
    mp_count = lax.axis_size("mp")
    dp_count = lax.axis_size("dp")
    mp_index = lax.axis_index("mp")
    dp_index = lax.axis_index("dp")
    local_rows = tokens.shape[0]
    group_rows = local_rows * mp_count
    seq_here = group_rows // LEN
    width_here = HEADS // mp_count * HDIM
    heads_here = HEADS // mp_count
    ff_here = FF // mp_count
    block_rows = min(512, LEN)
    blocks_seq = LEN // block_rows
    block_total = seq_here * blocks_seq
    scaling = HDIM ** (-0.5)
    qkv_w, proj_w, up_w, down_w = (
        lax.all_gather(qkv_master.astype(jnp.bfloat16), "dp", axis=1, tiled=True),
        lax.all_gather(proj_master.astype(jnp.bfloat16), "dp", axis=1, tiled=True),
        lax.all_gather(up_master.astype(jnp.bfloat16), "dp", axis=0, tiled=True),
        lax.all_gather(down_master.astype(jnp.bfloat16), "dp", axis=1, tiled=True),
    )
    bias_query = lax.dynamic_slice_in_dim(vectors[0], mp_index * width_here, width_here)
    bias_value = lax.dynamic_slice_in_dim(vectors[1], mp_index * width_here, width_here)
    bias_proj = vectors[2]
    gain_one = vectors[3]
    offset_one = vectors[4]
    bias_down = vectors[5]
    gain_two = vectors[6]
    offset_two = vectors[7]
    bias_up_whole = vectors[8:].reshape(FF)
    bias_up = lax.dynamic_slice_in_dim(bias_up_whole, mp_index * ff_here, ff_here)
    whole_x = lax.all_gather(tokens, "mp", axis=0, tiled=True)
    queries = (jnp.dot(whole_x, qkv_w[0], preferred_element_type=jnp.float32) + bias_query).astype(
        jnp.bfloat16
    )
    keys_all = jnp.dot(whole_x, qkv_w[1], preferred_element_type=jnp.float32).astype(jnp.bfloat16)
    values_all = (
        jnp.dot(whole_x, qkv_w[2], preferred_element_type=jnp.float32) + bias_value
    ).astype(jnp.bfloat16)
    shaped = (seq_here, LEN, heads_here, HDIM)
    query_seq = queries.reshape(shaped)
    key_seq = keys_all.reshape(shaped)
    value_seq = values_all.reshape(shaped)
    valid_keys = jnp.arange(LEN, dtype=jnp.int32)[None, :] < lengths[:, None]
    block_ids = jnp.arange(block_total, dtype=jnp.int32)

    def block_scores(position):
        seq_pick = position // blocks_seq
        block_pick = position % blocks_seq
        query_block = lax.dynamic_slice_in_dim(
            query_seq[seq_pick], block_pick * block_rows, block_rows, 0
        )
        key_block = key_seq[seq_pick]
        raw = jnp.einsum("qhd,khd->hqk", query_block, key_block, preferred_element_type=jnp.float32)
        masked = jnp.where(valid_keys[seq_pick][None, None, :], raw * scaling, NEG_FILL)
        return (query_block, key_block, masked)

    def attend_block(position):
        seq_pick = position // blocks_seq
        query_block, key_block, masked = block_scores(position)
        row_peak = jnp.max(masked, -1, keepdims=True)
        exponent = jnp.exp(masked - row_peak)
        row_total = jnp.sum(exponent, -1, keepdims=True)
        probs = (exponent / row_total).astype(jnp.bfloat16)
        attended = jnp.einsum(
            "hqk,khd->qhd", probs, value_seq[seq_pick], preferred_element_type=jnp.float32
        )
        return (attended.astype(jnp.bfloat16), (row_peak + jnp.log(row_total))[..., 0])

    attended_blocks, log_sums = lax.map(attend_block, block_ids)
    mixed = attended_blocks.reshape(group_rows, width_here)
    branch = lax.psum_scatter(
        jnp.dot(mixed, proj_w, preferred_element_type=jnp.float32),
        "mp",
        scatter_dimension=0,
        tiled=True,
    )
    first_sum = tokens.astype(jnp.float32) + branch + bias_proj
    normed, norm_one_back = jax.vjp(layer_norm, first_sum, gain_one, offset_one)
    normed_low = normed.astype(jnp.bfloat16)
    whole_normed = lax.all_gather(normed_low, "mp", axis=0, tiled=True)
    pre_act = jnp.dot(whole_normed, up_w, preferred_element_type=jnp.float32) + bias_up
    activated, gelu_back = jax.vjp(partial(jax.nn.gelu, approximate=False), pre_act)
    activated_low = activated.astype(jnp.bfloat16)
    feed = lax.psum_scatter(
        jnp.dot(
            lax.slice_in_dim(activated_low, 0, local_rows * lax.axis_size("mp"), axis=0),
            down_w,
            preferred_element_type=jnp.float32,
        ).astype(jnp.bfloat16),
        "mp",
        scatter_dimension=0,
        tiled=True,
    ).astype(jnp.float32)
    second_sum = normed + feed + bias_down
    block_out, norm_two_back = jax.vjp(layer_norm, second_sum, gain_two, offset_two)
    positions = mp_index * local_rows + jnp.arange(local_rows, dtype=jnp.int32)
    seq_of = positions // LEN
    within = positions % LEN
    picker = (seq_of[:, None] == jnp.arange(seq_here, dtype=jnp.int32)[None, :]).astype(jnp.int32)
    length_row = jnp.sum(picker * lengths[None, :], 1)
    start_row = jnp.sum(picker * starts[None, :], 1)
    end_row = jnp.sum(picker * ends[None, :], 1)
    flag_row = jnp.sum(picker * flags[None, :], 1).astype(jnp.float32)
    valid_row = (within < length_row).astype(jnp.float32)
    answer = (within == start_row).astype(jnp.float32) + (within == end_row).astype(jnp.float32)
    opening = (within == 0).astype(jnp.float32)
    row_weight = valid_row * (1.0 + 2.0 * (1.0 - flag_row) * answer + 4.0 * flag_row * opening)
    cotangent = out_cotangent.astype(jnp.float32) * row_weight[:, None]
    second_grad, gain_two_grad, offset_two_grad = norm_two_back(cotangent)
    bias_down_grad = jnp.sum(second_grad, 0)
    second_low = second_grad.astype(jnp.bfloat16)
    whole_second = lax.all_gather(second_low, "mp", axis=0, tiled=True)
    down_weight_grad = contract_rows(activated_low, whole_second)
    act_grad = contract_cols(whole_second, down_w)
    pre_grad = gelu_back(act_grad)[0].astype(jnp.bfloat16)
    bias_up_grad = jnp.sum(pre_grad, 0, dtype=jnp.float32)
    up_weight_grad = contract_rows(whole_normed, pre_grad)
    normed_grad = (
        lax.psum_scatter(
            contract_cols(pre_grad, up_w).astype(jnp.bfloat16),
            "mp",
            scatter_dimension=0,
            tiled=True,
        ).astype(jnp.float32)
        + second_grad
    )
    up_block = lax.dynamic_update_slice(
        jnp.zeros((FF,), jnp.float32), bias_up_grad, (mp_index * ff_here,)
    ).reshape(FF // D, D)
    first_grad, gain_one_grad, offset_one_grad = norm_one_back(normed_grad)
    bias_proj_grad = jnp.sum(first_grad, 0)
    whole_first = lax.all_gather(first_grad.astype(jnp.bfloat16), "mp", axis=0, tiled=True)
    proj_weight_grad = contract_rows(mixed, whole_first)
    mixed_grad = (
        contract_cols(whole_first, proj_w)
        .astype(jnp.bfloat16)
        .reshape(block_total, block_rows, heads_here, HDIM)
    )

    def attend_back(position):
        seq_pick = position // blocks_seq
        query_block, key_block, masked = block_scores(position)
        probs = jnp.exp(masked - log_sums[position][..., None])
        grad_block = mixed_grad[position]
        prob_grad = jnp.einsum(
            "qhd,khd->hqk", grad_block, value_seq[seq_pick], preferred_element_type=jnp.float32
        )
        score_grad = (
            probs * (prob_grad - jnp.sum(probs * prob_grad, -1, keepdims=True)) * scaling
        ).astype(jnp.bfloat16)
        query_grad = jnp.einsum(
            "hqk,khd->qhd", score_grad, key_block, preferred_element_type=jnp.float32
        ).astype(jnp.bfloat16)
        key_grad = jnp.einsum(
            "hqk,qhd->khd", score_grad, query_block, preferred_element_type=jnp.float32
        )
        value_grad = jnp.einsum(
            "hqk,qhd->khd",
            probs.astype(jnp.bfloat16),
            grad_block,
            preferred_element_type=jnp.float32,
        )
        return (query_grad, key_grad, value_grad)

    query_grads, key_grads, value_grads = lax.map(attend_back, block_ids)
    query_grad_all = query_grads.reshape(group_rows, width_here)
    key_grad_all = (
        jnp.sum(key_grads.reshape(seq_here, blocks_seq, LEN, width_here), 1)
        .reshape(group_rows, width_here)
        .astype(jnp.bfloat16)
    )
    value_grad_all = (
        jnp.sum(value_grads.reshape(seq_here, blocks_seq, LEN, width_here), 1)
        .reshape(group_rows, width_here)
        .astype(jnp.bfloat16)
    )
    qkv_weight_grad = jnp.stack(
        [
            contract_rows(whole_x, query_grad_all),
            contract_rows(whole_x, key_grad_all),
            contract_rows(whole_x, value_grad_all),
        ]
    )
    bias_query_grad = jnp.sum(query_grad_all, 0, dtype=jnp.float32)
    bias_value_grad = jnp.sum(value_grad_all, 0, dtype=jnp.float32)
    input_grad = (
        lax.psum_scatter(
            (
                contract_cols(query_grad_all, qkv_w[0])
                + contract_cols(key_grad_all, qkv_w[1])
                + contract_cols(value_grad_all, qkv_w[2])
            ).astype(jnp.bfloat16),
            "mp",
            scatter_dimension=0,
            tiled=True,
        ).astype(jnp.float32)
        + first_grad
    )
    zero_index = jnp.zeros((), jnp.int32)
    head_block = lax.dynamic_update_slice(
        jnp.zeros((2, D), jnp.float32),
        jnp.stack([bias_query_grad, bias_value_grad]),
        (zero_index, mp_index * width_here),
    )
    vector_part = jnp.concatenate(
        [
            head_block,
            jnp.stack(
                [
                    bias_proj_grad,
                    gain_one_grad,
                    offset_one_grad,
                    bias_down_grad,
                    gain_two_grad,
                    offset_two_grad,
                ]
            ),
            up_block,
        ],
        0,
    )
    vector_grad = lax.psum_scatter(vector_part, ("dp", "mp"), scatter_dimension=1, tiled=True)
    dp_part = D // dp_count
    summed = (
        lax.psum(qkv_weight_grad.astype(jnp.bfloat16), "dp").astype(jnp.float32),
        lax.psum(proj_weight_grad.astype(jnp.bfloat16), "dp").astype(jnp.float32),
        lax.psum(up_weight_grad.astype(jnp.bfloat16), "dp").astype(jnp.float32),
        lax.psum(down_weight_grad.astype(jnp.bfloat16), "dp").astype(jnp.float32),
    )
    qkv_sum = lax.dynamic_slice_in_dim(summed[0], dp_index * dp_part, dp_part, 1)
    proj_sum = lax.dynamic_slice_in_dim(summed[1], dp_index * dp_part, dp_part, 1)
    up_sum = lax.dynamic_slice_in_dim(summed[2], dp_index * dp_part, dp_part, 0)
    down_sum = lax.dynamic_slice_in_dim(summed[3], dp_index * dp_part, dp_part, 1)
    local_squares = (
        jnp.sum(qkv_sum * qkv_sum)
        + jnp.sum(proj_sum * proj_sum)
        + jnp.sum(up_sum * up_sum)
        + jnp.sum(down_sum * down_sum)
        + jnp.sum(vector_grad * vector_grad)
    )
    grad_norm = jnp.sqrt(lax.psum(local_squares, ("dp", "mp")))
    clip_factor = jnp.minimum(1.0, CLIP_NORM / (grad_norm + 1e-06))
    matrix_rate = MATRIX_RATE / math.sqrt(D)
    vec_columns = D // (dp_count * mp_count)
    vec_index = dp_index * mp_count + mp_index
    vector_shard = lax.dynamic_slice_in_dim(vectors, vec_index * vec_columns, vec_columns, 1)
    qkv_set = adamw(
        qkv_master, qkv_sum, qkv_first, qkv_second, matrix_rate, WEIGHT_DECAY, clip_factor
    )
    proj_set = adamw(
        proj_master, proj_sum, proj_first, proj_second, matrix_rate, WEIGHT_DECAY, clip_factor
    )
    up_set = adamw(up_master, up_sum, up_first, up_second, matrix_rate, WEIGHT_DECAY, clip_factor)
    down_set = adamw(
        down_master, down_sum, down_first, down_second, matrix_rate, WEIGHT_DECAY, clip_factor
    )
    vector_set = adamw(
        vector_shard, vector_grad, vector_first, vector_second, VECTOR_RATE, 0.0, clip_factor
    )
    return (
        block_out.astype(jnp.bfloat16),
        input_grad,
        grad_norm,
        qkv_set[0],
        qkv_set[1],
        qkv_set[2],
        qkv_set[3],
        proj_set[0],
        proj_set[1],
        proj_set[2],
        proj_set[3],
        up_set[0],
        up_set[1],
        up_set[2],
        up_set[3],
        down_set[0],
        down_set[1],
        down_set[2],
        down_set[3],
        vector_set[0],
        vector_set[1],
        vector_set[2],
        vector_set[3],
    )


def solution(mesh):
    placed = (
        P(("dp", "mp"), None),
        P(("dp", "mp"), None),
        P("dp"),
        P("dp"),
        P("dp"),
        P("dp"),
        P(None, "dp", "mp"),
        P("mp", "dp"),
        P("dp", "mp"),
        P("mp", "dp"),
        P(),
        P(None, "dp", "mp"),
        P("mp", "dp"),
        P("dp", "mp"),
        P("mp", "dp"),
        P(None, "dp", "mp"),
        P("mp", "dp"),
        P("dp", "mp"),
        P("mp", "dp"),
        P(None, ("dp", "mp")),
        P(None, ("dp", "mp")),
    )
    return jax.shard_map(
        shards,
        mesh=mesh,
        in_specs=placed,
        out_specs=(
            P(("dp", "mp"), None),
            P(("dp", "mp"), None),
            P(),
            P(None, "dp", "mp"),
            P(None, "dp", "mp"),
            P(None, "dp", "mp"),
            P(None, "dp", "mp"),
            P("mp", "dp"),
            P("mp", "dp"),
            P("mp", "dp"),
            P("mp", "dp"),
            P("dp", "mp"),
            P("dp", "mp"),
            P("dp", "mp"),
            P("dp", "mp"),
            P("mp", "dp"),
            P("mp", "dp"),
            P("mp", "dp"),
            P("mp", "dp"),
            P(None, ("dp", "mp")),
            P(None, ("dp", "mp")),
            P(None, ("dp", "mp")),
            P(None, ("dp", "mp")),
        ),
        check_vma=False,
    )
```

profile of v0, /device:TPU:0, one launch (start us, length us, event | category | flops | bytes accessed | tf_op | source)
XLA Modules:
  0.0 1381.4 jit_solution(10785745237289773479)
XLA Ops:
  10.8 12.1 all_gather.26
  24.6 11.8 all_gather.25
  37.2 65.4 %all-gather.7.cloned.1.call-done = bf16[3072,768]{1,0:T(8,128)(2,1)} async-done(((bf16[768,768]{1,0:T(8,128)(2,1)}), bf16[3072,768]{1,0:T(8,128)(2,1)}) %all-gather.7.cloned.1.call-update) | async-done | bytes 4718608 | tf_op jit(solution)/shard_map/all_gather | solution.py:110
  130.6 58.7 %while.32 = (s32[]{:T(128)}, bf16[6,512,3,64]{1,3,2,0:T(8,128)(2,1)}, f32[6,3,512]{2,1,0:T(4,128)}, s32[6]{0:T(128)}, bf16[3,1024,3,64]{1,3,2,0:T(8,128)(2,1)S(1...) while((s32[]{:T(128)}, ...), condition=%wide.region_3.4_spmd, body=%wide.region_0.3_spmd.sunk | while | flops 421624352 | bytes 20115928 | solution.py:148
  193.6 5.1 fusion.144
  200.4 158.2 %reduce-scatter.6.cloned.1.call-done = f32[768,768]{1,0:T(8,128)} async-done(((f32[3072,768]{1,0:T(8,128)}), f32[768,768]{1,0:T(8,128)}) %reduce-scatter.6.cloned.1.call-update) | async-done | bytes 2359312 | tf_op jit(solution)/shard_map/reduce_scatter | solution.py:150
  369.9 84.4 %all-gather.9.cloned.1.call-done = bf16[3072,768]{1,0:T(8,128)(2,1)} async-done(((bf16[768,768]{1,0:T(8,128)(2,1)}), bf16[3072,768]{1,0:T(8,128)(2,1)}) %all-gather.9.cloned.1.call-update) | async-done | bytes 4718608 | tf_op jit(solution)/shard_map/all_gather | solution.py:159
  454.3 27.0 %multiply_convert_fusion.1 = (bf16[3072,768]{1,0:T(8,128)(2,1)}, f32[3072,768]{1,0:T(8,128)}, f32[3072,768]{1,0:T(8,128)}) fusion(f32[768]{0:T(1024)} %dynamic_slice.109, bf16[3072,768]{1,0:T(8,128)(2,1)} %all-gather.9.cloned.1.call-done, bf16[768,768]{1,0:T(8,128)(2,1)} %all-gather.11.cloned.1.call-done), kind=kOutput, calls=%fused_computation.83 | convolution fusion | flops 3779592192 | bytes 29494272 | tf_op jit(solution)/shard_map/dot_general | solution.py:160
  481.4 8.7 convolution_convert_fusion.1
  491.6 82.2 %reduce-scatter.8.cloned.1.call-done = bf16[768,768]{1,0:T(8,128)(2,1)} async-done(((bf16[3072,768]{1,0:T(8,128)(2,1)}), bf16[768,768]{1,0:T(8,128)(2,1)}) %reduce-scatter.8.cloned.1.call-update) | async-done | bytes 1179664 | tf_op jit(solution)/shard_map/reduce_scatter | solution.py:163
  583.2 89.8 %all-gather.15.cloned.1.call-done = bf16[3072,768]{1,0:T(8,128)(2,1)} async-done(((bf16[768,768]{1,0:T(8,128)(2,1)}), bf16[3072,768]{1,0:T(8,128)(2,1)}) %all-gather.15.cloned.1.call-update) | async-done | bytes 4718608 | tf_op jit(solution)/shard_map/all_gather | solution.py:191
  673.1 13.9 %convert_reduce_fusion = (f32[768]{0:T(1024)}, bf16[3072,768]{1,0:T(8,128)(2,1)S(1)}) fusion(f32[3072,768]{1,0:T(8,128)} %get-tuple-element.640, f32[3072,768]{1,0:T(8,128)} %get-tuple-element.651, f32[768]{0:T(1024)} %dynamic_slice.109, bf16[3072,768]{1,0:T(8,128)(2,1)} %all-gather.15.cloned.1.call-done, bf16[768,768]{0,1:T(8,128)(2,1)} %all-gather.13.cloned.1.call-done), kind=kOutput, calls=%fused_computation.80 | convolution fusion | flops 3663985920 | bytes 29497344 | tf_op jit(solution)/shard_map/dot_general | solution.py:42
  689.1 5.7 convolution_convert_fusion
  694.8 83.8 %reduce-scatter.10.cloned.1.call-done = bf16[768,768]{1,0:T(8,128)(2,1)} async-done(((bf16[3072,768]{1,0:T(8,128)(2,1)}), bf16[768,768]{1,0:T(8,128)(2,1)}) %reduce-scatter.10.cloned.1.call-update) | async-done | bytes 1179664 | tf_op jit(solution)/shard_map/reduce_scatter | solution.py:198
  787.4 8.7 convolution_convert_fusion.4
  796.0 9.2 convolution_convert_fusion.5
  805.2 71.8 %all-gather.17.cloned.1.call-done = bf16[3072,768]{1,0:T(8,128)(2,1)} async-done(((bf16[768,768]{1,0:T(8,128)(2,1)}), bf16[3072,768]{1,0:T(8,128)(2,1)}) %all-gather.17.cloned.1.call-update) | async-done | bytes 4718608 | tf_op jit(solution)/shard_map/all_gather | solution.py:211
  885.9 322.1 %while.33 = (s32[]{:T(128)}, bf16[6,512,3,64]{1,3,2,0:T(8,128)(2,1)S(1)}, f32[6,1024,3,64]{1,3,2,0:T(8,128)}, f32[6,1024,3,64]{1,3,2,0:T(8,128)}, s32[6]{0:T(128...) while((s32[]{:T(128)}, ...), condition=%wide.region_21.22_spmd, body=%wide.region_19.21_spmd.sunk | while | flops 1047630848 | bytes 73004072 | solution.py:244
  889.8 4.8 fusion.209
  895.9 4.7 fusion.208
  901.9 17.1 %fusion.211 = f32[6,1024,3,64]{1,3,2,0:T(8,128)} fusion(f32[6,1024,3,64]{1,3,2,0:T(8,128)} %get-tuple-element.840, s32[]{:T(128)} %get-tuple-element.838, f32[3,512,1024]{2,1,0:T(8,128)} %fusion.208, f32[3,512,1024]{2,1,0:T(8,128)} %fusion.209, f32[3,512]{1,0:T(4,128)S(1)} %dynamic-slice_bitcast_fusion.2, ...), kind=kOutput, calls=%fused_computation.43.clone.1 | convolution fusion | flops 218630656 | bytes 26167816 | tf_op jit(solution)/shard_map/while/body/eval_jaxpr/hqk,qhd->khd/dot_general | solution.py:233
  919.0 15.4 %fusion.210 = bf16[6,512,3,64]{1,3,2,0:T(8,128)(2,1)S(1)} fusion(bf16[6,512,3,64]{1,3,2,0:T(8,128)(2,1)S(1)} %get-tuple-element.839, s32[]{:T(128)} %get-tuple-element.838, f32[3,512,1024]{2,1,0:T(8,128)} %fusion.208, f32[3,512,1024]{2,1,0:T(8,128)} %fusion.209, f32[3,512]{1,0:T(4,128)S(1)} %dynamic-slice_bitcast_fusion.2, ...), kind=kOutput, calls=%fused_computation.46.clone.1 | convolution fusion | flops 218728960 | bytes 25774596 | tf_op jit(solution)/shard_map/while/body/eval_jaxpr/hqk,khd->qhd/dot_general | solution.py:230
  934.5 5.1 fusion.212
  943.5 4.7 fusion.209
  955.6 17.1 %fusion.211 = f32[6,1024,3,64]{1,3,2,0:T(8,128)} fusion(f32[6,1024,3,64]{1,3,2,0:T(8,128)} %get-tuple-element.840, s32[]{:T(128)} %get-tuple-element.838, f32[3,512,1024]{2,1,0:T(8,128)} %fusion.208, f32[3,512,1024]{2,1,0:T(8,128)} %fusion.209, f32[3,512]{1,0:T(4,128)S(1)} %dynamic-slice_bitcast_fusion.2, ...), kind=kOutput, calls=%fused_computation.43.clone.1 | convolution fusion | flops 218630656 | bytes 26167816 | tf_op jit(solution)/shard_map/while/body/eval_jaxpr/hqk,qhd->khd/dot_general | solution.py:233
  972.6 15.4 %fusion.210 = bf16[6,512,3,64]{1,3,2,0:T(8,128)(2,1)S(1)} fusion(bf16[6,512,3,64]{1,3,2,0:T(8,128)(2,1)S(1)} %get-tuple-element.839, s32[]{:T(128)} %get-tuple-element.838, f32[3,512,1024]{2,1,0:T(8,128)} %fusion.208, f32[3,512,1024]{2,1,0:T(8,128)} %fusion.209, f32[3,512]{1,0:T(4,128)S(1)} %dynamic-slice_bitcast_fusion.2, ...), kind=kOutput, calls=%fused_computation.46.clone.1 | convolution fusion | flops 218728960 | bytes 25774596 | tf_op jit(solution)/shard_map/while/body/eval_jaxpr/hqk,khd->qhd/dot_general | solution.py:230
  988.1 5.1 fusion.212
  997.1 4.8 fusion.209
  1003.1 4.7 fusion.208
  1009.1 17.1 %fusion.211 = f32[6,1024,3,64]{1,3,2,0:T(8,128)} fusion(f32[6,1024,3,64]{1,3,2,0:T(8,128)} %get-tuple-element.840, s32[]{:T(128)} %get-tuple-element.838, f32[3,512,1024]{2,1,0:T(8,128)} %fusion.208, f32[3,512,1024]{2,1,0:T(8,128)} %fusion.209, f32[3,512]{1,0:T(4,128)S(1)} %dynamic-slice_bitcast_fusion.2, ...), kind=kOutput, calls=%fused_computation.43.clone.1 | convolution fusion | flops 218630656 | bytes 26167816 | tf_op jit(solution)/shard_map/while/body/eval_jaxpr/hqk,qhd->khd/dot_general | solution.py:233
  1026.3 15.4 %fusion.210 = bf16[6,512,3,64]{1,3,2,0:T(8,128)(2,1)S(1)} fusion(bf16[6,512,3,64]{1,3,2,0:T(8,128)(2,1)S(1)} %get-tuple-element.839, s32[]{:T(128)} %get-tuple-element.838, f32[3,512,1024]{2,1,0:T(8,128)} %fusion.208, f32[3,512,1024]{2,1,0:T(8,128)} %fusion.209, f32[3,512]{1,0:T(4,128)S(1)} %dynamic-slice_bitcast_fusion.2, ...), kind=kOutput, calls=%fused_computation.46.clone.1 | convolution fusion | flops 218728960 | bytes 25774596 | tf_op jit(solution)/shard_map/while/body/eval_jaxpr/hqk,khd->qhd/dot_general | solution.py:230
  1041.7 5.1 fusion.212
  1050.7 4.7 fusion.209
  1062.8 17.1 %fusion.211 = f32[6,1024,3,64]{1,3,2,0:T(8,128)} fusion(f32[6,1024,3,64]{1,3,2,0:T(8,128)} %get-tuple-element.840, s32[]{:T(128)} %get-tuple-element.838, f32[3,512,1024]{2,1,0:T(8,128)} %fusion.208, f32[3,512,1024]{2,1,0:T(8,128)} %fusion.209, f32[3,512]{1,0:T(4,128)S(1)} %dynamic-slice_bitcast_fusion.2, ...), kind=kOutput, calls=%fused_computation.43.clone.1 | convolution fusion | flops 218630656 | bytes 26167816 | tf_op jit(solution)/shard_map/while/body/eval_jaxpr/hqk,qhd->khd/dot_general | solution.py:233
  1079.9 15.4 %fusion.210 = bf16[6,512,3,64]{1,3,2,0:T(8,128)(2,1)S(1)} fusion(bf16[6,512,3,64]{1,3,2,0:T(8,128)(2,1)S(1)} %get-tuple-element.839, s32[]{:T(128)} %get-tuple-element.838, f32[3,512,1024]{2,1,0:T(8,128)} %fusion.208, f32[3,512,1024]{2,1,0:T(8,128)} %fusion.209, f32[3,512]{1,0:T(4,128)S(1)} %dynamic-slice_bitcast_fusion.2, ...), kind=kOutput, calls=%fused_computation.46.clone.1 | convolution fusion | flops 218728960 | bytes 25774596 | tf_op jit(solution)/shard_map/while/body/eval_jaxpr/hqk,khd->qhd/dot_general | solution.py:230
  1095.3 5.1 fusion.212
  1104.3 4.8 fusion.209
  1116.4 17.1 %fusion.211 = f32[6,1024,3,64]{1,3,2,0:T(8,128)} fusion(f32[6,1024,3,64]{1,3,2,0:T(8,128)} %get-tuple-element.840, s32[]{:T(128)} %get-tuple-element.838, f32[3,512,1024]{2,1,0:T(8,128)} %fusion.208, f32[3,512,1024]{2,1,0:T(8,128)} %fusion.209, f32[3,512]{1,0:T(4,128)S(1)} %dynamic-slice_bitcast_fusion.2, ...), kind=kOutput, calls=%fused_computation.43.clone.1 | convolution fusion | flops 218630656 | bytes 26167816 | tf_op jit(solution)/shard_map/while/body/eval_jaxpr/hqk,qhd->khd/dot_general | solution.py:233
  1133.5 15.4 %fusion.210 = bf16[6,512,3,64]{1,3,2,0:T(8,128)(2,1)S(1)} fusion(bf16[6,512,3,64]{1,3,2,0:T(8,128)(2,1)S(1)} %get-tuple-element.839, s32[]{:T(128)} %get-tuple-element.838, f32[3,512,1024]{2,1,0:T(8,128)} %fusion.208, f32[3,512,1024]{2,1,0:T(8,128)} %fusion.209, f32[3,512]{1,0:T(4,128)S(1)} %dynamic-slice_bitcast_fusion.2, ...), kind=kOutput, calls=%fused_computation.46.clone.1 | convolution fusion | flops 218728960 | bytes 25774596 | tf_op jit(solution)/shard_map/while/body/eval_jaxpr/hqk,khd->qhd/dot_general | solution.py:230
  1148.9 5.2 fusion.212
  1158.0 4.7 fusion.209
  1170.1 17.1 %fusion.211 = f32[6,1024,3,64]{1,3,2,0:T(8,128)} fusion(f32[6,1024,3,64]{1,3,2,0:T(8,128)} %get-tuple-element.840, s32[]{:T(128)} %get-tuple-element.838, f32[3,512,1024]{2,1,0:T(8,128)} %fusion.208, f32[3,512,1024]{2,1,0:T(8,128)} %fusion.209, f32[3,512]{1,0:T(4,128)S(1)} %dynamic-slice_bitcast_fusion.2, ...), kind=kOutput, calls=%fused_computation.43.clone.1 | convolution fusion | flops 218630656 | bytes 26167816 | tf_op jit(solution)/shard_map/while/body/eval_jaxpr/hqk,qhd->khd/dot_general | solution.py:233
  1187.2 15.4 %fusion.210 = bf16[6,512,3,64]{1,3,2,0:T(8,128)(2,1)S(1)} fusion(bf16[6,512,3,64]{1,3,2,0:T(8,128)(2,1)S(1)} %get-tuple-element.839, s32[]{:T(128)} %get-tuple-element.838, f32[3,512,1024]{2,1,0:T(8,128)} %fusion.208, f32[3,512,1024]{2,1,0:T(8,128)} %fusion.209, f32[3,512]{1,0:T(4,128)S(1)} %dynamic-slice_bitcast_fusion.2, ...), kind=kOutput, calls=%fused_computation.46.clone.1 | convolution fusion | flops 218728960 | bytes 25774596 | tf_op jit(solution)/shard_map/while/body/eval_jaxpr/hqk,khd->qhd/dot_general | solution.py:230
  1202.7 5.2 fusion.212
  1234.0 5.1 add_convert_fusion
  1244.5 44.1 %all-reduce = f32[12,768]{1,0:T(8,128)S(1)} all-reduce(f32[12,768]{1,0:T(8,128)S(1)} %concatenate.3), channel_id=6, replica_groups=mesh['dp'=8,'mp'=4] {'dp','mp'}, use_global_device_ids=true, to_apply=%region_42.43.clone | all-reduce | flops 9216 | bytes 73728
  1289.3 12.8 all-reduce.4.cloned.1.call-done
  1311.9 39.4 %psum.39 = f32[]{:T(128)} all-reduce(f32[]{:T(128)S(6)} %add.431), channel_id=1, replica_groups=mesh['dp'=8,'mp'=4] {'dp','mp'}, use_global_device_ids=true, to_apply=%region_44.45 | all-reduce | flops 1 | bytes 8 | tf_op jit(solution)/shard_map/psum | solution.py:320
  (279 shorter events, 216.6 us)
Async XLA Ops:
  8.0 94.5 %all-gather.7.cloned.1.call-start = ((), (), s32[]{:S(2)}) async-start(), calls=%async_computation.4 | async-start | bytes 5898240 | tf_op jit(solution)/shard_map/all_gather | solution.py:110
  8.8 349.9 %reduce-scatter.6.cloned.1.call-start = ((), (), s32[]{:S(2)}) async-start(), calls=%async_computation.5 | async-start | bytes 11796480 | tf_op jit(solution)/shard_map/reduce_scatter | solution.py:150
  36.5 75.0 %copy-start.14 = (bf16[3,768,192]{2,1,0:T(8,128)(2,1)}, bf16[3,768,192]{2,1,0:T(8,128)(2,1)S(1)}, u32[]{:S(2)}) copy-start(bf16[3,768,192]{2,1,0:T(8,128)(2,1)S(1)} %all_gather.25) | copy-start | bytes 2654212
  189.3 9.4 copy-start.6
  189.3 9.4 copy-start.7
  189.3 4.3 copy-start.18
  198.7 171.2 %all-gather.11.cloned.1.call-start = ((), (), s32[]{:S(2)}) async-start(), calls=%async_computation.7 | async-start | bytes 1327104 | tf_op jit(solution)/shard_map/all_gather | solution.py:97
  200.3 254.0 %all-gather.9.cloned.1.call-start = ((), (), s32[]{:S(2)}) async-start(), calls=%async_computation.6 | async-start | bytes 5898240 | tf_op jit(solution)/shard_map/all_gather | solution.py:159
  364.1 117.2 %all-gather.13.cloned.1.call-start = ((), (), s32[]{:S(2)}) async-start(), calls=%async_computation.8 | async-start | bytes 1327104 | tf_op jit(solution)/shard_map/all_gather | solution.py:98
  365.9 208.0 %reduce-scatter.8.cloned.1.call-start = ((), (), s32[]{:S(2)}) async-start(), calls=%async_computation.9 | async-start | bytes 5898240 | tf_op jit(solution)/shard_map/reduce_scatter | solution.py:163
  490.1 183.0 %all-gather.15.cloned.1.call-start = ((), (), s32[]{:S(2)}) async-start(), calls=%async_computation.10 | async-start | bytes 5898240 | tf_op jit(solution)/shard_map/all_gather | solution.py:191
  573.8 2.7 copy-start.17
  573.8 2.7 copy-start.29
  573.9 2.7 copy-start.30
  573.9 4.4 copy-start.31
  583.2 195.5 %reduce-scatter.10.cloned.1.call-start = ((), (), s32[]{:S(2)}) async-start(), calls=%async_computation.11 | async-start | bytes 5898240 | tf_op jit(solution)/shard_map/reduce_scatter | solution.py:198
  673.1 16.1 %copy-start.41 = (bf16[768,768]{1,0:T(8,128)(2,1)S(1)}, bf16[768,768]{1,0:T(8,128)(2,1)}, u32[]{:S(2)}) copy-start(bf16[768,768]{1,0:T(8,128)(2,1)} %all-gather.11.cloned.1.call-done) | copy-start | bytes 3538948
  687.0 2.1 copy-start.42
  694.8 182.2 %all-gather.17.cloned.1.call-start = ((), (), s32[]{:S(2)}) async-start(), calls=%async_computation.12 | async-start | bytes 5898240 | tf_op jit(solution)/shard_map/all_gather | solution.py:211
  778.7 3.7 copy-start.28
  778.7 3.7 copy-start.1
  778.7 3.7 copy-start.16
  778.7 3.7 copy-start.26
  787.1 515.0 %all-reduce.4.cloned.1.call-start = ((), (), s32[]{:S(2)}) async-start(), calls=%async_computation.14 | async-start | bytes 7077888 | tf_op jit(solution)/shard_map/psum | solution.py:304
  796.0 81.0 %copy-start.19 = (bf16[192,768]{0,1:T(8,128)(2,1)S(1)}, bf16[192,768]{0,1:T(8,128)(2,1)}, u32[]{:S(2)}) copy-start(bf16[192,768]{0,1:T(8,128)(2,1)} %all_gather.26) | copy-start | bytes 884740
  1208.1 2.3 copy-start.4
  1213.4 10.2 slice-start
  1219.0 5.7 copy-start.8
  1219.1 4.6 slice-start.1
  1219.2 5.6 copy-start.15
  1223.6 3.3 slice-start.2
  1224.8 2.2 copy-start.11
  1224.8 2.2 slice-start.3
  1228.8 140.8 %reduce-scatter.12.cloned.1.call-start = ((), (), s32[]{:S(2)}) async-start(), calls=%async_computation.13 | async-start | bytes 5898240 | tf_op jit(solution)/shard_map/reduce_scatter | solution.py:266
  1228.9 2.6 copy-start.13
  1239.1 3.9 copy-start.34
  1239.1 3.9 copy-start.33
  1239.1 3.9 copy-start.40
  1239.1 4.5 copy-start.32
  1239.1 4.5 copy-start.37
  1239.1 4.5 copy-start.36
  1239.1 4.5 copy-start.35
  1239.1 4.5 copy-start.5
  1240.0 122.0 %copy-start.38 = (f32[12,24]{1,0:T(8,128)S(1)}, f32[12,24]{1,0:T(8,128)}, u32[]{:S(2)}) copy-start(f32[12,24]{1,0:T(8,128)} %param.45) | copy-start | bytes 3460
  1240.0 122.0 %copy-start.39 = (f32[12,24]{1,0:T(8,128)S(1)}, f32[12,24]{1,0:T(8,128)}, u32[]{:S(2)}) copy-start(f32[12,24]{1,0:T(8,128)} %param.44) | copy-start | bytes 3460
  1241.0 124.3 %copy-start.21 = (f32[768,96]{0,1:T(8,128)S(1)}, f32[768,96]{0,1:T(8,128)}, u32[]{:S(2)}) copy-start(f32[768,96]{0,1:T(8,128)} %param.34) | copy-start | bytes 884740
  1244.0 123.5 %copy-start.23 = (f32[96,768]{1,0:T(8,128)S(1)}, f32[96,768]{1,0:T(8,128)}, u32[]{:S(2)}) copy-start(f32[96,768]{1,0:T(8,128)} %param.33) | copy-start | bytes 884740
  1352.0 17.6 %copy-start.3 = (f32[768,768]{1,0:T(8,128)S(1)}, f32[768,768]{1,0:T(8,128)}, u32[]{:S(2)}) copy-start(f32[768,768]{1,0:T(8,128)} %copy-done.2) | copy-start | bytes 7077892
  (10 other events, 12.4 us)
Sparse Core Ops, SparseCore 0:
  10.4 92.0 all-gather.6
  198.8 159.7 reduce-scatter.5
  694.9 83.7 reduce-scatter.9
  1239.3 85.2 reduce-scatter.11
Sparse Core Ops, SparseCore 1:
  201.6 22.3 all-gather.10
  364.2 90.1 all-gather.8
  456.7 22.3 all-gather.12
  490.2 83.6 reduce-scatter.7
  583.3 89.7 all-gather.14
  787.2 89.7 all-gather.16
  1228.9 73.1 all-reduce.3
where the time goes:
time: 1390 us; the launch traced here: 1380 us
  waiting for transfers between devices  649 us (47%)
  matrix products  418 us (30%)
  blocking collectives  107 us (8%)
  local copies, waits for them, and re-layouts  77 us (6%)
  other arithmetic  67.3 us (5%)
  loops' own time  39.7 us (3%)
  between operations  21.6 us (2%)
    reduce_scatter x1, waiting for transfers between devices, shards(): lax.psum_scatter(jnp.dot(mixed, proj_w, preferred_element_type=jnp.float3...  158 us
    dot_general x6, matrix products, attend_back(): jnp.einsum('hqk,qhd->khd', score_grad, query_block, preferred_element_typ...  103 us
    dot_general x6, matrix products, attend_back(): jnp.einsum('hqk,khd->qhd', score_grad, key_block, preferred_element_type=...  92.7 us
    all_gather x1, waiting for transfers between devices, shards(): whole_second = lax.all_gather(second_low, 'mp', axis=0, tiled=True)  89.8 us
    all_gather x1, waiting for transfers between devices, shards(): whole_normed = lax.all_gather(normed_low, 'mp', axis=0, tiled=True)  84.4 us
    reduce_scatter x1, waiting for transfers between devices, shards(): lax.psum_scatter(contract_cols(pre_grad, up_w).astype(jnp.bfloat16), 'mp'...  83.8 us
    reduce_scatter x1, waiting for transfers between devices, shards(): lax.psum_scatter(jnp.dot(lax.slice_in_dim(activated_low, 0, local_rows *...  82.2 us
    all_gather x1, waiting for transfers between devices, shards(): lax.all_gather(first_grad.astype(jnp.bfloat16), 'mp', axis=0, tiled=True)  71.8 us
  transfers between devices with their start and end apart: 11, of which 8 were waited for; matrix products, arithmetic and copies ran while one was open for 7% of the time, Pallas kernels for 0%

commit v1 on v0

v1 whole, which is shorter than its diff:
```python
from functools import partial
import math

import jax
import jax.numpy as jnp
import numpy as np
from jax import lax
from jax.experimental import pallas as pl
from jax.experimental.pallas import tpu as pltpu
from jax.sharding import PartitionSpec as P

D = 768
HEADS = 12
HDIM = 64
FF = 3072
LEN = 1024
STEP = 10

LN_EPS = 1e-06
BETA_ONE = 0.9
BETA_TWO = 0.999
ADAM_EPS = 1e-08
WEIGHT_DECAY = 0.01
CLIP_NORM = 1.0
VECTOR_RATE = 1.0
MATRIX_RATE = 2.0
NEG_FILL = -1e30

BF = jnp.bfloat16
F32 = jnp.float32
AXES = ("dp", "mp")
BLK = 256
ROWS = 768
PAIRS = HEADS // 2
RB = 8
RP = D // RB
VMEM_LIMIT = 60 * 1024 * 1024

KEY_BLOCKS = np.array(
    [
        [[0, 1, 2, 3]] * 3,
        [[3, 4, 5, 0], [1, 2, 6, 7], [1, 2, 6, 7]],
        [[6, 7, 0, 1], [6, 7, 0, 1], [2, 3, 4, 5]],
        [[5, 0, 1, 2]] * 3,
    ],
    np.int32,
)
BLOCK_SEQ = np.array(
    [[0, 0, 0, 0, 0, 0, 0, 0], [0, 1, 1, 0, 0, 0, 1, 1], [1, 1, 2, 2, 2, 2, 1, 1], [2, 2, 2, 2, 2, 2, 2, 2]], np.int32
)
BLOCK_PLACE = np.array(
    [[0, 1, 2, 3, 4, 4, 4, 4], [3, 0, 1, 0, 1, 2, 2, 3], [2, 3, 0, 1, 2, 3, 0, 1], [1, 2, 3, 4, 4, 0, 4, 4]], np.int32
)


def dot_nn(left, right):
    return jnp.dot(left, right, preferred_element_type=F32)


def dot_nt(left, right):
    return lax.dot_general(left, right, (((1,), (1,)), ((), ())), preferred_element_type=F32)


def lane_ids(rows):
    return lax.broadcasted_iota(jnp.int32, (rows, 128), 1)


def assemble(core, same_ref, other_ref, part, target, col):
    width = same_ref.shape[-1]
    for pos in range(RB // 2):
        same = same_ref[pos, part]
        other = other_ref[pos, part]
        first = jnp.where(core == 0, same, other)
        second = jnp.where(core == 0, other, same)
        target[2 * pos * RP : (2 * pos + 1) * RP, col : col + width] = first
        target[(2 * pos + 1) * RP : (2 * pos + 2) * RP, col : col + width] = second


def key_sides(k, count):
    rows = k.shape[0]
    lane = lane_ids(rows)
    place = lane % HDIM
    row = lax.broadcasted_iota(jnp.int32, (rows, 128), 0)
    mask = jnp.where(row >= count, NEG_FILL, 0.0)
    extra = jnp.where(place == 0, mask, jnp.where(place <= 3, 1.0, 0.0)).astype(BF)
    low = lane < HDIM
    return jnp.where(low, k, extra), jnp.where(low, extra, k)


def split_three(value):
    high = value.astype(BF)
    rest = value - high.astype(F32)
    mid = rest.astype(BF)
    low = (rest - mid.astype(F32)).astype(BF)
    return high, mid, low


def attend_kernel(
    tab, own_ref, nb_ref, mid_ref, same_ref, other_ref, vec_ref, o_ref, qe_ref, qo_ref, k_ref, v_ref, w_s, ka_e, ka_o, va_e, va_o
):
    core = tab[20]
    for part in range(3):
        assemble(core, same_ref, other_ref, part, w_s, 128 * part)
    bias_q = vec_ref[0:1, :]
    bias_v = vec_ref[1:2, :]
    low = lane_ids(BLK) < HDIM
    place = lane_ids(BLK) % HDIM
    ones = jnp.ones((BLK, 128), BF)
    for b in range(8):
        src, at = (own_ref, b) if b < 3 else (nb_ref, b - 3) if b < 6 else (mid_ref, b - 6)
        kv = dot_nn(src[at * BLK : (at + 1) * BLK, :], w_s[:, 128:384])
        k = kv[:, :128].astype(BF)
        v = (kv[:, 128:] + bias_v).astype(BF)
        k_ref[b * BLK : (b + 1) * BLK, :] = k
        v_ref[b * BLK : (b + 1) * BLK, :] = v
        k_even, k_odd = key_sides(k, tab[12 + b])
        ka_e[b] = k_even
        ka_o[b] = k_odd
        va_e[b] = jnp.where(low, v, ones)
        va_o[b] = jnp.where(low, ones, v)
    q_extra = jnp.where(place == 0, 1.0, 0.0).astype(BF)
    for i in range(3):
        q = (dot_nn(own_ref[i * BLK : (i + 1) * BLK, :], w_s[:, :128]) + bias_q).astype(BF) * jnp.asarray(0.125, BF)
        outs = []
        for head, (ka, va) in enumerate(((ka_e, va_e), (ka_o, va_o))):
            qa = jnp.where(low, q, q_extra) if head == 0 else jnp.where(low, q_extra, q)
            scores = [dot_nt(qa, ka[tab[4 * i + j]]) for j in range(4)]
            peak = jnp.max(
                jnp.maximum(jnp.maximum(scores[0], scores[1]), jnp.maximum(scores[2], scores[3])), -1, keepdims=True
            )
            acc = None
            for j in range(4):
                probs = jnp.exp(scores[j] - peak).astype(BF)
                part = dot_nn(probs, va[tab[4 * i + j]])
                acc = part if acc is None else acc + part
            log_sum = peak + jnp.log(acc)
            high, mid, small = split_three(-log_sum)
            extra = jnp.where(place == 0, 1.0, 0.0).astype(BF)
            extra = jnp.where(place == 1, high, extra)
            extra = jnp.where(place == 2, mid, extra)
            extra = jnp.where(place == 3, small, extra)
            if head == 0:
                qe_ref[i * BLK : (i + 1) * BLK, :] = jnp.where(low, q, extra)
            else:
                qo_ref[i * BLK : (i + 1) * BLK, :] = jnp.where(low, extra, q)
            outs.append(acc)
        total = jnp.where(low, outs[1], outs[0])
        value = jnp.where(low, outs[0], outs[1])
        o_ref[i * BLK : (i + 1) * BLK, :] = (value / pltpu.roll(total, HDIM, 1)).astype(BF)


def attend_back_kernel(
    tab,
    qe_ref,
    qo_ref,
    k_ref,
    v_ref,
    do_ref,
    o_ref,
    xt_ref,
    dq_ref,
    dk_ref,
    dv_ref,
    dw_ref,
    db_ref,
    ka_e,
    ka_o,
    vb_e,
    vb_o,
    kt_s,
    dk_s,
    dv_s,
    dkv_s,
):
    low = lane_ids(BLK) < HDIM
    place = lane_ids(BLK) % HDIM
    v_extra = jnp.where(place < 3, 1.0, 0.0).astype(BF)
    zero = jnp.zeros((BLK, 128), BF)
    for b in range(8):
        k = k_ref[b * BLK : (b + 1) * BLK, :]
        v = v_ref[b * BLK : (b + 1) * BLK, :]
        k_even, k_odd = key_sides(k, tab[12 + b])
        ka_e[b] = k_even
        ka_o[b] = k_odd
        vb_e[b] = jnp.where(low, v, v_extra)
        vb_o[b] = jnp.where(low, v_extra, v)
        kt_s[b] = k.T
        dk_s[b] = jnp.zeros((BLK, 128), F32)
        dv_s[b] = jnp.zeros((BLK, 128), F32)
    for i in range(3):
        rows = slice(i * BLK, (i + 1) * BLK)
        d_out = do_ref[rows, :]
        product = d_out.astype(F32) * o_ref[rows, :].astype(F32)
        qas = (qe_ref[rows, :], qo_ref[rows, :])
        sides = []
        for head in range(2):
            mine = low if head == 0 else jnp.logical_not(low)
            delta = jnp.sum(jnp.where(mine, product, 0.0), -1, keepdims=True)
            high, mid, small = split_three(-delta)
            extra = jnp.where(place == 0, high, jnp.where(place == 1, mid, jnp.where(place == 2, small, zero)))
            sides.append((jnp.where(mine, d_out, extra), jnp.where(mine, d_out, zero), jnp.where(mine, qas[head], zero)))
        dqt = [None, None]
        for j in range(4):
            b = tab[4 * i + j]
            dv_part = None
            dk_part = None
            for head, (ka, vb) in enumerate(((ka_e, vb_e), (ka_o, vb_o))):
                d_aug, d_only, q_only = sides[head]
                probs = jnp.exp(dot_nt(ka[b], qas[head]))
                d_probs = dot_nt(vb[b], d_aug)
                d_scores = (probs * d_probs).astype(BF)
                v_add = dot_nn(probs.astype(BF), d_only)
                k_add = dot_nn(d_scores, q_only)
                dv_part = v_add if dv_part is None else dv_part + v_add
                dk_part = k_add if dk_part is None else dk_part + k_add
                q_add = dot_nn(kt_s[b, head * HDIM : (head + 1) * HDIM, :], d_scores)
                dqt[head] = q_add if dqt[head] is None else dqt[head] + q_add
            dv_s[b] += dv_part
            dk_s[b] += dk_part
        dq_ref[rows, :] = (jnp.concatenate(dqt, 0).T * 0.125).astype(BF)
    for b in range(8):
        dk = dk_s[b].astype(BF)
        dv = dv_s[b].astype(BF)
        dk_ref[b * BLK : (b + 1) * BLK, :] = dk
        dv_ref[b * BLK : (b + 1) * BLK, :] = dv
        dkv_s[b * BLK : (b + 1) * BLK, :128] = dk
        dkv_s[b * BLK : (b + 1) * BLK, 128:] = dv
    dq_all = dq_ref[...]
    db_ref[0:1, :] = jnp.sum(dq_all.astype(F32), 0, keepdims=True)
    db_ref[1:2, :] = jnp.sum(dkv_s[:, 128:].astype(F32), 0, keepdims=True)
    dw_ref[:, 0] = dot_nn(xt_ref[:, :ROWS], dq_all).astype(BF).reshape(RB, RP, 128)
    dw_kv = dot_nn(xt_ref[...], dkv_s[...]).astype(BF)
    dw_ref[:, 1] = dw_kv[:, :128].reshape(RB, RP, 128)
    dw_ref[:, 2] = dw_kv[:, 128:].reshape(RB, RP, 128)


def gelu_both(pre):
    size = jnp.abs(pre)
    bell = jnp.exp(pre * pre * -0.5)
    t = 1.0 / (1.0 + size * (0.3275911 * math.sqrt(0.5)))
    poly = t * (
        0.5 * 0.254829592
        + t * (0.5 * -0.284496736 + t * (0.5 * 1.421413741 + t * (0.5 * -1.453152027 + t * (0.5 * 1.061405429))))
    )
    tail = poly * bell
    phi = jnp.where(pre >= 0, 1.0 - tail, tail)
    return pre * phi, phi + pre * bell * (1.0 / math.sqrt(2.0 * math.pi))


def norm_parts(summed):
    average = jnp.mean(summed, -1, keepdims=True)
    centered = summed - average
    variance = jnp.mean(centered * centered, -1, keepdims=True)
    root = lax.rsqrt(variance + LN_EPS)
    return centered * root, root


def norm_back(cot, gain, hat, root):
    gz = cot * gain
    return root * (gz - jnp.mean(gz, -1, keepdims=True) - hat * jnp.mean(gz * hat, -1, keepdims=True))


def feed_kernel(
    tab,
    o_ref,
    x_ref,
    same_ref,
    other_ref,
    vec_ref,
    w_ref,
    cot_ref,
    weight_ref,
    u_ref,
    gp_ref,
    out_ref,
    dz2_ref,
    e2_ref,
    e2t_ref,
    h1t_ref,
    hat1_ref,
    root1_ref,
    sums_ref,
    wo_s,
    h1_s,
    h1b_s,
    z2_s,
):
    step = pl.program_id(0)

    @pl.when(step == 0)
    def _():
        assemble(tab[20], same_ref, other_ref, 0, wo_s, 0)
        for i in range(3):
            rows = slice(i * BLK, (i + 1) * BLK)
            z1 = x_ref[rows, :].astype(F32) + dot_nt(o_ref[rows, :], wo_s[...]) + vec_ref[2:3, :]
            hat, root = norm_parts(z1)
            h1 = hat * vec_ref[3:4, :] + vec_ref[4:5, :]
            hat1_ref[rows, :] = hat
            root1_ref[rows, :] = root
            h1_s[rows, :] = h1
            h1b = h1.astype(BF)
            h1b_s[rows, :] = h1b
            h1t_ref[:, rows] = h1b.T

    w1 = w_ref[:, 0, 0].reshape(D, D)
    w2t = w_ref[:, 0, 1].reshape(D, D)
    bias = vec_ref[pl.ds(8 + step, 1), :]
    for i in range(3):
        rows = slice(i * BLK, (i + 1) * BLK)
        pre = dot_nn(h1b_s[rows, :], w1) + bias
        act, slope = gelu_both(pre)
        act = act.astype(BF)
        u_ref[rows, :] = act
        gp_ref[rows, :] = slope.astype(BF)
        feed = dot_nt(act, w2t)

        @pl.when(step == 0)
        def _():
            z2_s[rows, :] = feed

        @pl.when(step > 0)
        def _():
            z2_s[rows, :] += feed

    @pl.when(step == 3)
    def _():
        sums = [jnp.zeros((1, D), F32) for _ in range(3)]
        for i in range(3):
            rows = slice(i * BLK, (i + 1) * BLK)
            z2 = h1_s[rows, :] + z2_s[rows, :] + vec_ref[5:6, :]
            hat, root = norm_parts(z2)
            out_ref[rows, :] = (hat * vec_ref[6:7, :] + vec_ref[7:8, :]).astype(BF)
            cot = cot_ref[rows, :].astype(F32) * weight_ref[rows, :]
            dz2 = norm_back(cot, vec_ref[6:7, :], hat, root)
            dz2_ref[rows, :] = dz2
            e2 = dz2.astype(BF)
            e2_ref[rows, :] = e2
            e2t_ref[:, rows] = e2.T
            sums[0] += jnp.sum(dz2, 0, keepdims=True)
            sums[1] += jnp.sum(cot * hat, 0, keepdims=True)
            sums[2] += jnp.sum(cot, 0, keepdims=True)
        for n in range(3):
            sums_ref[n : n + 1, :] = sums[n]


def feed_back_kernel(
    tab,
    e2_ref,
    e2t_ref,
    h1t_ref,
    u_ref,
    gp_ref,
    w_ref,
    dz2_ref,
    hat1_ref,
    root1_ref,
    o_ref,
    same_ref,
    other_ref,
    vec_ref,
    dw_ref,
    dz1_ref,
    do_ref,
    dwo_ref,
    sums_ref,
    db1_ref,
    ep_s,
    dh_s,
    wo_s,
    e1t_s,
):
    step = pl.program_id(0)
    w1 = w_ref[:, 0, 0].reshape(D, D)
    w2t = w_ref[:, 0, 1].reshape(D, D)
    db1 = jnp.zeros((1, D), F32)
    for i in range(3):
        rows = slice(i * BLK, (i + 1) * BLK)
        du = dot_nn(e2_ref[rows, :], w2t)
        ep = (gp_ref[rows, :].astype(F32) * du).astype(BF)
        ep_s[rows, :] = ep
        db1 += jnp.sum(ep.astype(F32), 0, keepdims=True)
        back = dot_nt(ep, w1)

        @pl.when(step == 0)
        def _():
            dh_s[rows, :] = back + dz2_ref[rows, :]

        @pl.when(step > 0)
        def _():
            dh_s[rows, :] += back

    db1_ref[pl.ds(step, 1), :] = db1
    dw_ref[:, 0, 0] = dot_nn(h1t_ref[...], ep_s[...]).astype(BF).reshape(RB, RP, D)
    dw_ref[:, 0, 1] = dot_nn(e2t_ref[...], u_ref[...]).astype(BF).reshape(RB, RP, D)

    @pl.when(step == 3)
    def _():
        assemble(tab[20], same_ref, other_ref, 0, wo_s, 0)
        sums = [jnp.zeros((1, D), F32) for _ in range(3)]
        for i in range(3):
            rows = slice(i * BLK, (i + 1) * BLK)
            dh = dh_s[rows, :]
            hat = hat1_ref[rows, :]
            dz1 = norm_back(dh, vec_ref[3:4, :], hat, root1_ref[rows, :])
            dz1_ref[rows, :] = dz1
            e1 = dz1.astype(BF)
            e1t_s[:, rows] = e1.T
            do_ref[rows, :] = dot_nn(e1, wo_s[...]).astype(BF)
            sums[0] += jnp.sum(dz1, 0, keepdims=True)
            sums[1] += jnp.sum(dh * hat, 0, keepdims=True)
            sums[2] += jnp.sum(dh, 0, keepdims=True)
        for n in range(3):
            sums_ref[n : n + 1, :] = sums[n]
        dwo_ref[...] = dot_nn(e1t_s[...], o_ref[...]).astype(BF).reshape(RB, RP, D)


def input_kernel(tab, dq_ref, dk_ref, dv_ref, same_ref, other_ref, dz1_ref, own_ref, rest_ref, w_s):
    step = pl.program_id(0)

    @pl.when(step == 0)
    def _():
        for part in range(3):
            assemble(tab[20], same_ref, other_ref, part, w_s, D * part)

    back = dot_nt(dk_ref[...], w_s[:, D : 2 * D]) + dot_nt(dv_ref[...], w_s[:, 2 * D :])

    @pl.when(step < 3)
    def _():
        own_ref[...] = back + dot_nt(dq_ref[...], w_s[:, :D]) + dz1_ref[...]

    @pl.when(step >= 3)
    def _():
        rest_ref[...] = back.astype(BF)


def call(kernel, grid, in_specs, out_specs, out_shape, scratch, flops, bytes_accessed, name):
    return pl.pallas_call(
        kernel,
        grid_spec=pltpu.PrefetchScalarGridSpec(
            num_scalar_prefetch=1, grid=(grid,), in_specs=in_specs, out_specs=out_specs, scratch_shapes=scratch
        ),
        out_shape=out_shape,
        compiler_params=pltpu.CompilerParams(
            dimension_semantics=("arbitrary",), vmem_limit_bytes=VMEM_LIMIT
        ),
        cost_estimate=pl.CostEstimate(flops=flops, bytes_accessed=bytes_accessed, transcendentals=0),
        name=name,
    )


def whole(*shape):
    return pl.BlockSpec(shape, lambda s, t: (0,) * len(shape))


def columns(rows, width=128):
    return pl.BlockSpec((rows, width), lambda s, t: (0, s))


def shape_of(shape, dtype):
    return jax.ShapeDtypeStruct(shape, dtype)


def vm(shape, dtype):
    return pltpu.VMEM(shape, dtype)


def attend(tab, own, nb, mid, same, other, vectors):
    w_spec = pl.BlockSpec((4, 3, RP, 128), lambda s, t: (0, 0, 0, s))
    return call(
        attend_kernel,
        PAIRS,
        [whole(ROWS, D), whole(ROWS, D), whole(2 * BLK, D), w_spec, w_spec, columns(12)],
        [columns(ROWS), columns(ROWS), columns(ROWS), columns(8 * BLK), columns(8 * BLK)],
        [shape_of((ROWS, D), BF)] * 3 + [shape_of((8 * BLK, D), BF)] * 2,
        [vm((D, 384), BF)] + [vm((8, BLK, 128), BF)] * 4,
        28_000_000_000,
        16_000_000,
        "attend",
    )(tab, own, nb, mid, same, other, vectors)


def attend_back(tab, qe, qo, k, v, d_out, o, xt):
    return call(
        attend_back_kernel,
        PAIRS,
        [columns(ROWS), columns(ROWS), columns(8 * BLK), columns(8 * BLK), columns(ROWS), columns(ROWS), whole(D, 8 * BLK)],
        [
            columns(ROWS),
            columns(8 * BLK),
            columns(8 * BLK),
            pl.BlockSpec((RB, 3, RP, 128), lambda s, t: (0, 0, 0, s)),
            columns(2),
        ],
        [
            shape_of((ROWS, D), BF),
            shape_of((8 * BLK, D), BF),
            shape_of((8 * BLK, D), BF),
            shape_of((RB, 3, RP, D), BF),
            shape_of((2, D), F32),
        ],
        [vm((8, BLK, 128), BF)] * 4
        + [vm((8, 128, BLK), BF)]
        + [vm((8, BLK, 128), F32)] * 2
        + [vm((8 * BLK, BLK), BF)],
        50_000_000_000,
        24_000_000,
        "attend_back",
    )(tab, qe, qo, k, v, d_out, o, xt)


def feed(tab, o, x, same, other, vectors, w, cot, weight):
    wo_spec = pl.BlockSpec((4, 1, RP, D), lambda s, t: (0, 3, 0, 0))
    return call(
        feed_kernel,
        4,
        [
            whole(ROWS, D),
            whole(ROWS, D),
            wo_spec,
            wo_spec,
            whole(12, D),
            pl.BlockSpec((RB, 1, 2, RP, D), lambda s, t: (0, s, 0, 0, 0)),
            whole(ROWS, D),
            whole(ROWS, 1),
        ],
        [
            columns(ROWS, D),
            columns(ROWS, D),
            whole(ROWS, D),
            whole(ROWS, D),
            whole(ROWS, D),
            whole(D, ROWS),
            whole(D, ROWS),
            whole(ROWS, D),
            whole(ROWS, 1),
            whole(3, D),
        ],
        [
            shape_of((ROWS, FF), BF),
            shape_of((ROWS, FF), BF),
            shape_of((ROWS, D), BF),
            shape_of((ROWS, D), F32),
            shape_of((ROWS, D), BF),
            shape_of((D, ROWS), BF),
            shape_of((D, ROWS), BF),
            shape_of((ROWS, D), F32),
            shape_of((ROWS, 1), F32),
            shape_of((3, D), F32),
        ],
        [vm((D, D), BF), vm((ROWS, D), F32), vm((ROWS, D), BF), vm((ROWS, D), F32)],
        18_000_000_000,
        40_000_000,
        "feed",
    )(tab, o, x, same, other, vectors, w, cot, weight)


def feed_back(tab, e2, e2t, h1t, u, gp, w, dz2, hat1, root1, o, same, other, vectors):
    wo_spec = pl.BlockSpec((4, 1, RP, D), lambda s, t: (0, 3, 0, 0))
    w_spec = pl.BlockSpec((RB, 1, 2, RP, D), lambda s, t: (0, s, 0, 0, 0))
    return call(
        feed_back_kernel,
        4,
        [
            whole(ROWS, D),
            whole(D, ROWS),
            whole(D, ROWS),
            columns(ROWS, D),
            columns(ROWS, D),
            w_spec,
            whole(ROWS, D),
            whole(ROWS, D),
            whole(ROWS, 1),
            whole(ROWS, D),
            wo_spec,
            wo_spec,
            whole(12, D),
        ],
        [w_spec, whole(ROWS, D), whole(ROWS, D), whole(RB, RP, D), whole(3, D), whole(4, D)],
        [
            shape_of((RB, 4, 2, RP, D), BF),
            shape_of((ROWS, D), F32),
            shape_of((ROWS, D), BF),
            shape_of((RB, RP, D), BF),
            shape_of((3, D), F32),
            shape_of((4, D), F32),
        ],
        [vm((ROWS, D), BF), vm((ROWS, D), F32), vm((D, D), BF), vm((D, ROWS), BF)],
        24_000_000_000,
        48_000_000,
        "feed_back",
    )(tab, e2, e2t, h1t, u, gp, w, dz2, hat1, root1, o, same, other, vectors)


def input_back(tab, dq, dk, dv, same, other, dz1):
    w_spec = pl.BlockSpec((4, 3, RP, D), lambda s, t: (0, 0, 0, 0))
    first = pl.BlockSpec((BLK, D), lambda s, t: (jnp.minimum(s, 2), 0))
    each = pl.BlockSpec((BLK, D), lambda s, t: (s, 0))
    return call(
        input_kernel,
        8,
        [first, each, each, w_spec, w_spec, first],
        [first, pl.BlockSpec((BLK, D), lambda s, t: (jnp.maximum(s - 3, 0), 0))],
        [shape_of((ROWS, D), F32), shape_of((5 * BLK, D), BF)],
        [vm((D, 3 * D), BF)],
        6_000_000_000,
        16_000_000,
        "input_back",
    )(tab, dq, dk, dv, same, other, dz1)


def adamw(weight, grad, first, second, rate, decay, clip_factor):
    clipped = grad * clip_factor
    first_new = BETA_ONE * first + (1.0 - BETA_ONE) * clipped
    second_new = BETA_TWO * second + (1.0 - BETA_TWO) * clipped * clipped
    first_hat = first_new / (1.0 - BETA_ONE**STEP)
    second_hat = second_new / (1.0 - BETA_TWO**STEP)
    updated = weight * (1.0 - rate * decay) - rate * first_hat / (jnp.sqrt(second_hat) + ADAM_EPS)
    return (clipped, first_new, second_new, updated)


def shards(
    tokens,
    out_cotangent,
    lengths,
    starts,
    ends,
    flags,
    qkv_master,
    proj_master,
    up_master,
    down_master,
    vectors,
    qkv_first,
    proj_first,
    up_first,
    down_first,
    qkv_second,
    proj_second,
    up_second,
    down_second,
    vector_first,
    vector_second,
):
    mp_count = lax.axis_size("mp")
    dp_count = lax.axis_size("dp")
    devices = mp_count * dp_count
    z = lax.axis_index("mp")
    dp_index = lax.axis_index("dp")
    core = dp_index % 2
    chips = dp_count // 2
    part = D // dp_count
    head_cols = D // mp_count

    def linear(chip, core_of, z_of):
        return (chip * 2 + core_of) * mp_count + z_of

    planes = [[linear(chip, c, k) for chip in range(chips)] for c in range(2) for k in range(mp_count)]
    swap_core = [
        (linear(chip, c, k), linear(chip, 1 - c, k)) for chip in range(chips) for c in range(2) for k in range(mp_count)
    ]
    swap_z = [
        (linear(chip, c, k), linear(chip, c, k ^ 1)) for chip in range(chips) for c in range(2) for k in range(mp_count)
    ]
    middle = (0, 2, 1, 3)
    swap_mid = [
        (linear(chip, c, k), linear(chip, c, middle[k])) for chip in range(chips) for c in range(2) for k in range(mp_count)
    ]

    def over_plane(value):
        return lax.all_to_all(value, AXES, 0, 0, tiled=True, axis_index_groups=planes)

    def over_z(value):
        return lax.all_to_all(value, "mp", 0, 0, tiled=True)

    mine = jnp.concatenate(
        [qkv_master[0], qkv_master[1], qkv_master[2], proj_master.T], 1
    ).astype(BF)
    along_z = over_z(jnp.broadcast_to(mine[None], (mp_count, part, D)))
    along_z = along_z.reshape(mp_count, part, 4, head_cols).transpose(2, 1, 0, 3).reshape(4, part, D)
    same = over_plane(jnp.broadcast_to(along_z[None], (chips, 4, part, D)))
    other = lax.ppermute(same, AXES, swap_core)
    kernel_core = core
    if part != RP:
        both = jnp.where(core == 0, jnp.stack([same, other], 1), jnp.stack([other, same], 1))
        both = both.transpose(2, 0, 1, 3, 4).reshape(4, RB // 2, 2, RP, D).transpose(1, 2, 0, 3, 4)
        same, other = both[:, 0], both[:, 1]
        kernel_core = jnp.zeros((), jnp.int32)
    feed_mine = jnp.stack([up_master, down_master.T]).astype(BF)
    feed_w = lax.all_gather(feed_mine, AXES, axis=0, tiled=False).reshape(dp_count, mp_count, 2, part, D)
    if part != RP:
        feed_w = feed_w.transpose(1, 2, 0, 3, 4).reshape(mp_count, 2, RB, RP, D).transpose(2, 0, 1, 3, 4)

    mid_at = jnp.where(z == 1, BLK, 0)
    nb = lax.ppermute(tokens, AXES, swap_z)
    mid = lax.ppermute(lax.dynamic_slice_in_dim(tokens, mid_at, 2 * BLK, 0), AXES, swap_mid)
    xt = jnp.concatenate([tokens, nb, mid], 0).T

    place = jnp.asarray(BLOCK_PLACE)[z]
    counts = jnp.clip(lengths[jnp.asarray(BLOCK_SEQ)[z]] - BLK * place, 0, BLK)
    tab = jnp.concatenate(
        [jnp.asarray(KEY_BLOCKS)[z].reshape(12), counts, kernel_core.reshape(1)]
    ).astype(jnp.int32)

    positions = z * ROWS + jnp.arange(ROWS, dtype=jnp.int32)
    seq_of = positions // LEN
    within = positions % LEN
    picker = (seq_of[:, None] == jnp.arange(lengths.shape[0], dtype=jnp.int32)[None, :]).astype(jnp.int32)
    length_row = jnp.sum(picker * lengths[None, :], 1)
    start_row = jnp.sum(picker * starts[None, :], 1)
    end_row = jnp.sum(picker * ends[None, :], 1)
    flag_row = jnp.sum(picker * flags[None, :], 1).astype(F32)
    valid_row = (within < length_row).astype(F32)
    answer = (within == start_row).astype(F32) + (within == end_row).astype(F32)
    opening = (within == 0).astype(F32)
    row_weight = valid_row * (1.0 + 2.0 * (1.0 - flag_row) * answer + 4.0 * flag_row * opening)

    o, qe, qo, k, v = attend(tab, tokens, nb, mid, same, other, vectors)
    u, gp, block_out, dz2, e2, e2t, h1t, hat1, root1, sums_two = feed(
        tab, o, tokens, same, other, vectors, feed_w, out_cotangent, row_weight[:, None]
    )
    feed_dw, dz1, d_o, wo_dw, sums_one, bias_up_grad = feed_back(
        tab, e2, e2t, h1t, u, gp, feed_w, dz2, hat1, root1, o, same, other, vectors
    )

    def to_parts(grad):
        if part == RP:
            return grad
        lead = grad.shape[1:-2]
        moved = jnp.moveaxis(grad, 0, -3).reshape(*lead, dp_count, part, D)
        return jnp.moveaxis(moved, -3, 0)

    feed_dw = to_parts(feed_dw)
    feed_sum = lax.psum_scatter(feed_dw, "dp", scatter_dimension=0, tiled=False)
    feed_sum = lax.psum_scatter(feed_sum, "mp", scatter_dimension=0, tiled=False).astype(F32)

    dq, dk, dv, qkv_dw, sums_head = attend_back(tab, qe, qo, k, v, d_o, o, xt)
    head_dw = to_parts(jnp.concatenate([qkv_dw, wo_dw[:, None]], 1))
    head_dw = head_dw.reshape(chips, 2, 4, part, D)
    keep = lax.dynamic_index_in_dim(head_dw, core, 1, keepdims=False)
    give = lax.dynamic_index_in_dim(head_dw, 1 - core, 1, keepdims=False)
    got = lax.ppermute(give, AXES, swap_core)
    chip_sum = (keep.astype(F32) + got.astype(F32)).astype(BF)
    plane_sum = jnp.sum(over_plane(chip_sum).astype(F32), 0)
    plane_sum = plane_sum.astype(BF).reshape(4, part, mp_count, head_cols).transpose(2, 1, 0, 3)
    head_sum = jnp.sum(over_z(plane_sum.reshape(mp_count, part, D)).astype(F32), 0)

    dx_own, dx_rest = input_back(tab, dq, dk, dv, same, other, dz1)
    from_nb = lax.ppermute(dx_rest[: 3 * BLK], AXES, swap_z)
    from_mid = lax.ppermute(dx_rest[3 * BLK :], AXES, swap_mid)
    zero_block = jnp.zeros((BLK, D), BF)
    from_mid = jnp.where(
        z == 1, jnp.concatenate([zero_block, from_mid], 0), jnp.concatenate([from_mid, zero_block], 0)
    )
    input_grad = dx_own + from_nb.astype(F32) + from_mid.astype(F32)

    vector_part = jnp.concatenate([sums_head, sums_one, sums_two, bias_up_grad], 0)
    vec_columns = D // devices
    vector_part = vector_part.reshape(12, devices, vec_columns).transpose(1, 0, 2)
    vector_grad = jnp.sum(lax.all_to_all(vector_part, AXES, 0, 0, tiled=True), 0)

    qkv_sum = jnp.stack([head_sum[:, n * head_cols : (n + 1) * head_cols] for n in range(3)])
    proj_sum = head_sum[:, 3 * head_cols :].T
    up_sum = feed_sum[0]
    down_sum = feed_sum[1].T
    local_squares = jnp.sum(head_sum * head_sum) + jnp.sum(feed_sum * feed_sum) + jnp.sum(vector_grad * vector_grad)
    squares = lax.all_to_all(jnp.broadcast_to(local_squares, (devices,)), AXES, 0, 0, tiled=True)
    grad_norm = jnp.sqrt(jnp.sum(squares))
    clip_factor = jnp.minimum(1.0, CLIP_NORM / (grad_norm + 1e-06))
    matrix_rate = MATRIX_RATE / math.sqrt(D)
    vec_index = dp_index * mp_count + z
    vector_shard = lax.dynamic_slice_in_dim(vectors, vec_index * vec_columns, vec_columns, 1)
    qkv_set = adamw(qkv_master, qkv_sum, qkv_first, qkv_second, matrix_rate, WEIGHT_DECAY, clip_factor)
    proj_set = adamw(proj_master, proj_sum, proj_first, proj_second, matrix_rate, WEIGHT_DECAY, clip_factor)
    up_set = adamw(up_master, up_sum, up_first, up_second, matrix_rate, WEIGHT_DECAY, clip_factor)
    down_set = adamw(down_master, down_sum, down_first, down_second, matrix_rate, WEIGHT_DECAY, clip_factor)
    vector_set = adamw(vector_shard, vector_grad, vector_first, vector_second, VECTOR_RATE, 0.0, clip_factor)
    return (block_out, input_grad, grad_norm, *qkv_set, *proj_set, *up_set, *down_set, *vector_set)


def solution(mesh):
    rows = P(AXES, None)
    group = P("dp")
    qkv = P(None, "dp", "mp")
    proj = P("mp", "dp")
    up = P("dp", "mp")
    vec = P(None, AXES)
    return jax.shard_map(
        shards,
        mesh=mesh,
        in_specs=(rows, rows, group, group, group, group)
        + (qkv, proj, up, proj, P())
        + (qkv, proj, up, proj) * 2
        + (vec, vec),
        out_specs=(rows, rows, P()) + (qkv,) * 4 + (proj,) * 4 + (up,) * 4 + (proj,) * 4 + (vec,) * 4,
        check_vma=False,
    )
```

time: 1390 us -> 432 us (0.31)
  waiting for transfers between devices: 649 us -> 80 us
  matrix products: 418 us -> 0 us
  Pallas kernels: 0 us -> 162 us
  local copies, waits for them, and re-layouts: 77 us -> 22.1 us
  loops' own time: 39.7 us -> 0 us
  starting transfers between devices: 0.64 us -> 38.2 us
  blocking collectives: 107 us -> 70.1 us
  other arithmetic: 67.3 us -> 32.5 us
    dot_general x60 -> x0, matrix products: 418 us -> none  [the longest x6 103 us: attend_back(): jnp.einsum('hqk,qhd->khd', score_grad, query_block, preferred_element_typ...]
    reduce_scatter x4 -> x2, waiting for transfers between devices: 324 us -> 5.13 us  [the longest x1 5.13 us: shards(): feed_sum = lax.psum_scatter(feed_dw, 'dp', scatter_dimension=0, tiled=False)]
    all_gather x6 -> x1, waiting for transfers between devices: 311 us -> 0.02 us  [shards(): lax.all_gather(feed_mine, AXES, axis=0, tiled=False)]
    pallas_call x0 -> x5, Pallas kernels: none -> 162 us  [the longest x1 54 us: attend_back(): call(attend_back_kernel, PAIRS, [columns(ROWS), columns(ROWS), columns(8...]
    all_to_all x0 -> x2, blocking collectives: none -> 70.1 us  [the longest x1 41.7 us: over_plane(): lax.all_to_all(value, AXES, 0, 0, tiled=True, axis_index_groups=planes)]
    unnamed x1 -> x0, blocking collectives: 44.1 us -> none
    another operation x2 -> x0, loops' own time: 39.7 us -> none  [the longest x1 23.9 us: shards(): query_grads, key_grads, value_grads = lax.map(attend_back, block_ids)]
    psum x1 -> x0, blocking collectives: 39.4 us -> none  [shards(): grad_norm = jnp.sqrt(lax.psum(local_squares, ('dp', 'mp')))]
  transfers between devices with their start and end apart: 11 -> 13, of which waited for: 8 -> 6; matrix products, arithmetic and copies ran while one was open for 7% -> 9% of each run, Pallas kernels for 0% -> 24%
where the time goes in v1:
time: 432 us; the launch traced here: 423 us
  Pallas kernels  162 us (38%)
  waiting for transfers between devices  80 us (19%)
  blocking collectives  70.1 us (16%)
  starting transfers between devices  38.2 us (9%)
  other arithmetic  32.5 us (8%)
  local copies, waits for them, and re-layouts  22.1 us (5%)
  between operations  18.3 us (4%)
    pallas_call x1, Pallas kernels, attend_back(): call(attend_back_kernel, PAIRS, [columns(ROWS), columns(ROWS), columns(8...  54 us
    all_to_all x1, blocking collectives, over_plane(): lax.all_to_all(value, AXES, 0, 0, tiled=True, axis_index_groups=planes)  41.7 us
    ppermute x1, waiting for transfers between devices, shards(): nb = lax.ppermute(tokens, AXES, swap_z)  32.5 us
    pallas_call x1, Pallas kernels, feed_back(): call(feed_back_kernel, 4, [whole(ROWS, D), whole(D, ROWS), whole(D, ROWS)...  32.4 us
    pallas_call x1, Pallas kernels, attend(): call(attend_kernel, PAIRS, [whole(ROWS, D), whole(ROWS, D), whole(2 * BLK...  31.3 us
    pallas_call x1, Pallas kernels, feed(): call(feed_kernel, 4, [whole(ROWS, D), whole(ROWS, D), wo_spec, wo_spec, w...  30.1 us
    all_to_all x1, blocking collectives, over_z(): return lax.all_to_all(value, 'mp', 0, 0, tiled=True)  28.3 us
    all_to_all x1, waiting for transfers between devices, shards(): lax.all_to_all(vector_part, AXES, 0, 0, tiled=True)  22.3 us
  transfers between devices with their start and end apart: 13, of which 6 were waited for; matrix products, arithmetic and copies ran while one was open for 9% of the time, Pallas kernels for 24%

profile of v1, /device:TPU:0, one launch (start us, length us, event | category | flops | bytes accessed | tf_op | source)
XLA Modules:
  0.0 423.4 jit_solution(4742257572876693153)
XLA Ops:
  7.2 1.0 convert_bitcast_fusion
  8.2 1.0 convert_bitcast_fusion.1
  9.2 0.7 pad_maximum_fusion
  10.0 1.1 copy.176
  11.1 0.9 convert_bitcast_fusion.2
  12.3 28.3 %all_to_all.31 = bf16[4,96,768]{2,1,0:T(8,128)(2,1)S(1)} all-to-all(bf16[4,96,768]{2,1,0:T(8,128)(2,1)S(1)} %broadcast_in_dim.8), channel_id=1, replica_groups=mesh['dp'=8,'mp'=4] {'mp'}, dimensions={0} | all-to-all | bytes 1179648 | tf_op jit(solution)/shard_map/all_to_all | solution.py:673
  42.9 41.7 %all_to_all.32.same_ref = bf16[4,4,96,768]{3,2,1,0:T(8,128)(2,1)} all-to-all(bf16[4,4,96,768]{3,2,1,0:T(8,128)(2,1)S(1)} %broadcast_in_dim.10), channel_id=1, replica_groups={{0,8,16,24},{1,9,17,25},{2,10,18,26},{3,11,19,27},{4,12,20,28},{5,13,21..., dimensions={0} | all-to-all | bytes 4718592 | tf_op jit(solution)/shard_map/all_to_all | solution.py:670
  85.4 0.7 collective-permute-start
  86.1 0.9 constant_dynamic-slice_fusion
  87.1 1.8 collective-permute-start.1
  92.4 1.4 fusion.7.weight_ref
  93.8 1.2 copy.180.mid_ref
  95.0 32.5 %collective-permute-done = bf16[768,768]{0,1:T(8,128)(2,1)S(1)} collective-permute-done((bf16[768,768]{0,1:T(8,128)(2,1)S(1)}, bf16[768,768]{0,1:T(8,128)(2,1)S(1)}, u32[]{:S(2)}, u32[]{:S(2)}) %collective-permute-start) | collective-permute-done | bytes 1179680 | tf_op jit(solution)/shard_map/ppermute | solution.py:694
  127.5 1.4 copy.179.nb_ref
  128.9 31.3 %attend.1 = (bf16[768,768]{1,0:T(8,128)(2,1)}, bf16[768,768]{1,0:T(8,128)(2,1)}, bf16[768,768]{1,0:T(8,128)(2,1)}, bf16[2048,768]{1,0:T(8,128)(2,1)}, bf16[2048,768]{1,0:T(8,128)(2,1)}) custom-call(s32[21]{0:T(128)} %pad_add_fusion.tab, bf16[768,768]{1,0:T(8,128)(2,1)} %x_ref.1, bf16[768,768]{1,0:T(8,128)(2,1)} %copy.179.nb_ref, ...), custom_call_target="tpu_custom_call" | custom-call | flops 28000000000 | bytes 16000000 | tf_op jit(solution)/shard_map/attend/pallas_call | solution.py:469
  160.3 30.1 %feed.1 = (bf16[768,3072]{1,0:T(8,128)(2,1)}, bf16[768,3072]{1,0:T(8,128)(2,1)}, bf16[768,768]{1,0:T(8,128)(2,1)}, f32[768,768]{1,0:T(8,128)}, bf16[768,768]{1,0...) custom-call(s32[21]{0:T(128)} %pad_add_fusion.tab, ...), custom_call_target="tpu_custom_call" | custom-call | flops 17999998976 | bytes 40000000 | tf_op jit(solution)/shard_map/feed/pallas_call | solution.py:513
  190.3 32.4 %feed_back.1 = (bf16[8,4,2,96,768]{4,3,2,1,0:T(8,128)(2,1)}, f32[768,768]{1,0:T(8,128)}, bf16[768,768]{1,0:T(8,128)(2,1)}, bf16[8,96,768]{2,1,0:T(8,128)(2,1)}, f32[3,768]{1,0:T(4,128)}, /*index=5*/f32[4,768]{1,0:T(4,128)}) custom-call(s32[21]{0:T(128)} %pad_add_fusion.tab, bf16[768,768]{1,0:T(8,128)(2,1)} %get-tuple-element.57.e2_ref, ...), custom_call_target="tpu_custom_call" | custom-call | flops 24000000000 | bytes 48000000 | tf_op jit(solution)/shard_map/feed_back/pallas_call | solution.py:560
  222.8 1.9 maximum_bitcast_fusion.xt_ref
  224.7 54.0 %attend_back.1 = (bf16[768,768]{1,0:T(8,128)(2,1)}, bf16[2048,768]{1,0:T(8,128)(2,1)}, bf16[2048,768]{1,0:T(8,128)(2,1)}, bf16[8,3,96,768]{3,2,1,0:T(8,128)(2,1)}, f32[2,768]{1,0:T(2,128)}) custom-call(s32[21]{0:T(128)} %pad_add_fusion.tab, bf16[768,768]{1,0:T(8,128)(2,1)} %get-tuple-element.53.qe_ref, bf16[768,768]{1,0:T(8,128)(2,1)} %get-tuple-element.54.qo_ref, ...), custom_call_target="tpu_custom_call" | custom-call | flops 49999998976 | bytes 24000000 | tf_op jit(solution)/shard_map/attend_back/pallas_call | solution.py:483
  278.8 3.4 fusion.2
  282.1 4.9 %collective-permute-done.5 = bf16[4,4,96,768]{3,2,1,0:T(8,128)(2,1)} collective-permute-done((bf16[4,4,96,768]{3,2,1,0:T(8,128)(2,1)}, bf16[4,4,96,768]{3,2,1,0:T(8,128)(2,1)}, u32[]{:S(2)}, u32[]{:S(2)}) %collective-permute-start.5) | collective-permute-done | bytes 2359328 | tf_op jit(solution)/shard_map/ppermute | solution.py:741
  287.0 3.9 fusion
  290.9 3.7 all-to-all-start.2
  294.6 5.1 %reduce-scatter.3.cloned.1.call-done = bf16[1,4,2,96,768]{4,3,2,1,0:T(8,128)(2,1)} async-done(((bf16[8,4,2,96,768]{4,3,2,1,0:T(8,128)(2,1)}), bf16[1,4,2,96,768]{4,3,2,1,0:T(8,128)(2,1)}) %reduce-scatter.3.cloned.1.call-update) | async-done | bytes 1179664 | tf_op jit(solution)/shard_map/reduce_scatter | solution.py:733
  299.7 14.3 %input_back.1 = (f32[768,768]{1,0:T(8,128)}, bf16[1280,768]{1,0:T(8,128)(2,1)}) custom-call(s32[21]{0:T(128)} %pad_add_fusion.tab, bf16[768,768]{1,0:T(8,128)(2,1)} %get-tuple-element.66.dq_ref, bf16[2048,768]{1,0:T(8,128)(2,1)} %get-tuple-element.67.dk_ref, bf16[2048,768]{1,0:T(8,128)(2,1)} %get-tuple-element.68.dv_ref, ...), custom_call_target="tpu_custom_call" | custom-call | flops 6000000000 | bytes 16000000 | tf_op jit(solution)/shard_map/input_back/pallas_call | solution.py:598
  314.1 2.4 slice.41
  316.5 15.3 %collective-permute-start.3 = (bf16[768,768]{1,0:T(8,128)(2,1)}, bf16[768,768]{1,0:T(8,128)(2,1)}, u32[]{:S(2)}, u32[]{:S(2)}) collective-permute-start(bf16[768,768]{1,0:T(8,128)(2,1)} %slice.41), channel_id=1, source_target_pairs={{0,1},{1,0},{2,3},{3,2},{4,5},{5,4},{6,7},{7,6},{8,9},{9,8},{10,11... | collective-permute-start | bytes 3538952 | tf_op jit(solution)/shard_map/ppermute | solution.py:748
  331.7 2.1 slice.42
  333.8 7.4 %collective-permute-start.4 = (bf16[512,768]{1,0:T(8,128)(2,1)}, bf16[512,768]{1,0:T(8,128)(2,1)}, u32[]{:S(2)}, u32[]{:S(2)}) collective-permute-start(bf16[512,768]{1,0:T(8,128)(2,1)} %slice.42), channel_id=1, source_target_pairs={{0,0},{1,2},{2,1},{3,3},{4,4},{5,6},{6,5},{7,7},{8,8},{9,10},{10,9... | collective-permute-start | bytes 2359304 | tf_op jit(solution)/shard_map/ppermute | solution.py:749
  341.6 0.8 reshape.327
  342.4 2.9 all-to-all-start.4
  347.2 1.5 reshape.316
  348.8 22.3 %all-to-all-done.4 = f32[32,1,288]{2,1,0:T(1,128)S(1)} async-done(((f32[32,1,288]{2,1,0:T(1,128)}), f32[32,1,288]{2,1,0:T(1,128)S(1)}, u32[]{:S(2)}, u32[]{:S(2)}) %all-to-all-start.4) | async-done | bytes 36896 | tf_op jit(solution)/shard_map/all_to_all | solution.py:759
  371.0 3.5 all-to-all-start.3
  375.4 0.8 reduce.3
  376.9 4.2 %convert_add_fusion.1 = f32[768,768]{1,0:T(8,128)} fusion(f32[768,768]{1,0:T(8,128)} %get-tuple-element.70, bf16[768,768]{1,0:T(8,128)(2,1)} %collective-permute-done.3, bf16[512,768]{1,0:T(8,128)(2,1)} %collective-permute-done.4, pred[]{:T(512)S(6)} %eq.52), kind=kLoop, calls=%fused_computation.12 | loop fusion | flops 2949120 | bytes 6684673 | tf_op jit(solution)/shard_map/add | solution.py:754
  381.2 9.3 %all-to-all-done.3 = bf16[4,96,768]{2,1,0:T(8,128)(2,1)S(1)} async-done(((bf16[4,96,768]{2,1,0:T(8,128)(2,1)}), bf16[4,96,768]{2,1,0:T(8,128)(2,1)S(1)}, u32[]{:S(2)}, u32[]{:S(2)}) %all-to-all-start.3) | async-done | bytes 589856 | tf_op jit(solution)/shard_map/all_to_all | solution.py:673
  391.2 1.7 multiply_reduce_fusion
  395.5 2.8 all-to-all-start.5
  398.4 1.1 convert_element_type.84
  399.4 5.9 %all-to-all-done.5 = f32[32,1,1]{2,1,0:T(1,128)S(1)} async-done(((f32[32,1,1]{2,1,0:T(1,128)}), f32[32,1,1]{2,1,0:T(1,128)S(1)}, u32[]{:S(2)}, u32[]{:S(2)}) %all-to-all-start.5) | async-done | bytes 160 | tf_op jit(solution)/shard_map/all_to_all | solution.py:766
  406.9 0.7 copy.194
  407.6 0.7 copy.195
  408.4 0.7 copy.196
  409.9 1.1 divide_subtract_fusion.1
  411.0 2.0 divide_subtract_fusion
  413.0 1.4 divide_subtract_fusion.4
  414.4 1.1 divide_subtract_fusion.2
  (100 shorter events, 13.7 us)
Async XLA Ops:
  7.2 153.1 %all-gather.2.cloned.1.call-start = ((), (), s32[]{:S(2)}) async-start(), calls=%async_computation.8 | async-start | bytes 9732096 | tf_op jit(solution)/shard_map/all_gather | solution.py:689
  10.0 289.8 %reduce-scatter.3.cloned.1.call-start = ((), (), s32[]{:S(2)}) async-start(), calls=%async_computation.9 | async-start | bytes 10616832 | tf_op jit(solution)/shard_map/reduce_scatter | solution.py:733
  42.9 41.9 %copy-start.5 = (bf16[768,768]{1,0:T(8,128)(2,1)S(1)}, bf16[768,768]{1,0:T(8,128)(2,1)}, u32[]{:S(2)}) copy-start(bf16[768,768]{1,0:T(8,128)(2,1)} %x_ref.1) | copy-start | bytes 3538948
  84.6 4.9 %copy-start = (s32[3]{0:T(128)S(1)}, s32[3]{0:T(128)}, u32[]{:S(2)}) copy-start(s32[3]{0:T(128)} %param.26) | copy-start | bytes 40
  84.6 7.6 %copy-start.20 = (s32[3]{0:T(128)S(1)}, s32[3]{0:T(128)}, u32[]{:S(2)}) copy-start(s32[3]{0:T(128)} %param.28) | copy-start | bytes 40
  84.6 7.6 %copy-start.21 = (s32[3]{0:T(128)S(1)}, s32[3]{0:T(128)}, u32[]{:S(2)}) copy-start(s32[3]{0:T(128)} %param.27) | copy-start | bytes 40
  84.6 7.6 %copy-start.22 = (s32[3]{0:T(128)S(1)}, s32[3]{0:T(128)}, u32[]{:S(2)}) copy-start(s32[3]{0:T(128)} %param.29) | copy-start | bytes 40
  84.6 44.3 %collective-permute-start.2 = (bf16[4,4,96,768]{3,2,1,0:T(8,128)(2,1)}, bf16[4,4,96,768]{3,2,1,0:T(8,128)(2,1)}, u32[]{:S(2)}, u32[]{:S(2)}) collective-permute-start(bf16[4,4,96,768]{3,2,1,0:T(8,128)(2,1)} %all_to_all.32.same_ref), channel_id=1, source_target_pairs={{0,4},{1,5},{2,6},{3,7},{4,0},{5,1},{6,2},{7,3},{8,12},{9,13},{10,... | collective-permute-start | bytes 7077896 | tf_op jit(solution)/shard_map/ppermute | solution.py:681
  85.4 42.1 %collective-permute-start = (bf16[768,768]{0,1:T(8,128)(2,1)S(1)}, bf16[768,768]{0,1:T(8,128)(2,1)S(1)}, u32[]{:S(2)}, u32[]{:S(2)}) collective-permute-start(bf16[768,768]{0,1:T(8,128)(2,1)S(1)} %copy.174), channel_id=1, source_target_pairs={{0,1},{1,0},{2,3},{3,2},{4,5},{5,4},{6,7},{7,6},{8,9},{9,8},{10,11... | collective-permute-start | bytes 3538952 | tf_op jit(solution)/shard_map/ppermute | solution.py:694
  87.1 6.8 %collective-permute-start.1 = (bf16[512,768]{0,1:T(8,128)(2,1)}, bf16[512,768]{0,1:T(8,128)(2,1)S(1)}, u32[]{:S(2)}, u32[]{:S(2)}) collective-permute-start(bf16[512,768]{0,1:T(8,128)(2,1)} %constant_dynamic-slice_fusion), channel_id=1, source_target_pairs={{0,0},{1,2},{2,1},{3,3},{4,4},{5,6},{6,5},{7,7},{8,8},{9,10},{10,9... | collective-permute-start | bytes 2359304 | tf_op jit(solution)/shard_map/ppermute | solution.py:695
  278.8 8.3 %copy-start.1 = (bf16[8,3,96,768]{3,2,1,0:T(8,128)(2,1)S(1)}, bf16[8,3,96,768]{3,2,1,0:T(8,128)(2,1)}, u32[]{:S(2)}) copy-start(bf16[8,3,96,768]{3,2,1,0:T(8,128)(2,1)} %get-tuple-element.72) | copy-start | bytes 10616836
  282.1 4.9 %collective-permute-start.5 = (bf16[4,4,96,768]{3,2,1,0:T(8,128)(2,1)}, bf16[4,4,96,768]{3,2,1,0:T(8,128)(2,1)}, u32[]{:S(2)}, u32[]{:S(2)}) collective-permute-start(bf16[4,4,96,768]{3,2,1,0:T(8,128)(2,1)} %fusion.2), channel_id=1, source_target_pairs={{0,4},{1,5},{2,6},{3,7},{4,0},{5,1},{6,2},{7,3},{8,12},{9,13},{10,... | collective-permute-start | bytes 7077896 | tf_op jit(solution)/shard_map/ppermute | solution.py:741
  290.9 51.5 %all-to-all-start.2 = ((bf16[4,4,96,768]{3,2,1,0:T(8,128)(2,1)}), bf16[4,4,96,768]{3,2,1,0:T(8,128)(2,1)S(1)}, u32[]{:S(2)}, u32[]{:S(2)}) async-start(bf16[4,4,96,768]{3,2,1,0:T(8,128)(2,1)} %fusion), calls=%async_computation.2 | async-start | bytes 4718592 | tf_op jit(solution)/shard_map/all_to_all | solution.py:670
  294.5 96.7 %reduce-scatter.5.cloned.1.call-start = ((), (), s32[]{:S(2)}) async-start(), calls=%async_computation.10 | async-start | bytes 1474560 | tf_op jit(solution)/shard_map/reduce_scatter | solution.py:734
  314.0 27.2 %copy-start.14 = (f32[3,768]{1,0:T(4,128)S(1)}, f32[3,768]{1,0:T(4,128)}, u32[]{:S(2)}) copy-start(f32[3,768]{1,0:T(4,128)} %get-tuple-element.77) | copy-start | bytes 27652
  314.0 27.2 %copy-start.15 = (f32[3,768]{1,0:T(4,128)S(1)}, f32[3,768]{1,0:T(4,128)}, u32[]{:S(2)}) copy-start(f32[3,768]{1,0:T(4,128)} %get-tuple-element.76) | copy-start | bytes 27652
  314.0 27.2 %copy-start.16 = (f32[4,768]{1,0:T(4,128)S(1)}, f32[4,768]{1,0:T(4,128)}, u32[]{:S(2)}) copy-start(f32[4,768]{1,0:T(4,128)} %get-tuple-element.78) | copy-start | bytes 36868
  314.1 27.2 %copy-start.19 = (f32[2,768]{1,0:T(2,128)S(1)}, f32[2,768]{1,0:T(2,128)}, u32[]{:S(2)}) copy-start(f32[2,768]{1,0:T(2,128)} %get-tuple-element.75) | copy-start | bytes 18436
  316.5 60.5 %collective-permute-start.3 = (bf16[768,768]{1,0:T(8,128)(2,1)}, bf16[768,768]{1,0:T(8,128)(2,1)}, u32[]{:S(2)}, u32[]{:S(2)}) collective-permute-start(bf16[768,768]{1,0:T(8,128)(2,1)} %slice.41), channel_id=1, source_target_pairs={{0,1},{1,0},{2,3},{3,2},{4,5},{5,4},{6,7},{7,6},{8,9},{9,8},{10,11... | collective-permute-start | bytes 3538952 | tf_op jit(solution)/shard_map/ppermute | solution.py:748
  333.8 43.1 %collective-permute-start.4 = (bf16[512,768]{1,0:T(8,128)(2,1)}, bf16[512,768]{1,0:T(8,128)(2,1)}, u32[]{:S(2)}, u32[]{:S(2)}) collective-permute-start(bf16[512,768]{1,0:T(8,128)(2,1)} %slice.42), channel_id=1, source_target_pairs={{0,0},{1,2},{2,1},{3,3},{4,4},{5,6},{6,5},{7,7},{8,8},{9,10},{10,9... | collective-permute-start | bytes 2359304 | tf_op jit(solution)/shard_map/ppermute | solution.py:749
  342.4 28.7 %all-to-all-start.4 = ((f32[32,1,288]{2,1,0:T(1,128)}), f32[32,1,288]{2,1,0:T(1,128)S(1)}, u32[]{:S(2)}, u32[]{:S(2)}) async-start(f32[32,1,288]{2,1,0:T(1,128)} %reshape.327), calls=%async_computation.6 | async-start | bytes 98304 | tf_op jit(solution)/shard_map/all_to_all | solution.py:759
  346.6 27.9 %copy-start.6 = (f32[192,96]{1,0:T(8,128)S(1)}, f32[192,96]{1,0:T(8,128)}, u32[]{:S(2)}) copy-start(f32[192,96]{1,0:T(8,128)} %param.31) | copy-start | bytes 221188
  346.6 28.0 %copy-start.12 = (f32[192,96]{1,0:T(8,128)S(1)}, f32[192,96]{1,0:T(8,128)}, u32[]{:S(2)}) copy-start(f32[192,96]{1,0:T(8,128)} %param.40) | copy-start | bytes 221188
  346.6 28.1 %copy-start.13 = (f32[192,96]{1,0:T(8,128)S(1)}, f32[192,96]{1,0:T(8,128)}, u32[]{:S(2)}) copy-start(f32[192,96]{1,0:T(8,128)} %param.36) | copy-start | bytes 221188
  371.0 19.4 %all-to-all-start.3 = ((bf16[4,96,768]{2,1,0:T(8,128)(2,1)}), bf16[4,96,768]{2,1,0:T(8,128)(2,1)S(1)}, u32[]{:S(2)}, u32[]{:S(2)}) async-start(bf16[4,96,768]{2,1,0:T(8,128)(2,1)} %reshape.316), calls=%async_computation.3 | async-start | bytes 1179648 | tf_op jit(solution)/shard_map/all_to_all | solution.py:673
  381.2 28.7 %copy-start.2 = (f32[96,768]{1,0:T(8,128)S(1)}, f32[96,768]{1,0:T(8,128)}, u32[]{:S(2)}) copy-start(f32[96,768]{1,0:T(8,128)} %param.32) | copy-start | bytes 884740
  381.2 28.7 %copy-start.7 = (f32[96,768]{1,0:T(8,128)S(1)}, f32[96,768]{1,0:T(8,128)}, u32[]{:S(2)}) copy-start(f32[96,768]{1,0:T(8,128)} %param.41) | copy-start | bytes 884740
  381.2 28.7 %copy-start.8 = (f32[96,768]{1,0:T(8,128)S(1)}, f32[96,768]{1,0:T(8,128)}, u32[]{:S(2)}) copy-start(f32[96,768]{1,0:T(8,128)} %param.37) | copy-start | bytes 884740
  395.5 9.9 %all-to-all-start.5 = ((f32[32,1,1]{2,1,0:T(1,128)}), f32[32,1,1]{2,1,0:T(1,128)S(1)}, u32[]{:S(2)}, u32[]{:S(2)}) async-start(f32[32,1,1]{2,1,0:T(1,128)} %broadcast_in_dim.11), calls=%async_computation.7 | async-start | bytes 32768 | tf_op jit(solution)/shard_map/all_to_all | solution.py:766
  398.4 12.6 %copy-start.3 = (f32[768,96]{0,1:T(8,128)S(1)}, f32[768,96]{0,1:T(8,128)}, u32[]{:S(2)}) copy-start(f32[768,96]{0,1:T(8,128)} %param.33) | copy-start | bytes 884740
  398.4 12.6 %copy-start.9 = (f32[768,96]{0,1:T(8,128)S(1)}, f32[768,96]{0,1:T(8,128)}, u32[]{:S(2)}) copy-start(f32[768,96]{0,1:T(8,128)} %param.42) | copy-start | bytes 884740
  409.9 3.2 copy-start.17
  409.9 3.2 copy-start.18
  409.9 4.5 %copy-start.4 = (f32[3,96,192]{2,1,0:T(8,128)S(1)}, f32[3,96,192]{2,1,0:T(8,128)}, u32[]{:S(2)}) copy-start(f32[3,96,192]{2,1,0:T(8,128)} %param.30) | copy-start | bytes 663556
  409.9 4.5 %copy-start.10 = (f32[3,96,192]{2,1,0:T(8,128)S(1)}, f32[3,96,192]{2,1,0:T(8,128)}, u32[]{:S(2)}) copy-start(f32[3,96,192]{2,1,0:T(8,128)} %param.39) | copy-start | bytes 663556
  409.9 4.5 %copy-start.11 = (f32[3,96,192]{2,1,0:T(8,128)S(1)}, f32[3,96,192]{2,1,0:T(8,128)}, u32[]{:S(2)}) copy-start(f32[3,96,192]{2,1,0:T(8,128)} %param.35) | copy-start | bytes 663556
Sparse Core Ops, SparseCore 0:
  11.4 103.8 all-gather.1
  222.9 76.7 reduce-scatter.2
  302.0 56.9 reduce-scatter.4

commit v2 on v1

--- a/solution.py
+++ b/solution.py
@@ -65,15 +65,13 @@
     return lax.broadcasted_iota(jnp.int32, (rows, 128), 1)
 
 
-def assemble(core, same_ref, other_ref, part, target, col):
-    width = same_ref.shape[-1]
-    for pos in range(RB // 2):
-        same = same_ref[pos, part]
-        other = other_ref[pos, part]
-        first = jnp.where(core == 0, same, other)
-        second = jnp.where(core == 0, other, same)
-        target[2 * pos * RP : (2 * pos + 1) * RP, col : col + width] = first
-        target[(2 * pos + 1) * RP : (2 * pos + 2) * RP, col : col + width] = second
+def assemble(tab, pieces, part, target, col):
+    width = pieces[0].shape[-1]
+    core, chip = tab[20], tab[21]
+    for n in range(4):
+        for half in range(2):
+            at = ((n ^ chip) * 2 + (core ^ half)) * RP
+            target[pl.ds(pl.multiple_of(at, RP), RP), col : col + width] = pieces[4 * half + n][part]
 
 
 def key_sides(k, count):
@@ -96,11 +94,13 @@
 
 
 def attend_kernel(
-    tab, own_ref, nb_ref, mid_ref, same_ref, other_ref, vec_ref, o_ref, qe_ref, qo_ref, k_ref, v_ref, w_s, ka_e, ka_o, va_e, va_o
+    tab, own_ref, nb_ref, mid_ref, *refs
 ):
-    core = tab[20]
+    pieces = refs[:8]
+    vec_ref, o_ref, qe_ref, qo_ref, k_ref, v_ref, xt_ref, w_s, ka_e, ka_o, va_e, va_o = refs[8:]
+    mine = pl.ds(pl.multiple_of(pl.program_id(0) * 128, 128), 128)
     for part in range(3):
-        assemble(core, same_ref, other_ref, part, w_s, 128 * part)
+        assemble(tab, pieces, part, w_s, 128 * part)
     bias_q = vec_ref[0:1, :]
     bias_v = vec_ref[1:2, :]
     low = lane_ids(BLK) < HDIM
@@ -108,6 +108,7 @@
     ones = jnp.ones((BLK, 128), BF)
     for b in range(8):
         src, at = (own_ref, b) if b < 3 else (nb_ref, b - 3) if b < 6 else (mid_ref, b - 6)
+        xt_ref[:, b * BLK : (b + 1) * BLK] = src[at * BLK : (at + 1) * BLK, mine].T
         kv = dot_nn(src[at * BLK : (at + 1) * BLK, :], w_s[:, 128:384])
         k = kv[:, :128].astype(BF)
         v = (kv[:, 128:] + bias_v).astype(BF)
@@ -161,7 +162,8 @@
     dq_ref,
     dk_ref,
     dv_ref,
-    dw_ref,
+    keep_ref,
+    give_ref,
     db_ref,
     ka_e,
     ka_o,
@@ -228,10 +230,13 @@
     dq_all = dq_ref[...]
     db_ref[0:1, :] = jnp.sum(dq_all.astype(F32), 0, keepdims=True)
     db_ref[1:2, :] = jnp.sum(dkv_s[:, 128:].astype(F32), 0, keepdims=True)
-    dw_ref[:, 0] = dot_nn(xt_ref[:, :ROWS], dq_all).astype(BF).reshape(RB, RP, 128)
+    dw_q = dot_nn(xt_ref[:, :ROWS], dq_all).astype(BF)
     dw_kv = dot_nn(xt_ref[...], dkv_s[...]).astype(BF)
-    dw_ref[:, 1] = dw_kv[:, :128].reshape(RB, RP, 128)
-    dw_ref[:, 2] = dw_kv[:, 128:].reshape(RB, RP, 128)
+    for n, grad in enumerate((dw_q, dw_kv[:, :128], dw_kv[:, 128:])):
+        grad = grad.reshape(RB // 2, 2, RP, 128)
+        for pos in range(RB // 2):
+            keep_ref[pos ^ tab[21], n] = jnp.where(tab[20] == 0, grad[pos, 0], grad[pos, 1])
+            give_ref[pos ^ tab[21], n] = jnp.where(tab[20] == 0, grad[pos, 1], grad[pos, 0])
 
 
 def gelu_both(pre):
@@ -264,32 +269,16 @@
     tab,
     o_ref,
     x_ref,
-    same_ref,
-    other_ref,
-    vec_ref,
-    w_ref,
-    cot_ref,
-    weight_ref,
-    u_ref,
-    gp_ref,
-    out_ref,
-    dz2_ref,
-    e2_ref,
-    e2t_ref,
-    h1t_ref,
-    hat1_ref,
-    root1_ref,
-    sums_ref,
-    wo_s,
-    h1_s,
-    h1b_s,
-    z2_s,
+    *refs,
 ):
+    pieces = refs[:8]
+    (vec_ref, w_ref, cot_ref, weight_ref, u_ref, gp_ref, out_ref, dz2_ref, e2_ref, e2t_ref) = refs[8:18]
+    (h1t_ref, hat1_ref, root1_ref, sums_ref, wo_s, h1_s, h1b_s, z2_s) = refs[18:]
     step = pl.program_id(0)
 
     @pl.when(step == 0)
     def _():
-        assemble(tab[20], same_ref, other_ref, 0, wo_s, 0)
+        assemble(tab, pieces, 0, wo_s, 0)
         for i in range(3):
             rows = slice(i * BLK, (i + 1) * BLK)
             z1 = x_ref[rows, :].astype(F32) + dot_nt(o_ref[rows, :], wo_s[...]) + vec_ref[2:3, :]
@@ -355,47 +344,39 @@
     hat1_ref,
     root1_ref,
     o_ref,
-    same_ref,
-    other_ref,
-    vec_ref,
-    dw_ref,
-    dz1_ref,
-    do_ref,
-    dwo_ref,
-    sums_ref,
-    db1_ref,
-    ep_s,
-    dh_s,
-    wo_s,
-    e1t_s,
+    *refs,
 ):
+    pieces = refs[:8]
+    vec_ref, dw_ref, dz1_ref, do_ref, sums_ref, db1_ref, ep_s, dh_s, wo_s, e1t_s = refs[8:]
     step = pl.program_id(0)
-    w1 = w_ref[:, 0, 0].reshape(D, D)
-    w2t = w_ref[:, 0, 1].reshape(D, D)
-    db1 = jnp.zeros((1, D), F32)
-    for i in range(3):
-        rows = slice(i * BLK, (i + 1) * BLK)
-        du = dot_nn(e2_ref[rows, :], w2t)
-        ep = (gp_ref[rows, :].astype(F32) * du).astype(BF)
-        ep_s[rows, :] = ep
-        db1 += jnp.sum(ep.astype(F32), 0, keepdims=True)
-        back = dot_nt(ep, w1)
-
-        @pl.when(step == 0)
-        def _():
-            dh_s[rows, :] = back + dz2_ref[rows, :]
-
-        @pl.when(step > 0)
-        def _():
-            dh_s[rows, :] += back
-
-    db1_ref[pl.ds(step, 1), :] = db1
-    dw_ref[:, 0, 0] = dot_nn(h1t_ref[...], ep_s[...]).astype(BF).reshape(RB, RP, D)
-    dw_ref[:, 0, 1] = dot_nn(e2t_ref[...], u_ref[...]).astype(BF).reshape(RB, RP, D)
-
-    @pl.when(step == 3)
+    @pl.when(step < 4)
     def _():
-        assemble(tab[20], same_ref, other_ref, 0, wo_s, 0)
+        w1 = w_ref[:, 0, 0].reshape(D, D)
+        w2t = w_ref[:, 0, 1].reshape(D, D)
+        db1 = jnp.zeros((1, D), F32)
+        for i in range(3):
+            rows = slice(i * BLK, (i + 1) * BLK)
+            du = dot_nn(e2_ref[rows, :], w2t)
+            ep = (gp_ref[rows, :].astype(F32) * du).astype(BF)
+            ep_s[rows, :] = ep
+            db1 += jnp.sum(ep.astype(F32), 0, keepdims=True)
+            back = dot_nt(ep, w1)
+
+            @pl.when(step == 0)
+            def _():
+                dh_s[rows, :] = back + dz2_ref[rows, :]
+
+            @pl.when(step > 0)
+            def _():
+                dh_s[rows, :] += back
+
+        db1_ref[pl.ds(step, 1), :] = db1
+        dw_ref[:, 0, 0] = dot_nn(h1t_ref[...], ep_s[...]).astype(BF).reshape(RB, RP, D)
+        dw_ref[:, 0, 1] = dot_nn(e2t_ref[...], u_ref[...]).astype(BF).reshape(RB, RP, D)
+
+    @pl.when(step == 4)
+    def _():
+        assemble(tab, pieces, 0, wo_s, 0)
         sums = [jnp.zeros((1, D), F32) for _ in range(3)]
         for i in range(3):
             rows = slice(i * BLK, (i + 1) * BLK)
@@ -411,26 +392,73 @@
             sums[2] += jnp.sum(dh, 0, keepdims=True)
         for n in range(3):
             sums_ref[n : n + 1, :] = sums[n]
-        dwo_ref[...] = dot_nn(e1t_s[...], o_ref[...]).astype(BF).reshape(RB, RP, D)
-
-
-def input_kernel(tab, dq_ref, dk_ref, dv_ref, same_ref, other_ref, dz1_ref, own_ref, rest_ref, w_s):
+        dw_ref[:, 0, 0] = dot_nn(e1t_s[...], o_ref[...]).astype(BF).reshape(RB, RP, D)
+        dw_ref[:, 0, 1] = jnp.zeros((RB, RP, D), BF)
+
+
+def pack_kernel(tab, own_ref, *rest):
+    others, out_ref, line_s = rest[:-2], rest[-2], rest[-1]
+    line_s[0] = own_ref[...]
+    for n, ref in enumerate(others):
+        line_s[n + 1] = ref[...]
+    width = own_ref.shape[-1] // 4
+    for m in range(4):
+        shard = line_s[m ^ tab[0]]
+        for n in range(4):
+            out_ref[n, :, m * width : (m + 1) * width] = shard[:, n * width : (n + 1) * width]
+
+
+def input_rest_kernel(tab, dk_ref, dv_ref, *refs):
+    pieces, (nb_ref, mid_ref, w_s) = refs[:8], refs[8:]
     step = pl.program_id(0)
 
     @pl.when(step == 0)
     def _():
-        for part in range(3):
-            assemble(tab[20], same_ref, other_ref, part, w_s, D * part)
-
-    back = dot_nt(dk_ref[...], w_s[:, D : 2 * D]) + dot_nt(dv_ref[...], w_s[:, 2 * D :])
+        for part in range(2):
+            assemble(tab, pieces, part + 1, w_s, D * part)
+
+    back = (dot_nt(dk_ref[...], w_s[:, :D]) + dot_nt(dv_ref[...], w_s[:, D:])).astype(BF)
 
     @pl.when(step < 3)
     def _():
-        own_ref[...] = back + dot_nt(dq_ref[...], w_s[:, :D]) + dz1_ref[...]
+        nb_ref[...] = back
 
     @pl.when(step >= 3)
     def _():
-        rest_ref[...] = back.astype(BF)
+        mid_ref[...] = back
+
+
+def input_own_kernel(tab, dq_ref, dk_ref, dv_ref, *refs):
+    pieces, (dz1_ref, own_ref, w_s) = refs[:8], refs[8:]
+
+    @pl.when(pl.program_id(0) == 0)
+    def _():
+        for part in range(3):
+            assemble(tab, pieces, part, w_s, D * part)
+
+    back = dot_nt(dk_ref[...], w_s[:, D : 2 * D]) + dot_nt(dv_ref[...], w_s[:, 2 * D :])
+    own_ref[...] = back + dot_nt(dq_ref[...], w_s[:, :D]) + dz1_ref[...]
+
+
+def line_kernel(tab, own_ref, *refs):
+    chips, (feed_ref, *outs) = refs[:-5], refs[-5:]
+    total = own_ref[...].astype(F32)
+    for ref in chips:
+        total = total + ref[...].astype(F32)
+    total = total.astype(BF)
+    width = total.shape[-1] // 4
+    for n in range(4):
+        m = n ^ tab[0]
+        outs[n][:, :D] = feed_ref[m, 0]
+        outs[n][:, D : 2 * D] = feed_ref[m, 1]
+        for other in range(4):
+
+            @pl.when(m == other)
+            def _():
+                at = slice(other * width, (other + 1) * width)
+                for kind in range(3):
+                    outs[n][:, 2 * D + kind * width : 2 * D + (kind + 1) * width] = total[kind, :, at]
+                outs[n][:, 2 * D + 3 * width :] = feed_ref[4, 0, :, at]
 
 
 def call(kernel, grid, in_specs, out_specs, out_shape, scratch, flops, bytes_accessed, name):
@@ -464,19 +492,20 @@
     return pltpu.VMEM(shape, dtype)
 
 
-def attend(tab, own, nb, mid, same, other, vectors):
-    w_spec = pl.BlockSpec((4, 3, RP, 128), lambda s, t: (0, 0, 0, s))
+def attend(tab, own, nb, mid, pieces, vectors):
+    w_spec = pl.BlockSpec((3, RP, 128), lambda s, t: (0, 0, s))
     return call(
         attend_kernel,
         PAIRS,
-        [whole(ROWS, D), whole(ROWS, D), whole(2 * BLK, D), w_spec, w_spec, columns(12)],
-        [columns(ROWS), columns(ROWS), columns(ROWS), columns(8 * BLK), columns(8 * BLK)],
-        [shape_of((ROWS, D), BF)] * 3 + [shape_of((8 * BLK, D), BF)] * 2,
+        [whole(ROWS, D), whole(ROWS, D), whole(2 * BLK, D)] + [w_spec] * 8 + [columns(12)],
+        [columns(ROWS), columns(ROWS), columns(ROWS), columns(8 * BLK), columns(8 * BLK)]
+        + [pl.BlockSpec((128, 8 * BLK), lambda s, t: (s, 0))],
+        [shape_of((ROWS, D), BF)] * 3 + [shape_of((8 * BLK, D), BF)] * 2 + [shape_of((D, 8 * BLK), BF)],
         [vm((D, 384), BF)] + [vm((8, BLK, 128), BF)] * 4,
-        28_000_000_000,
+        5_000_000_000,
         16_000_000,
         "attend",
-    )(tab, own, nb, mid, same, other, vectors)
+    )(tab, own, nb, mid, *pieces, vectors)
 
 
 def attend_back(tab, qe, qo, k, v, d_out, o, xt):
@@ -488,14 +517,16 @@
             columns(ROWS),
             columns(8 * BLK),
             columns(8 * BLK),
-            pl.BlockSpec((RB, 3, RP, 128), lambda s, t: (0, 0, 0, s)),
+            pl.BlockSpec((RB // 2, 3, RP, 128), lambda s, t: (0, 0, 0, s)),
+            pl.BlockSpec((RB // 2, 3, RP, 128), lambda s, t: (0, 0, 0, s)),
             columns(2),
         ],
         [
             shape_of((ROWS, D), BF),
             shape_of((8 * BLK, D), BF),
             shape_of((8 * BLK, D), BF),
-            shape_of((RB, 3, RP, D), BF),
+            shape_of((RB // 2, 3, RP, D), BF),
+            shape_of((RB // 2, 3, RP, D), BF),
             shape_of((2, D), F32),
         ],
         [vm((8, BLK, 128), BF)] * 4
@@ -508,16 +539,15 @@
     )(tab, qe, qo, k, v, d_out, o, xt)
 
 
-def feed(tab, o, x, same, other, vectors, w, cot, weight):
-    wo_spec = pl.BlockSpec((4, 1, RP, D), lambda s, t: (0, 3, 0, 0))
+def feed(tab, o, x, pieces, vectors, w, cot, weight):
+    wo_spec = pl.BlockSpec((1, RP, D), lambda s, t: (3, 0, 0))
     return call(
         feed_kernel,
         4,
         [
             whole(ROWS, D),
             whole(ROWS, D),
-            wo_spec,
-            wo_spec,
+            *[wo_spec] * 8,
             whole(12, D),
             pl.BlockSpec((RB, 1, 2, RP, D), lambda s, t: (0, s, 0, 0, 0)),
             whole(ROWS, D),
@@ -551,36 +581,43 @@
         18_000_000_000,
         40_000_000,
         "feed",
-    )(tab, o, x, same, other, vectors, w, cot, weight)
-
-
-def feed_back(tab, e2, e2t, h1t, u, gp, w, dz2, hat1, root1, o, same, other, vectors):
-    wo_spec = pl.BlockSpec((4, 1, RP, D), lambda s, t: (0, 3, 0, 0))
-    w_spec = pl.BlockSpec((RB, 1, 2, RP, D), lambda s, t: (0, s, 0, 0, 0))
+    )(tab, o, x, *pieces, vectors, w, cot, weight)
+
+
+def feed_back(tab, e2, e2t, h1t, u, gp, w, dz2, hat1, root1, o, pieces, vectors):
+    wo_spec = pl.BlockSpec((1, RP, D), lambda s, t: (3, 0, 0))
+
+    def late(s):
+        return jnp.minimum(s, 3)
+
     return call(
         feed_back_kernel,
-        4,
+        5,
         [
             whole(ROWS, D),
             whole(D, ROWS),
             whole(D, ROWS),
-            columns(ROWS, D),
-            columns(ROWS, D),
-            w_spec,
+            pl.BlockSpec((ROWS, D), lambda s, t: (0, late(s))),
+            pl.BlockSpec((ROWS, D), lambda s, t: (0, late(s))),
+            pl.BlockSpec((RB, 1, 2, RP, D), lambda s, t: (0, late(s), 0, 0, 0)),
             whole(ROWS, D),
             whole(ROWS, D),
             whole(ROWS, 1),
             whole(ROWS, D),
-            wo_spec,
-            wo_spec,
+            *[wo_spec] * 8,
             whole(12, D),
         ],
-        [w_spec, whole(ROWS, D), whole(ROWS, D), whole(RB, RP, D), whole(3, D), whole(4, D)],
         [
-            shape_of((RB, 4, 2, RP, D), BF),
+            pl.BlockSpec((RB, 1, 2, RP, D), lambda s, t: (0, s, 0, 0, 0)),
+            whole(ROWS, D),
+            whole(ROWS, D),
+            whole(3, D),
+            whole(4, D),
+        ],
+        [
+            shape_of((RB, 5, 2, RP, D), BF),
             shape_of((ROWS, D), F32),
             shape_of((ROWS, D), BF),
-            shape_of((RB, RP, D), BF),
             shape_of((3, D), F32),
             shape_of((4, D), F32),
         ],
@@ -588,34 +625,159 @@
         24_000_000_000,
         48_000_000,
         "feed_back",
-    )(tab, e2, e2t, h1t, u, gp, w, dz2, hat1, root1, o, same, other, vectors)
-
-
-def input_back(tab, dq, dk, dv, same, other, dz1):
-    w_spec = pl.BlockSpec((4, 3, RP, D), lambda s, t: (0, 0, 0, 0))
-    first = pl.BlockSpec((BLK, D), lambda s, t: (jnp.minimum(s, 2), 0))
+    )(tab, e2, e2t, h1t, u, gp, w, dz2, hat1, root1, o, *pieces, vectors)
+
+
+def round_kernel(qkv_ref, proj_ref, up_ref, down_ref, mine_ref, feed_ref):
+    width = qkv_ref.shape[-1]
+    for n in range(3):
+        mine_ref[:, n * width : (n + 1) * width] = qkv_ref[n].astype(BF)
+    mine_ref[:, 3 * width :] = proj_ref[...].T.astype(BF)
+    feed_ref[0] = up_ref[...].astype(BF)
+    feed_ref[1] = down_ref[...].astype(BF)
+
+
+def round_shards(qkv, proj, up, down):
+    rows = up.shape[0]
+    return pl.pallas_call(
+        round_kernel,
+        in_specs=[pl.BlockSpec(memory_space=pltpu.VMEM)] * 4,
+        out_specs=[pl.BlockSpec(memory_space=pltpu.VMEM)] * 2,
+        out_shape=[shape_of((rows, D), BF), shape_of((2, rows, D), BF)],
+        cost_estimate=pl.CostEstimate(flops=1_000_000, bytes_accessed=1_500_000, transcendentals=0),
+        name="round_shards",
+    )(qkv, proj, up, down)
+
+
+def pack_line(z, own, others):
+    rows, width = own.shape
+    return call(
+        pack_kernel,
+        1,
+        [whole(rows, width)] * 4,
+        whole(4, rows, D),
+        shape_of((4, rows, D), BF),
+        [vm((4, rows, width), BF)],
+        60_000_000_000,
+        1_000_000,
+        "pack_line",
+    )(z.reshape(1).astype(jnp.int32), own, *others)
+
+
+def input_rest(tab, dk, dv, pieces):
+    w_spec = whole(3, RP, D)
+    each = pl.BlockSpec((BLK, D), lambda s, t: (s + 3, 0))
+    return call(
+        input_rest_kernel,
+        5,
+        [each, each] + [w_spec] * 8,
+        [
+            pl.BlockSpec((BLK, D), lambda s, t: (jnp.minimum(s, 2), 0)),
+            pl.BlockSpec((BLK, D), lambda s, t: (jnp.maximum(s - 3, 0), 0)),
+        ],
+        [shape_of((3 * BLK, D), BF), shape_of((2 * BLK, D), BF)],
+        [vm((D, 2 * D), BF)],
+        8_000_000_000,
+        12_000_000,
+        "input_rest",
+    )(tab, dk, dv, *pieces)
+
+
+def input_own(tab, dq, dk, dv, pieces, dz1):
+    w_spec = whole(3, RP, D)
     each = pl.BlockSpec((BLK, D), lambda s, t: (s, 0))
     return call(
-        input_kernel,
-        8,
-        [first, each, each, w_spec, w_spec, first],
-        [first, pl.BlockSpec((BLK, D), lambda s, t: (jnp.maximum(s - 3, 0), 0))],
-        [shape_of((ROWS, D), F32), shape_of((5 * BLK, D), BF)],
+        input_own_kernel,
+        3,
+        [each, each, each] + [w_spec] * 8 + [each],
+        each,
+        shape_of((ROWS, D), F32),
         [vm((D, 3 * D), BF)],
-        6_000_000_000,
-        16_000_000,
-        "input_back",
-    )(tab, dq, dk, dv, same, other, dz1)
-
-
-def adamw(weight, grad, first, second, rate, decay, clip_factor):
-    clipped = grad * clip_factor
+        5_000_000_000,
+        12_000_000,
+        "input_own",
+    )(tab, dq, dk, dv, *pieces, dz1)
+
+
+def line_parts(z, own, others, fed):
+    rows = own.shape[1]
+    return call(
+        line_kernel,
+        1,
+        [whole(3, rows, D)] * (1 + len(others)) + [whole(5, 2, rows, D)],
+        [whole(rows, 3 * D)] * 4,
+        [shape_of((rows, 3 * D), BF)] * 4,
+        [],
+        2_000_000,
+        4_000_000,
+        "line_parts",
+    )(z.reshape(1).astype(jnp.int32), own, *others, fed)
+
+
+def adamw(weight, clipped, first, second, rate, decay):
     first_new = BETA_ONE * first + (1.0 - BETA_ONE) * clipped
     second_new = BETA_TWO * second + (1.0 - BETA_TWO) * clipped * clipped
     first_hat = first_new / (1.0 - BETA_ONE**STEP)
     second_hat = second_new / (1.0 - BETA_TWO**STEP)
     updated = weight * (1.0 - rate * decay) - rate * first_hat / (jnp.sqrt(second_hat) + ADAM_EPS)
     return (clipped, first_new, second_new, updated)
+
+
+def update_kernel(clip_ref, sum_ref, vec_ref, *refs):
+    ins, outs = refs[:15], refs[15:]
+    clip = clip_ref[0, 0]
+    sums = sum_ref[...]
+    width = D // 4
+    grads = (
+        [sums[:, 2 * D + n * width : 2 * D + (n + 1) * width] for n in range(3)],
+        [sums[:, 2 * D + 3 * width :].T],
+        [sums[:, :D]],
+        [sums[:, D : 2 * D]],
+        [vec_ref[...]],
+    )
+    for kind, parts in enumerate(grads):
+        rate, decay = (VECTOR_RATE, 0.0) if kind == 4 else (MATRIX_RATE / math.sqrt(D), WEIGHT_DECAY)
+        for n, grad in enumerate(parts):
+            at = n if kind == 0 else Ellipsis
+            results = adamw(ins[kind][at], grad * clip, ins[5 + kind][at], ins[10 + kind][at], rate, decay)
+            for m, result in enumerate(results):
+                outs[4 * kind + m][at] = result
+
+
+def update(clip, sums, vec, weights, firsts, seconds):
+    shapes = [shape_of(one.shape, F32) for one in weights for _ in range(4)]
+    return pl.pallas_call(
+        update_kernel,
+        in_specs=[pl.BlockSpec(memory_space=pltpu.SMEM)] + [pl.BlockSpec(memory_space=pltpu.VMEM)] * 17,
+        out_specs=[pl.BlockSpec(memory_space=pltpu.VMEM)] * 20,
+        out_shape=shapes,
+        compiler_params=pltpu.CompilerParams(vmem_limit_bytes=VMEM_LIMIT),
+        cost_estimate=pl.CostEstimate(flops=10_000_000, bytes_accessed=8_000_000, transcendentals=0),
+        name="update",
+    )(clip, sums, vec, *weights, *firsts, *seconds)
+
+
+def total_kernel(vec_ref, *refs):
+    parts, (sum_out, square_out) = refs[:4], refs[4:]
+    sums = parts[0][...].astype(F32)
+    for ref in parts[1:]:
+        sums = sums + ref[...].astype(F32)
+    sum_out[...] = sums
+    vec = vec_ref[...]
+    square_out[0, 0] = jnp.sum(sums * sums) + jnp.sum(vec * vec)
+
+
+def total(vec, parts):
+    vmem = pl.BlockSpec(memory_space=pltpu.VMEM)
+    return pl.pallas_call(
+        total_kernel,
+        in_specs=[vmem] * 5,
+        out_specs=[vmem, pl.BlockSpec(memory_space=pltpu.SMEM)],
+        out_shape=[shape_of(parts[0].shape, F32), shape_of((1, 1), F32)],
+        compiler_params=pltpu.CompilerParams(vmem_limit_bytes=VMEM_LIMIT),
+        cost_estimate=pl.CostEstimate(flops=2_000_000, bytes_accessed=4_000_000, transcendentals=0),
+        name="total",
+    )(vec, *parts)
 
 
 def shards(
@@ -654,17 +816,21 @@
     def linear(chip, core_of, z_of):
         return (chip * 2 + core_of) * mp_count + z_of
 
+    def permutation(move):
+        return [
+            (linear(chip, c, k), linear(*move(chip, c, k)))
+            for chip in range(chips)
+            for c in range(2)
+            for k in range(mp_count)
+        ]
+
     planes = [[linear(chip, c, k) for chip in range(chips)] for c in range(2) for k in range(mp_count)]
-    swap_core = [
-        (linear(chip, c, k), linear(chip, 1 - c, k)) for chip in range(chips) for c in range(2) for k in range(mp_count)
-    ]
-    swap_z = [
-        (linear(chip, c, k), linear(chip, c, k ^ 1)) for chip in range(chips) for c in range(2) for k in range(mp_count)
-    ]
+    swap_core = permutation(lambda chip, c, k: (chip, 1 - c, k))
+    swap_z = [permutation(lambda chip, c, k, n=n: (chip, c, k ^ n)) for n in range(mp_count)]
+    swap_chip = [permutation(lambda chip, c, k, n=n: (chip ^ n, c, k)) for n in range(chips)]
     middle = (0, 2, 1, 3)
-    swap_mid = [
-        (linear(chip, c, k), linear(chip, c, middle[k])) for chip in range(chips) for c in range(2) for k in range(mp_count)
-    ]
+    swap_mid = permutation(lambda chip, c, k: (chip, c, middle[k]))
+    chip_index = dp_index // 2
 
     def over_plane(value):
         return lax.all_to_all(value, AXES, 0, 0, tiled=True, axis_index_groups=planes)
@@ -672,33 +838,36 @@
     def over_z(value):
         return lax.all_to_all(value, "mp", 0, 0, tiled=True)
 
-    mine = jnp.concatenate(
-        [qkv_master[0], qkv_master[1], qkv_master[2], proj_master.T], 1
-    ).astype(BF)
-    along_z = over_z(jnp.broadcast_to(mine[None], (mp_count, part, D)))
-    along_z = along_z.reshape(mp_count, part, 4, head_cols).transpose(2, 1, 0, 3).reshape(4, part, D)
-    same = over_plane(jnp.broadcast_to(along_z[None], (chips, 4, part, D)))
-    other = lax.ppermute(same, AXES, swap_core)
-    kernel_core = core
+    def absolute(same, other):
+        order = jnp.arange(chips, dtype=jnp.int32) ^ chip_index
+        same, other = jnp.stack(same)[order], jnp.stack(other)[order]
+        both = jnp.where(core == 0, jnp.stack([same, other], 1), jnp.stack([other, same], 1))
+        kinds = both.shape[2]
+        both = both.transpose(2, 0, 1, 3, 4).reshape(kinds, RB // 2, 2, RP, D).transpose(1, 2, 0, 3, 4)
+        return [both[n, half] for half in range(2) for n in range(RB // 2)]
+
+    mine, feed_mine = round_shards(qkv_master, proj_master, up_master, down_master.T)
+    feed_w = lax.all_gather(feed_mine, AXES, axis=0, tiled=False).reshape(dp_count, mp_count, 2, part, D)
+    line = [lax.ppermute(mine, AXES, swap_z[n]) for n in range(1, mp_count)]
+    tokens_late, mine, *line = lax.optimization_barrier((tokens, mine, *line))
+    along_z = pack_line(z, mine, line)
+    mid_at = jnp.where(z == 1, BLK, 0)
+    nb = lax.ppermute(tokens_late, AXES, swap_z[1])
+    mid = lax.ppermute(lax.dynamic_slice_in_dim(tokens_late, mid_at, 2 * BLK, 0), AXES, swap_mid)
+    same = [along_z] + [lax.ppermute(along_z, AXES, swap_chip[n]) for n in range(1, chips)]
+    first, same[1] = lax.optimization_barrier((along_z, same[1]))
+    other = [lax.ppermute(one, AXES, swap_core) for one in [first] + same[1:]]
+    pieces = same + other
+    kernel_core, kernel_chip = core, chip_index
     if part != RP:
-        both = jnp.where(core == 0, jnp.stack([same, other], 1), jnp.stack([other, same], 1))
-        both = both.transpose(2, 0, 1, 3, 4).reshape(4, RB // 2, 2, RP, D).transpose(1, 2, 0, 3, 4)
-        same, other = both[:, 0], both[:, 1]
-        kernel_core = jnp.zeros((), jnp.int32)
-    feed_mine = jnp.stack([up_master, down_master.T]).astype(BF)
-    feed_w = lax.all_gather(feed_mine, AXES, axis=0, tiled=False).reshape(dp_count, mp_count, 2, part, D)
-    if part != RP:
+        pieces = absolute(same, other)
         feed_w = feed_w.transpose(1, 2, 0, 3, 4).reshape(mp_count, 2, RB, RP, D).transpose(2, 0, 1, 3, 4)
-
-    mid_at = jnp.where(z == 1, BLK, 0)
-    nb = lax.ppermute(tokens, AXES, swap_z)
-    mid = lax.ppermute(lax.dynamic_slice_in_dim(tokens, mid_at, 2 * BLK, 0), AXES, swap_mid)
-    xt = jnp.concatenate([tokens, nb, mid], 0).T
+        kernel_core = kernel_chip = jnp.zeros((), jnp.int32)
 
     place = jnp.asarray(BLOCK_PLACE)[z]
     counts = jnp.clip(lengths[jnp.asarray(BLOCK_SEQ)[z]] - BLK * place, 0, BLK)
     tab = jnp.concatenate(
-        [jnp.asarray(KEY_BLOCKS)[z].reshape(12), counts, kernel_core.reshape(1)]
+        [jnp.asarray(KEY_BLOCKS)[z].reshape(12), counts, kernel_core.reshape(1), kernel_chip.reshape(1)]
     ).astype(jnp.int32)
 
     positions = z * ROWS + jnp.arange(ROWS, dtype=jnp.int32)
@@ -714,12 +883,9 @@
     opening = (within == 0).astype(F32)
     row_weight = valid_row * (1.0 + 2.0 * (1.0 - flag_row) * answer + 4.0 * flag_row * opening)
 
-    o, qe, qo, k, v = attend(tab, tokens, nb, mid, same, other, vectors)
+    o, qe, qo, k, v, xt = attend(tab, tokens, nb, mid, pieces, vectors)
     u, gp, block_out, dz2, e2, e2t, h1t, hat1, root1, sums_two = feed(
-        tab, o, tokens, same, other, vectors, feed_w, out_cotangent, row_weight[:, None]
-    )
-    feed_dw, dz1, d_o, wo_dw, sums_one, bias_up_grad = feed_back(
-        tab, e2, e2t, h1t, u, gp, feed_w, dz2, hat1, root1, o, same, other, vectors
+        tab, o, tokens, pieces, vectors, feed_w, out_cotangent, row_weight[:, None]
     )
 
     def to_parts(grad):
@@ -729,52 +895,59 @@
         moved = jnp.moveaxis(grad, 0, -3).reshape(*lead, dp_count, part, D)
         return jnp.moveaxis(moved, -3, 0)
 
-    feed_dw = to_parts(feed_dw)
-    feed_sum = lax.psum_scatter(feed_dw, "dp", scatter_dimension=0, tiled=False)
-    feed_sum = lax.psum_scatter(feed_sum, "mp", scatter_dimension=0, tiled=False).astype(F32)
-
-    dq, dk, dv, qkv_dw, sums_head = attend_back(tab, qe, qo, k, v, d_o, o, xt)
-    head_dw = to_parts(jnp.concatenate([qkv_dw, wo_dw[:, None]], 1))
-    head_dw = head_dw.reshape(chips, 2, 4, part, D)
-    keep = lax.dynamic_index_in_dim(head_dw, core, 1, keepdims=False)
-    give = lax.dynamic_index_in_dim(head_dw, 1 - core, 1, keepdims=False)
+    feed_dw, dz1, d_o, sums_one, bias_up_grad = feed_back(
+        tab, e2, e2t, h1t, u, gp, feed_w, dz2, hat1, root1, o, pieces, vectors
+    )
+    feed_part = lax.psum_scatter(to_parts(feed_dw), "dp", scatter_dimension=0, tiled=False)
+
+    dq, dk, dv, keep, give, sums_head = attend_back(tab, qe, qo, k, v, d_o, o, xt)
+    if part != RP:
+        both = jnp.stack([keep, give], 1).reshape(RB, 3, RP, D)
+        both = to_parts(both).reshape(chips, 2, 3, part, D)
+        order = jnp.arange(chips, dtype=jnp.int32) ^ chip_index
+        keep = lax.dynamic_index_in_dim(both, core, 1, keepdims=False)[order]
+        give = lax.dynamic_index_in_dim(both, 1 - core, 1, keepdims=False)[order]
     got = lax.ppermute(give, AXES, swap_core)
     chip_sum = (keep.astype(F32) + got.astype(F32)).astype(BF)
-    plane_sum = jnp.sum(over_plane(chip_sum).astype(F32), 0)
-    plane_sum = plane_sum.astype(BF).reshape(4, part, mp_count, head_cols).transpose(2, 1, 0, 3)
-    head_sum = jnp.sum(over_z(plane_sum.reshape(mp_count, part, D)).astype(F32), 0)
-
-    dx_own, dx_rest = input_back(tab, dq, dk, dv, same, other, dz1)
-    from_nb = lax.ppermute(dx_rest[: 3 * BLK], AXES, swap_z)
-    from_mid = lax.ppermute(dx_rest[3 * BLK :], AXES, swap_mid)
+    to_nb, to_mid = input_rest(tab, dk, dv, pieces)
+    chip_sum, dq, dk, dv, sums_head, to_nb, to_mid = lax.optimization_barrier(
+        (chip_sum, dq, dk, dv, sums_head, to_nb, to_mid)
+    )
+    from_chips = [lax.ppermute(chip_sum[n], AXES, swap_chip[n]) for n in range(1, chips)]
+    from_nb = lax.ppermute(to_nb, AXES, swap_z[1])
+    from_mid = lax.ppermute(to_mid, AXES, swap_mid)
+    dx_own = input_own(tab, dq, dk, dv, pieces, dz1)
+    vector_part = jnp.concatenate([sums_head, sums_one, sums_two, bias_up_grad], 0)
+    vec_columns = D // devices
+    vector_part = vector_part.reshape(12, devices, vec_columns).transpose(1, 0, 2)
+    vector_grad = jnp.sum(lax.all_to_all(vector_part, AXES, 0, 0, tiled=True), 0)
+    vector_grad, feed_part, dx_own, from_nb, from_mid, *from_chips = lax.optimization_barrier(
+        (vector_grad, feed_part, dx_own, from_nb, from_mid, *from_chips)
+    )
+    line_own, *line_rest = line_parts(z, chip_sum[0], from_chips, feed_part)
+    line_rest = [lax.ppermute(one, AXES, swap_z[n + 1]) for n, one in enumerate(line_rest)]
     zero_block = jnp.zeros((BLK, D), BF)
     from_mid = jnp.where(
         z == 1, jnp.concatenate([zero_block, from_mid], 0), jnp.concatenate([from_mid, zero_block], 0)
     )
     input_grad = dx_own + from_nb.astype(F32) + from_mid.astype(F32)
 
-    vector_part = jnp.concatenate([sums_head, sums_one, sums_two, bias_up_grad], 0)
-    vec_columns = D // devices
-    vector_part = vector_part.reshape(12, devices, vec_columns).transpose(1, 0, 2)
-    vector_grad = jnp.sum(lax.all_to_all(vector_part, AXES, 0, 0, tiled=True), 0)
-
-    qkv_sum = jnp.stack([head_sum[:, n * head_cols : (n + 1) * head_cols] for n in range(3)])
-    proj_sum = head_sum[:, 3 * head_cols :].T
-    up_sum = feed_sum[0]
-    down_sum = feed_sum[1].T
-    local_squares = jnp.sum(head_sum * head_sum) + jnp.sum(feed_sum * feed_sum) + jnp.sum(vector_grad * vector_grad)
-    squares = lax.all_to_all(jnp.broadcast_to(local_squares, (devices,)), AXES, 0, 0, tiled=True)
+    sums, local_squares = total(vector_grad, [line_own] + line_rest)
+    squares = lax.all_to_all(jnp.broadcast_to(local_squares.reshape(1), (devices,)), AXES, 0, 0, tiled=True)
     grad_norm = jnp.sqrt(jnp.sum(squares))
     clip_factor = jnp.minimum(1.0, CLIP_NORM / (grad_norm + 1e-06))
-    matrix_rate = MATRIX_RATE / math.sqrt(D)
     vec_index = dp_index * mp_count + z
     vector_shard = lax.dynamic_slice_in_dim(vectors, vec_index * vec_columns, vec_columns, 1)
-    qkv_set = adamw(qkv_master, qkv_sum, qkv_first, qkv_second, matrix_rate, WEIGHT_DECAY, clip_factor)
-    proj_set = adamw(proj_master, proj_sum, proj_first, proj_second, matrix_rate, WEIGHT_DECAY, clip_factor)
-    up_set = adamw(up_master, up_sum, up_first, up_second, matrix_rate, WEIGHT_DECAY, clip_factor)
-    down_set = adamw(down_master, down_sum, down_first, down_second, matrix_rate, WEIGHT_DECAY, clip_factor)
-    vector_set = adamw(vector_shard, vector_grad, vector_first, vector_second, VECTOR_RATE, 0.0, clip_factor)
-    return (block_out, input_grad, grad_norm, *qkv_set, *proj_set, *up_set, *down_set, *vector_set)
+    results = update(
+        clip_factor.reshape(1, 1),
+        sums,
+        vector_grad,
+        (qkv_master, proj_master, up_master, down_master.T, vector_shard),
+        (qkv_first, proj_first, up_first, down_first.T, vector_first),
+        (qkv_second, proj_second, up_second, down_second.T, vector_second),
+    )
+    down_set = [one.T for one in results[12:16]]
+    return (block_out, input_grad, grad_norm, *results[:12], *down_set, *results[16:])
 
 
 def solution(mesh):

time: 432 us -> 363 us (0.84)
  blocking collectives: 70.1 us -> 0 us
  other arithmetic: 32.5 us -> 9.26 us
  Pallas kernels: 162 us -> 183 us
  waiting for transfers between devices: 80 us -> 94.1 us
  local copies, waits for them, and re-layouts: 22.1 us -> 8.8 us
  starting transfers between devices: 38.2 us -> 46.1 us
    all_to_all x2 -> x0, blocking collectives: 70.1 us -> none  [the longest x1 41.7 us: over_plane(): lax.all_to_all(value, AXES, 0, 0, tiled=True, axis_index_groups=planes)]
    ppermute x5 -> x20, waiting for transfers between devices: 32.5 us -> 69.4 us  [the longest x3 28.9 us: shards(): lax.ppermute(one, AXES, swap_z[n + 1])]
    pallas_call x3 -> x9, Pallas kernels: 76.8 us -> 96 us  [the longest x1 32.2 us: feed_back(): call(feed_back_kernel, 5, [whole(ROWS, D), whole(D, ROWS), whole(D, ROWS)...]
    all_to_all x3 -> x1, waiting for transfers between devices: 15.2 us -> 3.87 us  [shards(): lax.all_to_all(jnp.broadcast_to(local_squares.reshape(1), (devices,)), AX...]
    ppermute x5 -> x20, starting transfers between devices: 25.3 us -> 32.1 us  [the longest x1 8.88 us: shards(): nb = lax.ppermute(tokens_late, AXES, swap_z[1])]
    sub x5 -> x0, other arithmetic: 5.72 us -> none  [adamw(): weight * (1.0 - rate * decay)]
    reduce_scatter x2 -> x1, waiting for transfers between devices: 5.13 us -> 0.02 us  [shards(): lax.psum_scatter(to_parts(feed_dw), 'dp', scatter_dimension=0, tiled=False)]
    ppermute x1, waiting for transfers between devices: 4.87 us -> 0.01 us  [shards(): got = lax.ppermute(give, AXES, swap_core)]
  transfers between devices with their start and end apart: 13 -> 25, of which waited for: 6 -> 11; matrix products, arithmetic and copies ran while one was open for 9% -> 4% of each run, Pallas kernels for 24% -> 30%
where the time goes in v2:
time: 363 us; the launch traced here: 357 us
  Pallas kernels  183 us (50%)
  waiting for transfers between devices  94.1 us (26%)
  starting transfers between devices  46.1 us (13%)
  between operations  16.5 us (5%)
  other arithmetic  9.26 us (3%)
  local copies, waits for them, and re-layouts  8.8 us (2%)
    pallas_call x1, Pallas kernels, attend_back(): call(attend_back_kernel, PAIRS, [columns(ROWS), columns(ROWS), columns(8...  54.1 us
    pallas_call x1, Pallas kernels, attend(): call(attend_kernel, PAIRS, [whole(ROWS, D), whole(ROWS, D), whole(2 * BLK...  32.5 us
    pallas_call x1, Pallas kernels, feed_back(): call(feed_back_kernel, 5, [whole(ROWS, D), whole(D, ROWS), whole(D, ROWS)...  32.2 us
    pallas_call x1, Pallas kernels, feed(): call(feed_kernel, 4, [whole(ROWS, D), whole(ROWS, D), *[wo_spec] * 8, who...  30.2 us
    ppermute x3, waiting for transfers between devices, shards(): lax.ppermute(one, AXES, swap_z[n + 1])  28.9 us
    all_to_all x1, waiting for transfers between devices, shards(): lax.all_to_all(vector_part, AXES, 0, 0, tiled=True)  20.8 us
    ppermute x3, waiting for transfers between devices, shards(): lax.ppermute(along_z, AXES, swap_chip[n])  19.6 us
    ppermute x3, waiting for transfers between devices, shards(): line = [lax.ppermute(mine, AXES, swap_z[n]) for n in range(1, mp_count)]  11.7 us
  transfers between devices with their start and end apart: 25, of which 11 were waited for; matrix products, arithmetic and copies ran while one was open for 4% of the time, Pallas kernels for 30%

profile of v2, /device:TPU:0, one launch (start us, length us, event | category | flops | bytes accessed | tf_op | source)
XLA Modules:
  0.0 357.4 jit_solution(9061345285965141550)
XLA Ops:
  7.2 2.1 round_shards.1
  9.5 3.1 collective-permute-start
  12.5 2.6 collective-permute-start.1
  15.1 3.5 collective-permute-done.rest_0_
  18.6 8.2 %collective-permute-done.1.rest_1_ = bf16[96,768]{1,0:T(8,128)(2,1)S(1)} collective-permute-done((bf16[96,768]{1,0:T(8,128)(2,1)}, bf16[96,768]{1,0:T(8,128)(2,1)S(1)}, u32[]{:S(2)}, u32[]{:S(2)}) %collective-permute-start.1) | collective-permute-done | bytes 147488 | tf_op jit(solution)/shard_map/ppermute | solution.py:851
  26.9 1.5 collective-permute-start.4
  28.5 2.4 pack_line.1.refs_0_
  30.9 1.5 collective-permute-start.5
  32.4 1.5 collective-permute-start.6
  34.4 8.9 %collective-permute-start.3 = (bf16[768,768]{1,0:T(8,128)(2,1)S(1)}, bf16[768,768]{1,0:T(8,128)(2,1)S(1)}, u32[]{:S(2)}, u32[]{:S(2)}) collective-permute-start(bf16[768,768]{1,0:T(8,128)(2,1)S(1)} %copy-done.4), channel_id=1, source_target_pairs={{0,1},{1,0},{2,3},{3,2},{4,5},{5,4},{6,7},{7,6},{8,9},{9,8},{10,11... | collective-permute-start | bytes 3538952 | tf_op jit(solution)/shard_map/ppermute | solution.py:855
  44.0 0.7 fusion.14
  45.4 0.7 fusion.15
  46.1 5.0 %collective-permute-done.5.refs_1_ = bf16[4,96,768]{2,1,0:T(8,128)(2,1)} collective-permute-done((bf16[4,96,768]{2,1,0:T(8,128)(2,1)}, bf16[4,96,768]{2,1,0:T(8,128)(2,1)}, u32[]{:S(2)}, u32[]{:S(2)}) %collective-permute-start.5) | collective-permute-done | bytes 589856 | tf_op jit(solution)/shard_map/ppermute | solution.py:857
  51.1 2.9 collective-permute-done.6.refs_2_
  53.9 11.8 %collective-permute-done.7.refs_3_ = bf16[4,96,768]{2,1,0:T(8,128)(2,1)} collective-permute-done((bf16[4,96,768]{2,1,0:T(8,128)(2,1)}, bf16[4,96,768]{2,1,0:T(8,128)(2,1)}, u32[]{:S(2)}, u32[]{:S(2)}) %collective-permute-start.7) | collective-permute-done | bytes 589856 | tf_op jit(solution)/shard_map/ppermute | solution.py:857
  67.0 1.4 fusion.2.refs_11_
  68.8 8.7 %collective-permute-done.3.nb_ref = bf16[768,768]{1,0:T(8,128)(2,1)S(1)} collective-permute-done((bf16[768,768]{1,0:T(8,128)(2,1)S(1)}, bf16[768,768]{1,0:T(8,128)(2,1)S(1)}, u32[]{:S(2)}, u32[]{:S(2)}) %collective-permute-start.3) | collective-permute-done | bytes 1179680 | tf_op jit(solution)/shard_map/ppermute | solution.py:855
  77.5 1.0 copy-done.12
  78.5 32.5 %attend.1 = (bf16[768,768]{1,0:T(8,128)(2,1)}, bf16[768,768]{1,0:T(8,128)(2,1)}, bf16[768,768]{1,0:T(8,128)(2,1)}, bf16[2048,768]{1,0:T(8,128)(2,1)}, bf16[2048,...) custom-call(s32[22]{0:T(128)} %pad_add_fusion.tab, bf16[768,768]{1,0:T(8,128)(2,1)} %x_ref.1, bf16[768,768]{1,0:T(8,128)(2,1)} %copy-done.12, ...), custom_call_target="tpu_custom_call" | custom-call | flops 5000000000 | bytes 16000000 | tf_op jit(solution)/shard_map/attend/pallas_call | solution.py:497
  111.1 30.2 %feed.1 = (bf16[768,3072]{1,0:T(8,128)(2,1)}, bf16[768,3072]{1,0:T(8,128)(2,1)}, bf16[768,768]{1,0:T(8,128)(2,1)}, f32[768,768]{1,0:T(8,128)}, bf16[768,768]{1,0...) custom-call(s32[22]{0:T(128)} %pad_add_fusion.tab, ...), custom_call_target="tpu_custom_call" | custom-call | flops 17999998976 | bytes 40000000 | tf_op jit(solution)/shard_map/feed/pallas_call | solution.py:544
  141.2 32.2 %feed_back.1 = (bf16[8,5,2,96,768]{4,3,2,1,0:T(8,128)(2,1)}, f32[768,768]{1,0:T(8,128)}, bf16[768,768]{1,0:T(8,128)(2,1)}, f32[3,768]{1,0:T(4,128)}, f32[4,768]{1,0:T(4,128)}) custom-call(s32[22]{0:T(128)} %pad_add_fusion.tab, bf16[768,768]{1,0:T(8,128)(2,1)} %get-tuple-element.117.e2_ref, bf16[768,768]{1,0:T(8,128)(2,1)} %get-tuple-element.118.e2t_ref, ...), custom_call_target="tpu_custom_call" | custom-call | flops 24000000000 | bytes 48000000 | tf_op jit(solution)/shard_map/feed_back/pallas_call | solution.py:593
  173.5 54.1 %attend_back.1 = (bf16[768,768]{1,0:T(8,128)(2,1)}, bf16[2048,768]{1,0:T(8,128)(2,1)}, bf16[2048,768]{1,0:T(8,128)(2,1)}, bf16[4,3,96,768]{3,2,1,0:T(8,128)(2,1)...) custom-call(s32[22]{0:T(128)} %pad_add_fusion.tab, bf16[768,768]{1,0:T(8,128)(2,1)} %get-tuple-element.113.qe_ref, ...), custom_call_target="tpu_custom_call" | custom-call | flops 49999998976 | bytes 24000000 | tf_op jit(solution)/shard_map/attend_back/pallas_call | solution.py:512
  227.7 9.1 %input_rest.1 = (bf16[768,768]{1,0:T(8,128)(2,1)}, bf16[512,768]{1,0:T(8,128)(2,1)}) custom-call(s32[22]{0:T(128)} %pad_add_fusion.tab, bf16[2048,768]{1,0:T(8,128)(2,1)} %get-tuple-element.141.dk_ref, bf16[2048,768]{1,0:T(8,128)(2,1)} %get-tuple-element.142.dv_ref, bf16[4,96,768]{2,1,0:T(8,128)(2,1)} %pack_line.1.refs_0_, ...), custom_call_target="tpu_custom_call" | custom-call | flops 8000000000 | bytes 12000000 | tf_op jit(solution)/shard_map/input_rest/pallas_call | solution.py:670
  237.3 2.3 collective-permute-start.13
  239.6 1.8 collective-permute-start.14
  241.4 1.0 slice_bitcast_fusion
  242.4 1.1 collective-permute-start.15
  243.6 1.5 collective-permute-start.16
  245.1 0.8 collective-permute-start.17
  246.3 0.8 reshape.247
  247.0 3.6 %all-to-all-start = ((f32[32,1,288]{2,1,0:T(1,128)}), f32[32,1,288]{2,1,0:T(1,128)S(1)}, u32[]{:S(2)}, u32[]{:S(2)}) async-start(f32[32,1,288]{2,1,0:T(1,128)} %reshape.247), calls=%async_computation | async-start | bytes 98304 | tf_op jit(solution)/shard_map/all_to_all | solution.py:923
  250.7 8.5 %input_own.1 = f32[768,768]{1,0:T(8,128)} custom-call(s32[22]{0:T(128)} %pad_add_fusion.tab, bf16[768,768]{1,0:T(8,128)(2,1)} %get-tuple-element.140.dq_ref, bf16[2048,768]{1,0:T(8,128)(2,1)} %get-tuple-element.141.dk_ref, bf16[2048,768]{1,0:T(8,128)(2,1)} %get-tuple-element.142.dv_ref, bf16[4,96,768]{2,1,0:T(8,128)(2,1)} %pack_line.1.refs_0_, ...), custom_call_target="tpu_custom_call" | custom-call | flops 5000000000 | bytes 12000000 | tf_op jit(solution)/shard_map/input_own/pallas_call | solution.py:689
  259.2 20.8 %all-to-all-done = f32[32,1,288]{2,1,0:T(1,128)S(1)} async-done(((f32[32,1,288]{2,1,0:T(1,128)}), f32[32,1,288]{2,1,0:T(1,128)S(1)}, u32[]{:S(2)}, u32[]{:S(2)}) %all-to-all-start) | async-done | bytes 36896 | tf_op jit(solution)/shard_map/all_to_all | solution.py:923
  280.5 0.8 reduce.1
  282.1 0.9 copy-done.3
  283.0 4.4 %line_parts.1 = (bf16[96,2304]{1,0:T(8,128)(2,1)}, bf16[96,2304]{1,0:T(8,128)(2,1)}, bf16[96,2304]{1,0:T(8,128)(2,1)}, bf16[96,2304]{1,0:T(8,128)(2,1)}) custom-call(s32[1]{0:T(128)} %bitcast.6.tab, bf16[3,96,768]{2,1,0:T(8,128)(2,1)} %get-tuple-element.185.own_ref, bf16[3,96,768]{2,1,0:T(8,128)(2,1)} %collective-permute-done.15.refs_0_, ...), custom_call_target="tpu_custom_call" | custom-call | flops 2000000 | bytes 4000000 | tf_op jit(solution)/shard_map/line_parts/pallas_call | solution.py:704
  287.4 1.5 collective-permute-start.18
  288.9 1.6 collective-permute-start.19
  290.4 1.4 collective-permute-start.20
  291.8 1.4 constant_dynamic-slice_fusion.refs_4_
  293.2 15.6 %collective-permute-done.18.refs_1_ = bf16[96,2304]{1,0:T(8,128)(2,1)} collective-permute-done((bf16[96,2304]{1,0:T(8,128)(2,1)}, bf16[96,2304]{1,0:T(8,128)(2,1)}, u32[]{:S(2)}, u32[]{:S(2)}) %collective-permute-start.18) | collective-permute-done | bytes 442400 | tf_op jit(solution)/shard_map/ppermute | solution.py:928
  308.7 13.4 %collective-permute-done.19.refs_2_ = bf16[96,2304]{1,0:T(8,128)(2,1)} collective-permute-done((bf16[96,2304]{1,0:T(8,128)(2,1)}, bf16[96,2304]{1,0:T(8,128)(2,1)}, u32[]{:S(2)}, u32[]{:S(2)}) %collective-permute-start.19) | collective-permute-done | bytes 442400 | tf_op jit(solution)/shard_map/ppermute | solution.py:928
  322.1 2.8 total.1
  324.9 1.3 broadcast_in_dim.5
  326.1 10.2 %all-to-all-start.1 = ((f32[32,1,1]{2,1,0:T(1,128)}), f32[32,1,1]{2,1,0:T(1,128)S(1)}, u32[]{:S(2)}, u32[]{:S(2)}) async-start(f32[32,1,1]{2,1,0:T(1,128)} %broadcast_in_dim.5), calls=%async_computation.2 | async-start | bytes 32768 | tf_op jit(solution)/shard_map/all_to_all | solution.py:936
  336.4 3.2 convert_add_fusion
  339.6 3.9 %all-to-all-done.1 = f32[32,1,1]{2,1,0:T(1,128)S(1)} async-done(((f32[32,1,1]{2,1,0:T(1,128)}), f32[32,1,1]{2,1,0:T(1,128)S(1)}, u32[]{:S(2)}, u32[]{:S(2)}) %all-to-all-start.1) | async-done | bytes 160 | tf_op jit(solution)/shard_map/all_to_all | solution.py:936
  344.8 4.3 %update.1 = (f32[3,96,192]{2,1,0:T(8,128)}, f32[3,96,192]{2,1,0:T(8,128)}, f32[3,96,192]{2,1,0:T(8,128)}, f32[3,96,192]{2,1,0:T(8,128)}, f32[192,96]{1,0:T(8,128...) custom-call(f32[1,1]{1,0:T(1,128)} %bitcast.15.clip_ref, ...), custom_call_target="tpu_custom_call" | custom-call | flops 10000000 | bytes 8000000 | tf_op jit(solution)/shard_map/update/pallas_call | solution.py:749
  (75 shorter events, 6.6 us)
Async XLA Ops:
  7.2 19.7 %copy-start.4 = (bf16[768,768]{1,0:T(8,128)(2,1)S(1)}, bf16[768,768]{1,0:T(8,128)(2,1)}, u32[]{:S(2)}) copy-start(bf16[768,768]{1,0:T(8,128)(2,1)} %x_ref.1) | copy-start | bytes 3538948
  7.2 103.9 %all-gather.3.cloned.1.call-start = ((), (), s32[]{:S(2)}) async-start(), calls=%async_computation.4 | async-start | bytes 9732096 | tf_op jit(solution)/shard_map/all_gather | solution.py:850
  9.4 272.7 %reduce-scatter.2.cloned.1.call-start = ((), (), s32[]{:S(2)}) async-start(), calls=%async_computation.3 | async-start | bytes 13271040 | tf_op jit(solution)/shard_map/reduce_scatter | solution.py:901
  9.5 9.2 %collective-permute-start = (bf16[96,768]{1,0:T(8,128)(2,1)}, bf16[96,768]{1,0:T(8,128)(2,1)S(1)}, u32[]{:S(2)}, u32[]{:S(2)}) collective-permute-start(bf16[96,768]{1,0:T(8,128)(2,1)} %get-tuple-element.104.own_ref), channel_id=1, source_target_pairs={{0,1},{1,0},{2,3},{3,2},{4,5},{5,4},{6,7},{7,6},{8,9},{9,8},{10,11... | collective-permute-start | bytes 442376 | tf_op jit(solution)/shard_map/ppermute | solution.py:851
  12.5 14.3 %collective-permute-start.1 = (bf16[96,768]{1,0:T(8,128)(2,1)}, bf16[96,768]{1,0:T(8,128)(2,1)S(1)}, u32[]{:S(2)}, u32[]{:S(2)}) collective-permute-start(bf16[96,768]{1,0:T(8,128)(2,1)} %get-tuple-element.104.own_ref), channel_id=1, source_target_pairs={{0,2},{1,3},{2,0},{3,1},{4,6},{5,7},{6,4},{7,5},{8,10},{9,11},{10,... | collective-permute-start | bytes 442376 | tf_op jit(solution)/shard_map/ppermute | solution.py:851
  15.1 11.7 %collective-permute-start.2 = (bf16[96,768]{1,0:T(8,128)(2,1)}, bf16[96,768]{1,0:T(8,128)(2,1)S(1)}, u32[]{:S(2)}, u32[]{:S(2)}) collective-permute-start(bf16[96,768]{1,0:T(8,128)(2,1)} %get-tuple-element.104.own_ref), channel_id=1, source_target_pairs={{0,3},{1,2},{2,1},{3,0},{4,7},{5,6},{6,5},{7,4},{8,11},{9,10},{10,... | collective-permute-start | bytes 442376 | tf_op jit(solution)/shard_map/ppermute | solution.py:851
  18.6 9.9 %copy-start.14 = (bf16[96,768]{1,0:T(8,128)(2,1)}, bf16[96,768]{1,0:T(8,128)(2,1)S(1)}, u32[]{:S(2)}) copy-start(bf16[96,768]{1,0:T(8,128)(2,1)S(1)} %collective-permute-done.rest_0_) | copy-start | bytes 442372
  26.9 1.6 copy-start.15
  26.9 1.6 copy-start.16
  26.9 38.8 %collective-permute-start.4 = (bf16[512,768]{1,0:T(8,128)(2,1)S(1)}, bf16[512,768]{1,0:T(8,128)(2,1)}, u32[]{:S(2)}, u32[]{:S(2)}) collective-permute-start(bf16[512,768]{1,0:T(8,128)(2,1)S(1)} %constant_dynamic-slice_fusion.1), channel_id=1, source_target_pairs={{0,0},{1,2},{2,1},{3,3},{4,4},{5,6},{6,5},{7,7},{8,8},{9,10},{10,9... | collective-permute-start | bytes 2359304 | tf_op jit(solution)/shard_map/ppermute | solution.py:856
  28.5 16.2 %copy-start = (s32[3]{0:T(128)S(1)}, s32[3]{0:T(128)}, u32[]{:S(2)}) copy-start(s32[3]{0:T(128)} %param.26) | copy-start | bytes 40
  28.5 38.3 %copy-start.9 = (s32[3]{0:T(128)S(1)}, s32[3]{0:T(128)}, u32[]{:S(2)}) copy-start(s32[3]{0:T(128)} %param.28) | copy-start | bytes 40
  28.5 38.3 %copy-start.10 = (s32[3]{0:T(128)S(1)}, s32[3]{0:T(128)}, u32[]{:S(2)}) copy-start(s32[3]{0:T(128)} %param.27) | copy-start | bytes 40
  28.5 38.3 %copy-start.11 = (s32[3]{0:T(128)S(1)}, s32[3]{0:T(128)}, u32[]{:S(2)}) copy-start(s32[3]{0:T(128)} %param.29) | copy-start | bytes 40
  30.9 20.1 %collective-permute-start.5 = (bf16[4,96,768]{2,1,0:T(8,128)(2,1)}, bf16[4,96,768]{2,1,0:T(8,128)(2,1)}, u32[]{:S(2)}, u32[]{:S(2)}) collective-permute-start(bf16[4,96,768]{2,1,0:T(8,128)(2,1)} %pack_line.1.refs_0_), channel_id=1, source_target_pairs={{0,8},{1,9},{2,10},{3,11},{4,12},{5,13},{6,14},{7,15},{8,0},{9,1},... | collective-permute-start | bytes 1769480 | tf_op jit(solution)/shard_map/ppermute | solution.py:857
  32.4 21.5 %collective-permute-start.6 = (bf16[4,96,768]{2,1,0:T(8,128)(2,1)}, bf16[4,96,768]{2,1,0:T(8,128)(2,1)}, u32[]{:S(2)}, u32[]{:S(2)}) collective-permute-start(bf16[4,96,768]{2,1,0:T(8,128)(2,1)} %pack_line.1.refs_0_), channel_id=1, source_target_pairs={{0,16},{1,17},{2,18},{3,19},{4,20},{5,21},{6,22},{7,23},{8,24},{9,... | collective-permute-start | bytes 1769480 | tf_op jit(solution)/shard_map/ppermute | solution.py:857
  33.9 31.8 %collective-permute-start.7 = (bf16[4,96,768]{2,1,0:T(8,128)(2,1)}, bf16[4,96,768]{2,1,0:T(8,128)(2,1)}, u32[]{:S(2)}, u32[]{:S(2)}) collective-permute-start(bf16[4,96,768]{2,1,0:T(8,128)(2,1)} %pack_line.1.refs_0_), channel_id=1, source_target_pairs={{0,24},{1,25},{2,26},{3,27},{4,28},{5,29},{6,30},{7,31},{8,16},{9,... | collective-permute-start | bytes 1769480 | tf_op jit(solution)/shard_map/ppermute | solution.py:857
  34.4 43.1 %collective-permute-start.3 = (bf16[768,768]{1,0:T(8,128)(2,1)S(1)}, bf16[768,768]{1,0:T(8,128)(2,1)S(1)}, u32[]{:S(2)}, u32[]{:S(2)}) collective-permute-start(bf16[768,768]{1,0:T(8,128)(2,1)S(1)} %copy-done.4), channel_id=1, source_target_pairs={{0,1},{1,0},{2,3},{3,2},{4,5},{5,4},{6,7},{7,6},{8,9},{9,8},{10,11... | collective-permute-start | bytes 3538952 | tf_op jit(solution)/shard_map/ppermute | solution.py:855
  51.0 17.4 %collective-permute-start.9 = (bf16[4,96,768]{2,1,0:T(8,128)(2,1)}, bf16[4,96,768]{2,1,0:T(8,128)(2,1)}, u32[]{:S(2)}, u32[]{:S(2)}) collective-permute-start(bf16[4,96,768]{2,1,0:T(8,128)(2,1)} %collective-permute-done.5.refs_1_), channel_id=1, source_target_pairs={{0,4},{1,5},{2,6},{3,7},{4,0},{5,1},{6,2},{7,3},{8,12},{9,13},{10,... | collective-permute-start | bytes 1769480 | tf_op jit(solution)/shard_map/ppermute | solution.py:859
  53.9 14.5 %collective-permute-start.8 = (bf16[4,96,768]{2,1,0:T(8,128)(2,1)}, bf16[4,96,768]{2,1,0:T(8,128)(2,1)}, u32[]{:S(2)}, u32[]{:S(2)}) collective-permute-start(bf16[4,96,768]{2,1,0:T(8,128)(2,1)} %pack_line.1.refs_0_), channel_id=1, source_target_pairs={{0,4},{1,5},{2,6},{3,7},{4,0},{5,1},{6,2},{7,3},{8,12},{9,13},{10,... | collective-permute-start | bytes 1769480 | tf_op jit(solution)/shard_map/ppermute | solution.py:859
  65.7 3.1 collective-permute-start.10
  65.7 3.1 collective-permute-start.11
  68.8 8.7 %copy-start.13 = (bf16[4,96,768]{2,1,0:T(8,128)(2,1)}, bf16[4,96,768]{2,1,0:T(8,128)(2,1)S(1)}, u32[]{:S(2)}) copy-start(bf16[4,96,768]{2,1,0:T(8,128)(2,1)S(1)} %collective-permute-done.11.refs_7_) | copy-start | bytes 1769476
  77.5 1.0 copy-start.12
  227.6 9.2 %collective-permute-start.12 = (bf16[4,3,96,768]{3,2,1,0:T(8,128)(2,1)}, bf16[4,3,96,768]{3,2,1,0:T(8,128)(2,1)S(1)}, u32[]{:S(2)}, u32[]{:S(2)}) collective-permute-start(bf16[4,3,96,768]{3,2,1,0:T(8,128)(2,1)} %get-tuple-element.128), channel_id=1, source_target_pairs={{0,4},{1,5},{2,6},{3,7},{4,0},{5,1},{6,2},{7,3},{8,12},{9,13},{10,... | collective-permute-start | bytes 5308424 | tf_op jit(solution)/shard_map/ppermute | solution.py:910
  227.6 9.1 %copy-start.2 = (bf16[4,3,96,768]{3,2,1,0:T(8,128)(2,1)S(1)}, bf16[4,3,96,768]{3,2,1,0:T(8,128)(2,1)}, u32[]{:S(2)}) copy-start(bf16[4,3,96,768]{3,2,1,0:T(8,128)(2,1)} %get-tuple-element.127) | copy-start | bytes 5308420
  237.2 8.7 %copy-start.5 = (f32[3,768]{1,0:T(4,128)S(1)}, f32[3,768]{1,0:T(4,128)}, u32[]{:S(2)}) copy-start(f32[3,768]{1,0:T(4,128)} %get-tuple-element.137) | copy-start | bytes 27652
  237.3 8.7 %copy-start.6 = (f32[3,768]{1,0:T(4,128)S(1)}, f32[3,768]{1,0:T(4,128)}, u32[]{:S(2)}) copy-start(f32[3,768]{1,0:T(4,128)} %get-tuple-element.136) | copy-start | bytes 27652
  237.3 8.7 %copy-start.7 = (f32[4,768]{1,0:T(4,128)S(1)}, f32[4,768]{1,0:T(4,128)}, u32[]{:S(2)}) copy-start(f32[4,768]{1,0:T(4,128)} %get-tuple-element.138) | copy-start | bytes 36868
  237.3 8.7 %copy-start.8 = (f32[2,768]{1,0:T(2,128)S(1)}, f32[2,768]{1,0:T(2,128)}, u32[]{:S(2)}) copy-start(f32[2,768]{1,0:T(2,128)} %get-tuple-element.135) | copy-start | bytes 18436
  237.3 44.8 %collective-permute-start.13 = (bf16[768,768]{1,0:T(8,128)(2,1)}, bf16[768,768]{1,0:T(8,128)(2,1)S(1)}, u32[]{:S(2)}, u32[]{:S(2)}) collective-permute-start(bf16[768,768]{1,0:T(8,128)(2,1)} %get-tuple-element.144), channel_id=1, source_target_pairs={{0,1},{1,0},{2,3},{3,2},{4,5},{5,4},{6,7},{7,6},{8,9},{9,8},{10,11... | collective-permute-start | bytes 3538952 | tf_op jit(solution)/shard_map/ppermute | solution.py:917
  239.6 42.4 %collective-permute-start.14 = (bf16[512,768]{1,0:T(8,128)(2,1)}, bf16[512,768]{1,0:T(8,128)(2,1)S(1)}, u32[]{:S(2)}, u32[]{:S(2)}) collective-permute-start(bf16[512,768]{1,0:T(8,128)(2,1)} %get-tuple-element.145), channel_id=1, source_target_pairs={{0,0},{1,2},{2,1},{3,3},{4,4},{5,6},{6,5},{7,7},{8,8},{9,10},{10,9... | collective-permute-start | bytes 2359304 | tf_op jit(solution)/shard_map/ppermute | solution.py:918
  242.4 39.6 %collective-permute-start.15 = (bf16[3,96,768]{2,1,0:T(8,128)(2,1)}, bf16[3,96,768]{2,1,0:T(8,128)(2,1)}, u32[]{:S(2)}, u32[]{:S(2)}) collective-permute-start(bf16[3,96,768]{2,1,0:T(8,128)(2,1)} %get-tuple-element.188), channel_id=1, source_target_pairs={{0,8},{1,9},{2,10},{3,11},{4,12},{5,13},{6,14},{7,15},{8,0},{9,1},... | collective-permute-start | bytes 1327112 | tf_op jit(solution)/shard_map/ppermute | solution.py:916
  243.6 38.5 %collective-permute-start.16 = (bf16[3,96,768]{2,1,0:T(8,128)(2,1)S(1)}, bf16[3,96,768]{2,1,0:T(8,128)(2,1)}, u32[]{:S(2)}, u32[]{:S(2)}) collective-permute-start(bf16[3,96,768]{2,1,0:T(8,128)(2,1)S(1)} %get-tuple-element.187), channel_id=1, source_target_pairs={{0,16},{1,17},{2,18},{3,19},{4,20},{5,21},{6,22},{7,23},{8,24},{9,... | collective-permute-start | bytes 1327112 | tf_op jit(solution)/shard_map/ppermute | solution.py:916
  245.1 36.9 %collective-permute-start.17 = (bf16[3,96,768]{2,1,0:T(8,128)(2,1)S(1)}, bf16[3,96,768]{2,1,0:T(8,128)(2,1)}, u32[]{:S(2)}, u32[]{:S(2)}) collective-permute-start(bf16[3,96,768]{2,1,0:T(8,128)(2,1)S(1)} %get-tuple-element.186), channel_id=1, source_target_pairs={{0,24},{1,25},{2,26},{3,27},{4,28},{5,29},{6,30},{7,31},{8,16},{9,... | collective-permute-start | bytes 1327112 | tf_op jit(solution)/shard_map/ppermute | solution.py:916
  247.0 32.9 %all-to-all-start = ((f32[32,1,288]{2,1,0:T(1,128)}), f32[32,1,288]{2,1,0:T(1,128)S(1)}, u32[]{:S(2)}, u32[]{:S(2)}) async-start(f32[32,1,288]{2,1,0:T(1,128)} %reshape.247), calls=%async_computation | async-start | bytes 98304 | tf_op jit(solution)/shard_map/all_to_all | solution.py:923
  282.1 0.9 copy-start.3
  283.0 53.4 %copy-start.1 = (f32[768,768]{1,0:T(8,128)S(1)}, f32[768,768]{1,0:T(8,128)}, u32[]{:S(2)}) copy-start(f32[768,768]{1,0:T(8,128)} %input_own.1) | copy-start | bytes 7077892
  287.4 21.3 %collective-permute-start.18 = (bf16[96,2304]{1,0:T(8,128)(2,1)}, bf16[96,2304]{1,0:T(8,128)(2,1)}, u32[]{:S(2)}, u32[]{:S(2)}) collective-permute-start(bf16[96,2304]{1,0:T(8,128)(2,1)} %get-tuple-element.156), channel_id=1, source_target_pairs={{0,1},{1,0},{2,3},{3,2},{4,5},{5,4},{6,7},{7,6},{8,9},{9,8},{10,11... | collective-permute-start | bytes 1327112 | tf_op jit(solution)/shard_map/ppermute | solution.py:928
  288.9 33.2 %collective-permute-start.19 = (bf16[96,2304]{1,0:T(8,128)(2,1)}, bf16[96,2304]{1,0:T(8,128)(2,1)}, u32[]{:S(2)}, u32[]{:S(2)}) collective-permute-start(bf16[96,2304]{1,0:T(8,128)(2,1)} %get-tuple-element.157), channel_id=1, source_target_pairs={{0,2},{1,3},{2,0},{3,1},{4,6},{5,7},{6,4},{7,5},{8,10},{9,11},{10,... | collective-permute-start | bytes 1327112 | tf_op jit(solution)/shard_map/ppermute | solution.py:928
  290.4 31.7 %collective-permute-start.20 = (bf16[96,2304]{1,0:T(8,128)(2,1)}, bf16[96,2304]{1,0:T(8,128)(2,1)}, u32[]{:S(2)}, u32[]{:S(2)}) collective-permute-start(bf16[96,2304]{1,0:T(8,128)(2,1)} %get-tuple-element.158), channel_id=1, source_target_pairs={{0,3},{1,2},{2,1},{3,0},{4,7},{5,6},{6,5},{7,4},{8,11},{9,10},{10,... | collective-permute-start | bytes 1327112 | tf_op jit(solution)/shard_map/ppermute | solution.py:928
  326.1 17.3 %all-to-all-start.1 = ((f32[32,1,1]{2,1,0:T(1,128)}), f32[32,1,1]{2,1,0:T(1,128)S(1)}, u32[]{:S(2)}, u32[]{:S(2)}) async-start(f32[32,1,1]{2,1,0:T(1,128)} %broadcast_in_dim.5), calls=%async_computation.2 | async-start | bytes 32768 | tf_op jit(solution)/shard_map/all_to_all | solution.py:936
Sparse Core Ops, SparseCore 0:
  11.4 97.8 all-gather.2
  173.6 102.1 reduce-scatter.1

commit v3 on v2

--- a/solution.py
+++ b/solution.py
@@ -74,15 +74,11 @@
             target[pl.ds(pl.multiple_of(at, RP), RP), col : col + width] = pieces[4 * half + n][part]
 
 
-def key_sides(k, count):
-    rows = k.shape[0]
-    lane = lane_ids(rows)
-    place = lane % HDIM
-    row = lax.broadcasted_iota(jnp.int32, (rows, 128), 0)
+def key_extra(count):
+    place = lane_ids(BLK) % HDIM
+    row = lax.broadcasted_iota(jnp.int32, (BLK, 128), 0)
     mask = jnp.where(row >= count, NEG_FILL, 0.0)
-    extra = jnp.where(place == 0, mask, jnp.where(place <= 3, 1.0, 0.0)).astype(BF)
-    low = lane < HDIM
-    return jnp.where(low, k, extra), jnp.where(low, extra, k)
+    return jnp.where(place == 0, mask, jnp.where(place <= 3, 1.0, 0.0)).astype(BF)
 
 
 def split_three(value):
@@ -97,8 +93,14 @@
     tab, own_ref, nb_ref, mid_ref, *refs
 ):
     pieces = refs[:8]
-    vec_ref, o_ref, qe_ref, qo_ref, k_ref, v_ref, xt_ref, w_s, ka_e, ka_o, va_e, va_o = refs[8:]
+    vec_ref, o_ref, qe_ref, qo_ref, k_ref, v_ref, xt_ref, w_s, ka_e, ka_o, va_s, extra_s = refs[8:]
     mine = pl.ds(pl.multiple_of(pl.program_id(0) * 128, 128), 128)
+
+    @pl.when(pl.program_id(0) == 0)
+    def _():
+        for b in range(8):
+            extra_s[b] = key_extra(tab[12 + b])
+
     for part in range(3):
         assemble(tab, pieces, part, w_s, 128 * part)
     bias_q = vec_ref[0:1, :]
@@ -106,48 +108,56 @@
     low = lane_ids(BLK) < HDIM
     place = lane_ids(BLK) % HDIM
     ones = jnp.ones((BLK, 128), BF)
+    for src, first, count in ((own_ref, 0, 3), (nb_ref, 3, 3), (mid_ref, 6, 2)):
+        at = slice(first * BLK, (first + count) * BLK)
+        xt_ref[:, at] = src[:, mine].T
+        kv = dot_nn(src[...], w_s[:, 128:384])
+        k_ref[at, :] = kv[:, :128].astype(BF)
+        v_ref[at, :] = (kv[:, 128:] + bias_v).astype(BF)
     for b in range(8):
-        src, at = (own_ref, b) if b < 3 else (nb_ref, b - 3) if b < 6 else (mid_ref, b - 6)
-        xt_ref[:, b * BLK : (b + 1) * BLK] = src[at * BLK : (at + 1) * BLK, mine].T
-        kv = dot_nn(src[at * BLK : (at + 1) * BLK, :], w_s[:, 128:384])
-        k = kv[:, :128].astype(BF)
-        v = (kv[:, 128:] + bias_v).astype(BF)
-        k_ref[b * BLK : (b + 1) * BLK, :] = k
-        v_ref[b * BLK : (b + 1) * BLK, :] = v
-        k_even, k_odd = key_sides(k, tab[12 + b])
-        ka_e[b] = k_even
-        ka_o[b] = k_odd
-        va_e[b] = jnp.where(low, v, ones)
-        va_o[b] = jnp.where(low, ones, v)
+        at = slice(b * BLK, (b + 1) * BLK)
+        k = k_ref[at, :]
+        ka_e[b] = jnp.where(low, k, extra_s[b])
+        ka_o[b] = jnp.where(low, extra_s[b], k)
+        va_s[0, b] = jnp.where(low, v_ref[at, :], ones)
+        va_s[1, b] = jnp.where(low, ones, v_ref[at, :])
     q_extra = jnp.where(place == 0, 1.0, 0.0).astype(BF)
+    queries = []
     for i in range(3):
         q = (dot_nn(own_ref[i * BLK : (i + 1) * BLK, :], w_s[:, :128]) + bias_q).astype(BF) * jnp.asarray(0.125, BF)
-        outs = []
-        for head, (ka, va) in enumerate(((ka_e, va_e), (ka_o, va_o))):
-            qa = jnp.where(low, q, q_extra) if head == 0 else jnp.where(low, q_extra, q)
-            scores = [dot_nt(qa, ka[tab[4 * i + j]]) for j in range(4)]
-            peak = jnp.max(
-                jnp.maximum(jnp.maximum(scores[0], scores[1]), jnp.maximum(scores[2], scores[3])), -1, keepdims=True
-            )
-            acc = None
-            for j in range(4):
-                probs = jnp.exp(scores[j] - peak).astype(BF)
-                part = dot_nn(probs, va[tab[4 * i + j]])
-                acc = part if acc is None else acc + part
-            log_sum = peak + jnp.log(acc)
-            high, mid, small = split_three(-log_sum)
-            extra = jnp.where(place == 0, 1.0, 0.0).astype(BF)
-            extra = jnp.where(place == 1, high, extra)
-            extra = jnp.where(place == 2, mid, extra)
-            extra = jnp.where(place == 3, small, extra)
-            if head == 0:
-                qe_ref[i * BLK : (i + 1) * BLK, :] = jnp.where(low, q, extra)
-            else:
-                qo_ref[i * BLK : (i + 1) * BLK, :] = jnp.where(low, extra, q)
-            outs.append(acc)
-        total = jnp.where(low, outs[1], outs[0])
-        value = jnp.where(low, outs[0], outs[1])
-        o_ref[i * BLK : (i + 1) * BLK, :] = (value / pltpu.roll(total, HDIM, 1)).astype(BF)
+        queries.append((jnp.where(low, q, q_extra), jnp.where(low, q_extra, q)))
+    keys = (ka_e, ka_o)
+
+    def score(unit, j):
+        i, head = unit
+        return dot_nt(queries[i][head], keys[head][tab[4 * i + j]])
+
+    units = [(i, head) for i in range(3) for head in range(2)]
+    now = [score(units[0], j) for j in range(4)]
+    for n, (i, head) in enumerate(units):
+        peak = jnp.max(jnp.maximum(jnp.maximum(now[0], now[1]), jnp.maximum(now[2], now[3])), -1, keepdims=True)
+        acc = jnp.zeros((BLK, 128), F32)
+        later = []
+        for j in range(4):
+            if n + 1 < len(units):
+                later.append(score(units[n + 1], j))
+            probs = jnp.exp(now[j] - peak).astype(BF)
+            acc = acc + dot_nn(probs, va_s[head, tab[4 * i + j]])
+        now = later
+        rows = slice(i * BLK, (i + 1) * BLK)
+        high, mid, small = split_three(-(peak + jnp.log(acc)))
+        extra = jnp.where(place == 0, 1.0, 0.0).astype(BF)
+        extra = jnp.where(place == 1, high, extra)
+        extra = jnp.where(place == 2, mid, extra)
+        extra = jnp.where(place == 3, small, extra)
+        if head == 0:
+            qe_ref[rows, :] = jnp.where(low, queries[i][0], extra)
+            even = acc
+        else:
+            qo_ref[rows, :] = jnp.where(low, extra, queries[i][1])
+            total = jnp.where(low, acc, even)
+            value = jnp.where(low, even, acc)
+            o_ref[rows, :] = (value / pltpu.roll(total, HDIM, 1)).astype(BF)
 
 
 def attend_back_kernel(
@@ -169,60 +179,76 @@
     ka_o,
     vb_e,
     vb_o,
-    kt_s,
+    extra_s,
     dk_s,
     dv_s,
     dkv_s,
 ):
+    @pl.when(pl.program_id(0) == 0)
+    def _():
+        for b in range(8):
+            extra_s[b] = key_extra(tab[12 + b])
+
     low = lane_ids(BLK) < HDIM
     place = lane_ids(BLK) % HDIM
     v_extra = jnp.where(place < 3, 1.0, 0.0).astype(BF)
     zero = jnp.zeros((BLK, 128), BF)
     for b in range(8):
-        k = k_ref[b * BLK : (b + 1) * BLK, :]
-        v = v_ref[b * BLK : (b + 1) * BLK, :]
-        k_even, k_odd = key_sides(k, tab[12 + b])
-        ka_e[b] = k_even
-        ka_o[b] = k_odd
+        at = slice(b * BLK, (b + 1) * BLK)
+        k = k_ref[at, :]
+        v = v_ref[at, :]
+        ka_e[b] = jnp.where(low, k, extra_s[b])
+        ka_o[b] = jnp.where(low, extra_s[b], k)
         vb_e[b] = jnp.where(low, v, v_extra)
         vb_o[b] = jnp.where(low, v_extra, v)
-        kt_s[b] = k.T
-        dk_s[b] = jnp.zeros((BLK, 128), F32)
-        dv_s[b] = jnp.zeros((BLK, 128), F32)
+    dk_s[...] = jnp.zeros(dk_s.shape, F32)
+    dv_s[...] = jnp.zeros(dv_s.shape, F32)
+    sides = ((ka_e, vb_e), (ka_o, vb_o))
+    given = []
     for i in range(3):
         rows = slice(i * BLK, (i + 1) * BLK)
         d_out = do_ref[rows, :]
         product = d_out.astype(F32) * o_ref[rows, :].astype(F32)
         qas = (qe_ref[rows, :], qo_ref[rows, :])
-        sides = []
+        d_augs = []
         for head in range(2):
             mine = low if head == 0 else jnp.logical_not(low)
             delta = jnp.sum(jnp.where(mine, product, 0.0), -1, keepdims=True)
             high, mid, small = split_three(-delta)
             extra = jnp.where(place == 0, high, jnp.where(place == 1, mid, jnp.where(place == 2, small, zero)))
-            sides.append((jnp.where(mine, d_out, extra), jnp.where(mine, d_out, zero), jnp.where(mine, qas[head], zero)))
-        dqt = [None, None]
+            d_augs.append(jnp.where(mine, d_out, extra))
+        given.append((qas, d_augs, d_out.T, jnp.where(low, qas[0], qas[1]).T))
+
+    def score(unit, j):
+        i, head = unit
+        b = tab[4 * i + j]
+        qas, d_augs = given[i][:2]
+        return dot_nt(qas[head], sides[head][0][b]), dot_nt(d_augs[head], sides[head][1][b])
+
+    units = [(i, head) for i in range(3) for head in range(2)]
+    now = [score(units[0], j) for j in range(4)]
+    for n, (i, head) in enumerate(units):
+        lanes = slice(head * HDIM, (head + 1) * HDIM)
+        dot_t, qt = given[i][2:]
+        dq = jnp.zeros((BLK, 128), F32)
+        later = []
         for j in range(4):
+            if n + 1 < len(units):
+                later.append(score(units[n + 1], j))
             b = tab[4 * i + j]
-            dv_part = None
-            dk_part = None
-            for head, (ka, vb) in enumerate(((ka_e, vb_e), (ka_o, vb_o))):
-                d_aug, d_only, q_only = sides[head]
-                probs = jnp.exp(dot_nt(ka[b], qas[head]))
-                d_probs = dot_nt(vb[b], d_aug)
-                d_scores = (probs * d_probs).astype(BF)
-                v_add = dot_nn(probs.astype(BF), d_only)
-                k_add = dot_nn(d_scores, q_only)
-                dv_part = v_add if dv_part is None else dv_part + v_add
-                dk_part = k_add if dk_part is None else dk_part + k_add
-                q_add = dot_nn(kt_s[b, head * HDIM : (head + 1) * HDIM, :], d_scores)
-                dqt[head] = q_add if dqt[head] is None else dqt[head] + q_add
-            dv_s[b] += dv_part
-            dk_s[b] += dk_part
-        dq_ref[rows, :] = (jnp.concatenate(dqt, 0).T * 0.125).astype(BF)
+            probs = jnp.exp(now[j][0])
+            d_scores = (probs * now[j][1]).astype(BF)
+            dv_s[b, lanes, :] += dot_nn(dot_t[lanes, :], probs.astype(BF))
+            dk_s[b, lanes, :] += dot_nn(qt[lanes, :], d_scores)
+            dq = dq + dot_nn(d_scores, k_ref[pl.ds(pl.multiple_of(b * BLK, BLK), BLK), :])
+        now = later
+        if head == 0:
+            even = dq
+        else:
+            dq_ref[i * BLK : (i + 1) * BLK, :] = (jnp.where(low, even, dq) * 0.125).astype(BF)
     for b in range(8):
-        dk = dk_s[b].astype(BF)
-        dv = dv_s[b].astype(BF)
+        dk = dk_s[b].T.astype(BF)
+        dv = dv_s[b].T.astype(BF)
         dk_ref[b * BLK : (b + 1) * BLK, :] = dk
         dv_ref[b * BLK : (b + 1) * BLK, :] = dv
         dkv_s[b * BLK : (b + 1) * BLK, :128] = dk
@@ -265,134 +291,95 @@
     return root * (gz - jnp.mean(gz, -1, keepdims=True) - hat * jnp.mean(gz * hat, -1, keepdims=True))
 
 
-def feed_kernel(
-    tab,
-    o_ref,
-    x_ref,
-    *refs,
-):
+def feed_kernel(tab, o_ref, x_ref, *refs):
     pieces = refs[:8]
-    (vec_ref, w_ref, cot_ref, weight_ref, u_ref, gp_ref, out_ref, dz2_ref, e2_ref, e2t_ref) = refs[8:18]
-    (h1t_ref, hat1_ref, root1_ref, sums_ref, wo_s, h1_s, h1b_s, z2_s) = refs[18:]
+    vec_ref, w_ref, cot_ref, weight_ref, out_ref, dw_ref, dz1_ref, do_ref, sums_ref, db1_ref = refs[8:18]
+    wo_s, h1b_s, h1t_s, hat1_s, root1_s, z2_s, u_s, gp_s, e2_s, e2t_s, ep_s = refs[18:]
     step = pl.program_id(0)
+    blocks = [slice(i * BLK, (i + 1) * BLK) for i in range(3)]
 
     @pl.when(step == 0)
     def _():
         assemble(tab, pieces, 0, wo_s, 0)
-        for i in range(3):
-            rows = slice(i * BLK, (i + 1) * BLK)
+        for rows in blocks:
             z1 = x_ref[rows, :].astype(F32) + dot_nt(o_ref[rows, :], wo_s[...]) + vec_ref[2:3, :]
             hat, root = norm_parts(z1)
             h1 = hat * vec_ref[3:4, :] + vec_ref[4:5, :]
-            hat1_ref[rows, :] = hat
-            root1_ref[rows, :] = root
-            h1_s[rows, :] = h1
+            hat1_s[rows, :] = hat
+            root1_s[rows, :] = root
+            z2_s[rows, :] = h1 + vec_ref[5:6, :]
             h1b = h1.astype(BF)
             h1b_s[rows, :] = h1b
-            h1t_ref[:, rows] = h1b.T
-
-    w1 = w_ref[:, 0, 0].reshape(D, D)
-    w2t = w_ref[:, 0, 1].reshape(D, D)
-    bias = vec_ref[pl.ds(8 + step, 1), :]
-    for i in range(3):
-        rows = slice(i * BLK, (i + 1) * BLK)
-        pre = dot_nn(h1b_s[rows, :], w1) + bias
-        act, slope = gelu_both(pre)
-        act = act.astype(BF)
-        u_ref[rows, :] = act
-        gp_ref[rows, :] = slope.astype(BF)
-        feed = dot_nt(act, w2t)
-
-        @pl.when(step == 0)
-        def _():
-            z2_s[rows, :] = feed
-
-        @pl.when(step > 0)
-        def _():
-            z2_s[rows, :] += feed
+            h1t_s[:, rows] = h1b.T
+
+    @pl.when(step < 4)
+    def _():
+        w1 = w_ref[:, 0, 0].reshape(D, D)
+        w2t = w_ref[:, 0, 1].reshape(D, D)
+        bias = vec_ref[pl.ds(8 + step, 1), :]
+        now = dot_nn(h1b_s[:BLK, :], w1)
+        for i, rows in enumerate(blocks):
+            later = dot_nn(h1b_s[blocks[i + 1], :], w1) if i < 2 else None
+            act, slope = gelu_both(now + bias)
+            act = act.astype(BF)
+            u_s[step, rows, :] = act
+            gp_s[step, rows, :] = slope.astype(BF)
+            z2_s[rows, :] += dot_nt(act, w2t)
+            now = later
 
     @pl.when(step == 3)
     def _():
         sums = [jnp.zeros((1, D), F32) for _ in range(3)]
-        for i in range(3):
-            rows = slice(i * BLK, (i + 1) * BLK)
-            z2 = h1_s[rows, :] + z2_s[rows, :] + vec_ref[5:6, :]
-            hat, root = norm_parts(z2)
+        for rows in blocks:
+            hat, root = norm_parts(z2_s[rows, :])
             out_ref[rows, :] = (hat * vec_ref[6:7, :] + vec_ref[7:8, :]).astype(BF)
             cot = cot_ref[rows, :].astype(F32) * weight_ref[rows, :]
             dz2 = norm_back(cot, vec_ref[6:7, :], hat, root)
-            dz2_ref[rows, :] = dz2
+            z2_s[rows, :] = dz2
             e2 = dz2.astype(BF)
-            e2_ref[rows, :] = e2
-            e2t_ref[:, rows] = e2.T
+            e2_s[rows, :] = e2
+            e2t_s[:, rows] = e2.T
             sums[0] += jnp.sum(dz2, 0, keepdims=True)
             sums[1] += jnp.sum(cot * hat, 0, keepdims=True)
             sums[2] += jnp.sum(cot, 0, keepdims=True)
         for n in range(3):
-            sums_ref[n : n + 1, :] = sums[n]
-
-
-def feed_back_kernel(
-    tab,
-    e2_ref,
-    e2t_ref,
-    h1t_ref,
-    u_ref,
-    gp_ref,
-    w_ref,
-    dz2_ref,
-    hat1_ref,
-    root1_ref,
-    o_ref,
-    *refs,
-):
-    pieces = refs[:8]
-    vec_ref, dw_ref, dz1_ref, do_ref, sums_ref, db1_ref, ep_s, dh_s, wo_s, e1t_s = refs[8:]
-    step = pl.program_id(0)
-    @pl.when(step < 4)
-    def _():
+            sums_ref[3 + n : 4 + n, :] = sums[n]
+
+    @pl.when(jnp.logical_and(step >= 4, step < 8))
+    def _():
+        m = step - 4
         w1 = w_ref[:, 0, 0].reshape(D, D)
         w2t = w_ref[:, 0, 1].reshape(D, D)
         db1 = jnp.zeros((1, D), F32)
-        for i in range(3):
-            rows = slice(i * BLK, (i + 1) * BLK)
-            du = dot_nn(e2_ref[rows, :], w2t)
-            ep = (gp_ref[rows, :].astype(F32) * du).astype(BF)
+        now = dot_nn(e2_s[:BLK, :], w2t)
+        for i, rows in enumerate(blocks):
+            later = dot_nn(e2_s[blocks[i + 1], :], w2t) if i < 2 else None
+            ep = (gp_s[m, rows, :].astype(F32) * now).astype(BF)
             ep_s[rows, :] = ep
             db1 += jnp.sum(ep.astype(F32), 0, keepdims=True)
-            back = dot_nt(ep, w1)
-
-            @pl.when(step == 0)
-            def _():
-                dh_s[rows, :] = back + dz2_ref[rows, :]
-
-            @pl.when(step > 0)
-            def _():
-                dh_s[rows, :] += back
-
-        db1_ref[pl.ds(step, 1), :] = db1
-        dw_ref[:, 0, 0] = dot_nn(h1t_ref[...], ep_s[...]).astype(BF).reshape(RB, RP, D)
-        dw_ref[:, 0, 1] = dot_nn(e2t_ref[...], u_ref[...]).astype(BF).reshape(RB, RP, D)
-
-    @pl.when(step == 4)
-    def _():
-        assemble(tab, pieces, 0, wo_s, 0)
+            z2_s[rows, :] += dot_nt(ep, w1)
+            now = later
+        db1_ref[pl.ds(m, 1), :] = db1
+        dw_ref[:, 0, 0] = dot_nn(h1t_s[...], ep_s[...]).astype(BF).reshape(RB, RP, D)
+        dw_ref[:, 0, 1] = dot_nn(e2t_s[...], u_s[m]).astype(BF).reshape(RB, RP, D)
+
+    @pl.when(step == 8)
+    def _():
         sums = [jnp.zeros((1, D), F32) for _ in range(3)]
-        for i in range(3):
-            rows = slice(i * BLK, (i + 1) * BLK)
-            dh = dh_s[rows, :]
-            hat = hat1_ref[rows, :]
-            dz1 = norm_back(dh, vec_ref[3:4, :], hat, root1_ref[rows, :])
+        for rows in blocks:
+            dh = z2_s[rows, :]
+            hat = hat1_s[rows, :]
+            dz1 = norm_back(dh, vec_ref[3:4, :], hat, root1_s[rows, :])
             dz1_ref[rows, :] = dz1
             e1 = dz1.astype(BF)
-            e1t_s[:, rows] = e1.T
+            e2t_s[:, rows] = e1.T
             do_ref[rows, :] = dot_nn(e1, wo_s[...]).astype(BF)
             sums[0] += jnp.sum(dz1, 0, keepdims=True)
             sums[1] += jnp.sum(dh * hat, 0, keepdims=True)
             sums[2] += jnp.sum(dh, 0, keepdims=True)
         for n in range(3):
             sums_ref[n : n + 1, :] = sums[n]
-        dw_ref[:, 0, 0] = dot_nn(e1t_s[...], o_ref[...]).astype(BF).reshape(RB, RP, D)
+        dw_ref[:, 0, 0] = dot_nn(e2t_s[...], o_ref[...]).astype(BF).reshape(RB, RP, D)
         dw_ref[:, 0, 1] = jnp.zeros((RB, RP, D), BF)
 
 
@@ -501,7 +488,7 @@
         [columns(ROWS), columns(ROWS), columns(ROWS), columns(8 * BLK), columns(8 * BLK)]
         + [pl.BlockSpec((128, 8 * BLK), lambda s, t: (s, 0))],
         [shape_of((ROWS, D), BF)] * 3 + [shape_of((8 * BLK, D), BF)] * 2 + [shape_of((D, 8 * BLK), BF)],
-        [vm((D, 384), BF)] + [vm((8, BLK, 128), BF)] * 4,
+        [vm((D, 384), BF)] + [vm((8, BLK, 128), BF)] * 2 + [vm((2, 8, BLK, 128), BF), vm((8, BLK, 128), BF)],
         5_000_000_000,
         16_000_000,
         "attend",
@@ -529,9 +516,8 @@
             shape_of((RB // 2, 3, RP, D), BF),
             shape_of((2, D), F32),
         ],
-        [vm((8, BLK, 128), BF)] * 4
-        + [vm((8, 128, BLK), BF)]
-        + [vm((8, BLK, 128), F32)] * 2
+        [vm((8, BLK, 128), BF)] * 5
+        + [vm((8, 128, BLK), F32)] * 2
         + [vm((8 * BLK, BLK), BF)],
         50_000_000_000,
         24_000_000,
@@ -541,91 +527,55 @@
 
 def feed(tab, o, x, pieces, vectors, w, cot, weight):
     wo_spec = pl.BlockSpec((1, RP, D), lambda s, t: (3, 0, 0))
+
+    def group(s):
+        return jnp.where(s < 4, s, jnp.minimum(s - 4, 3))
+
     return call(
         feed_kernel,
-        4,
+        9,
         [
             whole(ROWS, D),
             whole(ROWS, D),
             *[wo_spec] * 8,
             whole(12, D),
-            pl.BlockSpec((RB, 1, 2, RP, D), lambda s, t: (0, s, 0, 0, 0)),
+            pl.BlockSpec((RB, 1, 2, RP, D), lambda s, t: (0, group(s), 0, 0, 0)),
             whole(ROWS, D),
             whole(ROWS, 1),
         ],
         [
-            columns(ROWS, D),
-            columns(ROWS, D),
+            whole(ROWS, D),
+            pl.BlockSpec((RB, 1, 2, RP, D), lambda s, t: (0, jnp.maximum(s - 4, 0), 0, 0, 0)),
             whole(ROWS, D),
             whole(ROWS, D),
-            whole(ROWS, D),
-            whole(D, ROWS),
-            whole(D, ROWS),
-            whole(ROWS, D),
-            whole(ROWS, 1),
-            whole(3, D),
-        ],
-        [
-            shape_of((ROWS, FF), BF),
-            shape_of((ROWS, FF), BF),
-            shape_of((ROWS, D), BF),
-            shape_of((ROWS, D), F32),
-            shape_of((ROWS, D), BF),
-            shape_of((D, ROWS), BF),
-            shape_of((D, ROWS), BF),
-            shape_of((ROWS, D), F32),
-            shape_of((ROWS, 1), F32),
-            shape_of((3, D), F32),
-        ],
-        [vm((D, D), BF), vm((ROWS, D), F32), vm((ROWS, D), BF), vm((ROWS, D), F32)],
-        18_000_000_000,
-        40_000_000,
-        "feed",
-    )(tab, o, x, *pieces, vectors, w, cot, weight)
-
-
-def feed_back(tab, e2, e2t, h1t, u, gp, w, dz2, hat1, root1, o, pieces, vectors):
-    wo_spec = pl.BlockSpec((1, RP, D), lambda s, t: (3, 0, 0))
-
-    def late(s):
-        return jnp.minimum(s, 3)
-
-    return call(
-        feed_back_kernel,
-        5,
-        [
-            whole(ROWS, D),
-            whole(D, ROWS),
-            whole(D, ROWS),
-            pl.BlockSpec((ROWS, D), lambda s, t: (0, late(s))),
-            pl.BlockSpec((ROWS, D), lambda s, t: (0, late(s))),
-            pl.BlockSpec((RB, 1, 2, RP, D), lambda s, t: (0, late(s), 0, 0, 0)),
-            whole(ROWS, D),
-            whole(ROWS, D),
-            whole(ROWS, 1),
-            whole(ROWS, D),
-            *[wo_spec] * 8,
-            whole(12, D),
-        ],
-        [
-            pl.BlockSpec((RB, 1, 2, RP, D), lambda s, t: (0, s, 0, 0, 0)),
-            whole(ROWS, D),
-            whole(ROWS, D),
-            whole(3, D),
+            whole(6, D),
             whole(4, D),
         ],
         [
+            shape_of((ROWS, D), BF),
             shape_of((RB, 5, 2, RP, D), BF),
             shape_of((ROWS, D), F32),
             shape_of((ROWS, D), BF),
-            shape_of((3, D), F32),
+            shape_of((6, D), F32),
             shape_of((4, D), F32),
         ],
-        [vm((ROWS, D), BF), vm((ROWS, D), F32), vm((D, D), BF), vm((D, ROWS), BF)],
-        24_000_000_000,
+        [
+            vm((D, D), BF),
+            vm((ROWS, D), BF),
+            vm((D, ROWS), BF),
+            vm((ROWS, D), F32),
+            vm((ROWS, 1), F32),
+            vm((ROWS, D), F32),
+            vm((4, ROWS, D), BF),
+            vm((4, ROWS, D), BF),
+            vm((ROWS, D), BF),
+            vm((D, ROWS), BF),
+            vm((ROWS, D), BF),
+        ],
+        40_000_000_000,
         48_000_000,
-        "feed_back",
-    )(tab, e2, e2t, h1t, u, gp, w, dz2, hat1, root1, o, *pieces, vectors)
+        "feed",
+    )(tab, o, x, *pieces, vectors, w, cot, weight)
 
 
 def round_kernel(qkv_ref, proj_ref, up_ref, down_ref, mine_ref, feed_ref):
@@ -884,7 +834,7 @@
     row_weight = valid_row * (1.0 + 2.0 * (1.0 - flag_row) * answer + 4.0 * flag_row * opening)
 
     o, qe, qo, k, v, xt = attend(tab, tokens, nb, mid, pieces, vectors)
-    u, gp, block_out, dz2, e2, e2t, h1t, hat1, root1, sums_two = feed(
+    block_out, feed_dw, dz1, d_o, sums_norm, bias_up_grad = feed(
         tab, o, tokens, pieces, vectors, feed_w, out_cotangent, row_weight[:, None]
     )
 
@@ -895,9 +845,6 @@
         moved = jnp.moveaxis(grad, 0, -3).reshape(*lead, dp_count, part, D)
         return jnp.moveaxis(moved, -3, 0)
 
-    feed_dw, dz1, d_o, sums_one, bias_up_grad = feed_back(
-        tab, e2, e2t, h1t, u, gp, feed_w, dz2, hat1, root1, o, pieces, vectors
-    )
     feed_part = lax.psum_scatter(to_parts(feed_dw), "dp", scatter_dimension=0, tiled=False)
 
     dq, dk, dv, keep, give, sums_head = attend_back(tab, qe, qo, k, v, d_o, o, xt)
@@ -917,7 +864,7 @@
     from_nb = lax.ppermute(to_nb, AXES, swap_z[1])
     from_mid = lax.ppermute(to_mid, AXES, swap_mid)
     dx_own = input_own(tab, dq, dk, dv, pieces, dz1)
-    vector_part = jnp.concatenate([sums_head, sums_one, sums_two, bias_up_grad], 0)
+    vector_part = jnp.concatenate([sums_head, sums_norm, bias_up_grad], 0)
     vec_columns = D // devices
     vector_part = vector_part.reshape(12, devices, vec_columns).transpose(1, 0, 2)
     vector_grad = jnp.sum(lax.all_to_all(vector_part, AXES, 0, 0, tiled=True), 0)

time: 363 us -> 327 us (0.901); the launches traced: 357 us -> 326 us
  Pallas kernels: 183 us -> 146 us
  waiting for transfers between devices: 94.1 us -> 101 us
    pallas_call x2 -> x1, Pallas kernels: 62.4 us -> 44.2 us  [feed(): call(feed_kernel, 9, [whole(ROWS, D), whole(ROWS, D), *[wo_spec] * 8, who...]
    pallas_call x1, Pallas kernels: 54.1 us -> 37.7 us  [attend_back(): call(attend_back_kernel, PAIRS, [columns(ROWS), columns(ROWS), columns(8...]
    reduce_scatter x1, waiting for transfers between devices: 0.02 us -> 11.9 us  [shards(): lax.psum_scatter(to_parts(feed_dw), 'dp', scatter_dimension=0, tiled=False)]
    all_to_all x1, waiting for transfers between devices: 20.8 us -> 15.5 us  [shards(): lax.all_to_all(vector_part, AXES, 0, 0, tiled=True)]
  transfers between devices with their start and end apart: 25 -> 25, of which waited for: 11 -> 13; matrix products, arithmetic and copies ran while one was open for 4% -> 4% of each run, Pallas kernels for 30% -> 27%
where the time goes in v3:
time: 327 us; the launch traced here: 326 us
  Pallas kernels  146 us (45%)
  waiting for transfers between devices  101 us (31%)
  starting transfers between devices  45.7 us (14%)
  between operations  16.2 us (5%)
  other arithmetic  9.21 us (3%)
  local copies, waits for them, and re-layouts  7.95 us (2%)
    pallas_call x1, Pallas kernels, feed(): call(feed_kernel, 9, [whole(ROWS, D), whole(ROWS, D), *[wo_spec] * 8, who...  44.2 us
    pallas_call x1, Pallas kernels, attend_back(): call(attend_back_kernel, PAIRS, [columns(ROWS), columns(ROWS), columns(8...  37.7 us
    pallas_call x1, Pallas kernels, attend(): call(attend_kernel, PAIRS, [whole(ROWS, D), whole(ROWS, D), whole(2 * BLK...  30.2 us
    ppermute x3, waiting for transfers between devices, shards(): lax.ppermute(one, AXES, swap_z[n + 1])  28.9 us
    ppermute x3, waiting for transfers between devices, shards(): lax.ppermute(along_z, AXES, swap_chip[n])  19.6 us
    all_to_all x1, waiting for transfers between devices, shards(): lax.all_to_all(vector_part, AXES, 0, 0, tiled=True)  15.5 us
    reduce_scatter x1, waiting for transfers between devices, shards(): lax.psum_scatter(to_parts(feed_dw), 'dp', scatter_dimension=0, tiled=False)  11.9 us
    ppermute x3, waiting for transfers between devices, shards(): line = [lax.ppermute(mine, AXES, swap_z[n]) for n in range(1, mp_count)]  11.7 us
  transfers between devices with their start and end apart: 25, of which 13 were waited for; matrix products, arithmetic and copies ran while one was open for 4% of the time, Pallas kernels for 27%

profile of v3, /device:TPU:0, one launch (start us, length us, event | category | flops | bytes accessed | tf_op | source)
XLA Modules:
  0.0 326.0 jit_solution(8946066381220906845)
XLA Ops:
  7.2 2.1 round_shards.1
  9.5 3.1 collective-permute-start
  12.5 2.6 collective-permute-start.1
  15.1 3.5 %collective-permute-done.rest_0_ = bf16[96,768]{1,0:T(8,128)(2,1)S(1)} collective-permute-done((bf16[96,768]{1,0:T(8,128)(2,1)}, bf16[96,768]{1,0:T(8,128)(2,1)S(1)}, u32[]{:S(2)}, u32[]{:S(2)}) %collective-permute-start) | collective-permute-done | bytes 147488 | tf_op jit(solution)/shard_map/ppermute | solution.py:801
  18.6 8.2 %collective-permute-done.1.rest_1_ = bf16[96,768]{1,0:T(8,128)(2,1)S(1)} collective-permute-done((bf16[96,768]{1,0:T(8,128)(2,1)}, bf16[96,768]{1,0:T(8,128)(2,1)S(1)}, u32[]{:S(2)}, u32[]{:S(2)}) %collective-permute-start.1) | collective-permute-done | bytes 147488 | tf_op jit(solution)/shard_map/ppermute | solution.py:801
  26.9 1.6 collective-permute-start.4
  28.6 2.3 pack_line.1.refs_0_
  30.9 1.5 collective-permute-start.5
  32.4 1.5 collective-permute-start.6
  34.4 8.9 %collective-permute-start.3 = (bf16[768,768]{1,0:T(8,128)(2,1)S(1)}, bf16[768,768]{1,0:T(8,128)(2,1)S(1)}, u32[]{:S(2)}, u32[]{:S(2)}) collective-permute-start(bf16[768,768]{1,0:T(8,128)(2,1)S(1)} %copy-done.4), channel_id=1, source_target_pairs={{0,1},{1,0},{2,3},{3,2},{4,5},{5,4},{6,7},{7,6},{8,9},{9,8},{10,11... | collective-permute-start | bytes 3538952 | tf_op jit(solution)/shard_map/ppermute | solution.py:805
  43.3 0.7 constant_dynamic-slice_fusion.4
  44.0 0.7 fusion.14
  44.7 0.6 gather_fusion
  45.4 0.7 fusion.15
  46.1 5.0 %collective-permute-done.5.refs_1_ = bf16[4,96,768]{2,1,0:T(8,128)(2,1)} collective-permute-done((bf16[4,96,768]{2,1,0:T(8,128)(2,1)}, bf16[4,96,768]{2,1,0:T(8,128)(2,1)}, u32[]{:S(2)}, u32[]{:S(2)}) %collective-permute-start.5) | collective-permute-done | bytes 589856 | tf_op jit(solution)/shard_map/ppermute | solution.py:807
  51.0 2.9 collective-permute-done.6.refs_2_
  54.0 11.8 %collective-permute-done.7.refs_3_ = bf16[4,96,768]{2,1,0:T(8,128)(2,1)} collective-permute-done((bf16[4,96,768]{2,1,0:T(8,128)(2,1)}, bf16[4,96,768]{2,1,0:T(8,128)(2,1)}, u32[]{:S(2)}, u32[]{:S(2)}) %collective-permute-start.7) | collective-permute-done | bytes 589856 | tf_op jit(solution)/shard_map/ppermute | solution.py:807
  67.0 1.4 fusion.2.refs_11_
  68.8 8.7 %collective-permute-done.3.nb_ref = bf16[768,768]{1,0:T(8,128)(2,1)S(1)} collective-permute-done((bf16[768,768]{1,0:T(8,128)(2,1)S(1)}, bf16[768,768]{1,0:T(8,128)(2,1)S(1)}, u32[]{:S(2)}, u32[]{:S(2)}) %collective-permute-start.3) | collective-permute-done | bytes 1179680 | tf_op jit(solution)/shard_map/ppermute | solution.py:805
  77.5 1.0 copy-done.11
  78.5 30.2 %attend.1 = (bf16[768,768]{1,0:T(8,128)(2,1)}, bf16[768,768]{1,0:T(8,128)(2,1)}, bf16[768,768]{1,0:T(8,128)(2,1)}, bf16[2048,768]{1,0:T(8,128)(2,1)}, bf16[2048,...) custom-call(s32[22]{0:T(128)} %pad_add_fusion.tab, bf16[768,768]{1,0:T(8,128)(2,1)} %x_ref.1, bf16[768,768]{1,0:T(8,128)(2,1)} %copy-done.11, ...), custom_call_target="tpu_custom_call" | custom-call | flops 5000000000 | bytes 16000000 | tf_op jit(solution)/shard_map/attend/pallas_call | solution.py:484
  109.3 44.2 %feed.1 = (bf16[768,768]{1,0:T(8,128)(2,1)}, bf16[8,5,2,96,768]{4,3,2,1,0:T(8,128)(2,1)}, f32[768,768]{1,0:T(8,128)}, bf16[768,768]{1,0:T(8,128)(2,1)}, f32[6,768]{1,0:T(8,128)}, /*index=5*/f32[4,768]{1,0:T(4,128)}) custom-call(s32[22]{0:T(128)} %pad_add_fusion.tab, bf16[768,768]{1,0:T(8,128)(2,1)} %get-tuple-element.101.o_ref, bf16[768,768]{1,0:T(8,128)(2,1)} %x_ref.1, ...), custom_call_target="tpu_custom_call" | custom-call | flops 40000000000 | bytes 48000000 | tf_op jit(solution)/shard_map/feed/pallas_call | solution.py:534
  153.5 37.7 %attend_back.1 = (bf16[768,768]{1,0:T(8,128)(2,1)}, bf16[2048,768]{1,0:T(8,128)(2,1)}, bf16[2048,768]{1,0:T(8,128)(2,1)}, bf16[4,3,96,768]{3,2,1,0:T(8,128)(2,1)...) custom-call(s32[22]{0:T(128)} %pad_add_fusion.tab, bf16[768,768]{1,0:T(8,128)(2,1)} %get-tuple-element.104.qe_ref, ...), custom_call_target="tpu_custom_call" | custom-call | flops 49999998976 | bytes 24000000 | tf_op jit(solution)/shard_map/attend_back/pallas_call | solution.py:499
  191.5 9.3 %input_rest.1 = (bf16[768,768]{1,0:T(8,128)(2,1)}, bf16[512,768]{1,0:T(8,128)(2,1)}) custom-call(s32[22]{0:T(128)} %pad_add_fusion.tab, bf16[2048,768]{1,0:T(8,128)(2,1)} %get-tuple-element.123.dk_ref, bf16[2048,768]{1,0:T(8,128)(2,1)} %get-tuple-element.124.dv_ref, bf16[4,96,768]{2,1,0:T(8,128)(2,1)} %pack_line.1.refs_0_, ...), custom_call_target="tpu_custom_call" | custom-call | flops 8000000000 | bytes 12000000 | tf_op jit(solution)/shard_map/input_rest/pallas_call | solution.py:620
  201.3 1.6 collective-permute-start.13
  203.0 1.8 collective-permute-start.14
  204.8 1.0 slice_bitcast_fusion
  205.8 1.3 collective-permute-start.15
  207.1 1.2 collective-permute-start.16
  208.3 1.0 collective-permute-start.17
  209.6 0.8 reshape.247
  210.4 3.5 %all-to-all-start = ((f32[32,1,288]{2,1,0:T(1,128)}), f32[32,1,288]{2,1,0:T(1,128)S(1)}, u32[]{:S(2)}, u32[]{:S(2)}) async-start(f32[32,1,288]{2,1,0:T(1,128)} %reshape.247), calls=%async_computation | async-start | bytes 98304 | tf_op jit(solution)/shard_map/all_to_all | solution.py:870
  213.9 8.5 %input_own.1 = f32[768,768]{1,0:T(8,128)} custom-call(s32[22]{0:T(128)} %pad_add_fusion.tab, bf16[768,768]{1,0:T(8,128)(2,1)} %get-tuple-element.122.dq_ref, bf16[2048,768]{1,0:T(8,128)(2,1)} %get-tuple-element.123.dk_ref, bf16[2048,768]{1,0:T(8,128)(2,1)} %get-tuple-element.124.dv_ref, bf16[4,96,768]{2,1,0:T(8,128)(2,1)} %pack_line.1.refs_0_, ...), custom_call_target="tpu_custom_call" | custom-call | flops 5000000000 | bytes 12000000 | tf_op jit(solution)/shard_map/input_own/pallas_call | solution.py:639
  222.4 15.5 %all-to-all-done = f32[32,1,288]{2,1,0:T(1,128)S(1)} async-done(((f32[32,1,288]{2,1,0:T(1,128)}), f32[32,1,288]{2,1,0:T(1,128)S(1)}, u32[]{:S(2)}, u32[]{:S(2)}) %all-to-all-start) | async-done | bytes 36896 | tf_op jit(solution)/shard_map/all_to_all | solution.py:870
  238.5 0.8 reduce.1
  240.1 11.9 %reduce-scatter.2.cloned.1.call-done = bf16[1,5,2,96,768]{4,3,2,1,0:T(8,128)(2,1)} async-done(((bf16[8,5,2,96,768]{4,3,2,1,0:T(8,128)(2,1)}), bf16[1,5,2,96,768]{4,3,2,1,0:T(8,128)(2,1)}) %reduce-scatter.2.cloned.1.call-update) | async-done | bytes 1474576 | tf_op jit(solution)/shard_map/reduce_scatter | solution.py:848
  252.0 4.1 %line_parts.1 = (bf16[96,2304]{1,0:T(8,128)(2,1)}, bf16[96,2304]{1,0:T(8,128)(2,1)}, bf16[96,2304]{1,0:T(8,128)(2,1)}, bf16[96,2304]{1,0:T(8,128)(2,1)}) custom-call(s32[1]{0:T(128)} %bitcast.6.tab, bf16[3,96,768]{2,1,0:T(8,128)(2,1)} %get-tuple-element.167.own_ref, bf16[3,96,768]{2,1,0:T(8,128)(2,1)} %collective-permute-done.15.refs_0_, ...), custom_call_target="tpu_custom_call" | custom-call | flops 2000000 | bytes 4000000 | tf_op jit(solution)/shard_map/line_parts/pallas_call | solution.py:654
  256.1 1.5 collective-permute-start.18
  257.6 2.4 collective-permute-start.19
  260.5 1.4 constant_dynamic-slice_fusion.refs_4_
  261.9 15.5 %collective-permute-done.18.refs_1_ = bf16[96,2304]{1,0:T(8,128)(2,1)} collective-permute-done((bf16[96,2304]{1,0:T(8,128)(2,1)}, bf16[96,2304]{1,0:T(8,128)(2,1)}, u32[]{:S(2)}, u32[]{:S(2)}) %collective-permute-start.18) | collective-permute-done | bytes 442400 | tf_op jit(solution)/shard_map/ppermute | solution.py:875
  277.4 13.5 %collective-permute-done.19.refs_2_ = bf16[96,2304]{1,0:T(8,128)(2,1)} collective-permute-done((bf16[96,2304]{1,0:T(8,128)(2,1)}, bf16[96,2304]{1,0:T(8,128)(2,1)}, u32[]{:S(2)}, u32[]{:S(2)}) %collective-permute-start.19) | collective-permute-done | bytes 442400 | tf_op jit(solution)/shard_map/ppermute | solution.py:875
  290.9 2.7 total.1
  293.6 1.3 broadcast_in_dim.5
  294.9 10.4 %all-to-all-start.1 = ((f32[32,1,1]{2,1,0:T(1,128)}), f32[32,1,1]{2,1,0:T(1,128)S(1)}, u32[]{:S(2)}, u32[]{:S(2)}) async-start(f32[32,1,1]{2,1,0:T(1,128)} %broadcast_in_dim.5), calls=%async_computation.2 | async-start | bytes 32768 | tf_op jit(solution)/shard_map/all_to_all | solution.py:883
  305.2 3.2 convert_add_fusion
  308.4 3.9 %all-to-all-done.1 = f32[32,1,1]{2,1,0:T(1,128)S(1)} async-done(((f32[32,1,1]{2,1,0:T(1,128)}), f32[32,1,1]{2,1,0:T(1,128)S(1)}, u32[]{:S(2)}, u32[]{:S(2)}) %all-to-all-start.1) | async-done | bytes 160 | tf_op jit(solution)/shard_map/all_to_all | solution.py:883
  313.7 4.3 %update.1 = (f32[3,96,192]{2,1,0:T(8,128)}, f32[3,96,192]{2,1,0:T(8,128)}, f32[3,96,192]{2,1,0:T(8,128)}, f32[3,96,192]{2,1,0:T(8,128)}, f32[192,96]{1,0:T(8,128...) custom-call(f32[1,1]{1,0:T(1,128)} %bitcast.15.clip_ref, ...), custom_call_target="tpu_custom_call" | custom-call | flops 10000000 | bytes 8000000 | tf_op jit(solution)/shard_map/update/pallas_call | solution.py:699
  (72 shorter events, 6.5 us)
Async XLA Ops:
  7.2 19.7 %copy-start.4 = (bf16[768,768]{1,0:T(8,128)(2,1)S(1)}, bf16[768,768]{1,0:T(8,128)(2,1)}, u32[]{:S(2)}) copy-start(bf16[768,768]{1,0:T(8,128)(2,1)} %x_ref.1) | copy-start | bytes 3538948
  7.2 102.1 %all-gather.3.cloned.1.call-start = ((), (), s32[]{:S(2)}) async-start(), calls=%async_computation.4 | async-start | bytes 9732096 | tf_op jit(solution)/shard_map/all_gather | solution.py:800
  9.4 242.6 %reduce-scatter.2.cloned.1.call-start = ((), (), s32[]{:S(2)}) async-start(), calls=%async_computation.3 | async-start | bytes 13271040 | tf_op jit(solution)/shard_map/reduce_scatter | solution.py:848
  9.5 9.2 %collective-permute-start = (bf16[96,768]{1,0:T(8,128)(2,1)}, bf16[96,768]{1,0:T(8,128)(2,1)S(1)}, u32[]{:S(2)}, u32[]{:S(2)}) collective-permute-start(bf16[96,768]{1,0:T(8,128)(2,1)} %get-tuple-element.95.own_ref), channel_id=1, source_target_pairs={{0,1},{1,0},{2,3},{3,2},{4,5},{5,4},{6,7},{7,6},{8,9},{9,8},{10,11... | collective-permute-start | bytes 442376 | tf_op jit(solution)/shard_map/ppermute | solution.py:801
  12.5 14.3 %collective-permute-start.1 = (bf16[96,768]{1,0:T(8,128)(2,1)}, bf16[96,768]{1,0:T(8,128)(2,1)S(1)}, u32[]{:S(2)}, u32[]{:S(2)}) collective-permute-start(bf16[96,768]{1,0:T(8,128)(2,1)} %get-tuple-element.95.own_ref), channel_id=1, source_target_pairs={{0,2},{1,3},{2,0},{3,1},{4,6},{5,7},{6,4},{7,5},{8,10},{9,11},{10,... | collective-permute-start | bytes 442376 | tf_op jit(solution)/shard_map/ppermute | solution.py:801
  15.1 11.7 %collective-permute-start.2 = (bf16[96,768]{1,0:T(8,128)(2,1)}, bf16[96,768]{1,0:T(8,128)(2,1)S(1)}, u32[]{:S(2)}, u32[]{:S(2)}) collective-permute-start(bf16[96,768]{1,0:T(8,128)(2,1)} %get-tuple-element.95.own_ref), channel_id=1, source_target_pairs={{0,3},{1,2},{2,1},{3,0},{4,7},{5,6},{6,5},{7,4},{8,11},{9,10},{10,... | collective-permute-start | bytes 442376 | tf_op jit(solution)/shard_map/ppermute | solution.py:801
  18.6 9.9 %copy-start.13 = (bf16[96,768]{1,0:T(8,128)(2,1)}, bf16[96,768]{1,0:T(8,128)(2,1)S(1)}, u32[]{:S(2)}) copy-start(bf16[96,768]{1,0:T(8,128)(2,1)S(1)} %collective-permute-done.rest_0_) | copy-start | bytes 442372
  26.9 1.7 copy-start.14
  26.9 1.6 copy-start.15
  26.9 38.8 %collective-permute-start.4 = (bf16[512,768]{1,0:T(8,128)(2,1)S(1)}, bf16[512,768]{1,0:T(8,128)(2,1)}, u32[]{:S(2)}, u32[]{:S(2)}) collective-permute-start(bf16[512,768]{1,0:T(8,128)(2,1)S(1)} %constant_dynamic-slice_fusion.1), channel_id=1, source_target_pairs={{0,0},{1,2},{2,1},{3,3},{4,4},{5,6},{6,5},{7,7},{8,8},{9,10},{10,9... | collective-permute-start | bytes 2359304 | tf_op jit(solution)/shard_map/ppermute | solution.py:806
  28.5 16.2 %copy-start = (s32[3]{0:T(128)S(1)}, s32[3]{0:T(128)}, u32[]{:S(2)}) copy-start(s32[3]{0:T(128)} %param.26) | copy-start | bytes 40
  28.5 38.3 %copy-start.8 = (s32[3]{0:T(128)S(1)}, s32[3]{0:T(128)}, u32[]{:S(2)}) copy-start(s32[3]{0:T(128)} %param.28) | copy-start | bytes 40
  28.5 38.3 %copy-start.9 = (s32[3]{0:T(128)S(1)}, s32[3]{0:T(128)}, u32[]{:S(2)}) copy-start(s32[3]{0:T(128)} %param.27) | copy-start | bytes 40
  28.5 38.3 %copy-start.10 = (s32[3]{0:T(128)S(1)}, s32[3]{0:T(128)}, u32[]{:S(2)}) copy-start(s32[3]{0:T(128)} %param.29) | copy-start | bytes 40
  30.9 20.1 %collective-permute-start.5 = (bf16[4,96,768]{2,1,0:T(8,128)(2,1)}, bf16[4,96,768]{2,1,0:T(8,128)(2,1)}, u32[]{:S(2)}, u32[]{:S(2)}) collective-permute-start(bf16[4,96,768]{2,1,0:T(8,128)(2,1)} %pack_line.1.refs_0_), channel_id=1, source_target_pairs={{0,8},{1,9},{2,10},{3,11},{4,12},{5,13},{6,14},{7,15},{8,0},{9,1},... | collective-permute-start | bytes 1769480 | tf_op jit(solution)/shard_map/ppermute | solution.py:807
  32.4 21.6 %collective-permute-start.6 = (bf16[4,96,768]{2,1,0:T(8,128)(2,1)}, bf16[4,96,768]{2,1,0:T(8,128)(2,1)}, u32[]{:S(2)}, u32[]{:S(2)}) collective-permute-start(bf16[4,96,768]{2,1,0:T(8,128)(2,1)} %pack_line.1.refs_0_), channel_id=1, source_target_pairs={{0,16},{1,17},{2,18},{3,19},{4,20},{5,21},{6,22},{7,23},{8,24},{9,... | collective-permute-start | bytes 1769480 | tf_op jit(solution)/shard_map/ppermute | solution.py:807
  33.9 31.8 %collective-permute-start.7 = (bf16[4,96,768]{2,1,0:T(8,128)(2,1)}, bf16[4,96,768]{2,1,0:T(8,128)(2,1)}, u32[]{:S(2)}, u32[]{:S(2)}) collective-permute-start(bf16[4,96,768]{2,1,0:T(8,128)(2,1)} %pack_line.1.refs_0_), channel_id=1, source_target_pairs={{0,24},{1,25},{2,26},{3,27},{4,28},{5,29},{6,30},{7,31},{8,16},{9,... | collective-permute-start | bytes 1769480 | tf_op jit(solution)/shard_map/ppermute | solution.py:807
  34.4 43.1 %collective-permute-start.3 = (bf16[768,768]{1,0:T(8,128)(2,1)S(1)}, bf16[768,768]{1,0:T(8,128)(2,1)S(1)}, u32[]{:S(2)}, u32[]{:S(2)}) collective-permute-start(bf16[768,768]{1,0:T(8,128)(2,1)S(1)} %copy-done.4), channel_id=1, source_target_pairs={{0,1},{1,0},{2,3},{3,2},{4,5},{5,4},{6,7},{7,6},{8,9},{9,8},{10,11... | collective-permute-start | bytes 3538952 | tf_op jit(solution)/shard_map/ppermute | solution.py:805
  51.0 17.4 %collective-permute-start.9 = (bf16[4,96,768]{2,1,0:T(8,128)(2,1)}, bf16[4,96,768]{2,1,0:T(8,128)(2,1)}, u32[]{:S(2)}, u32[]{:S(2)}) collective-permute-start(bf16[4,96,768]{2,1,0:T(8,128)(2,1)} %collective-permute-done.5.refs_1_), channel_id=1, source_target_pairs={{0,4},{1,5},{2,6},{3,7},{4,0},{5,1},{6,2},{7,3},{8,12},{9,13},{10,... | collective-permute-start | bytes 1769480 | tf_op jit(solution)/shard_map/ppermute | solution.py:809
  54.0 14.5 %collective-permute-start.8 = (bf16[4,96,768]{2,1,0:T(8,128)(2,1)}, bf16[4,96,768]{2,1,0:T(8,128)(2,1)}, u32[]{:S(2)}, u32[]{:S(2)}) collective-permute-start(bf16[4,96,768]{2,1,0:T(8,128)(2,1)} %pack_line.1.refs_0_), channel_id=1, source_target_pairs={{0,4},{1,5},{2,6},{3,7},{4,0},{5,1},{6,2},{7,3},{8,12},{9,13},{10,... | collective-permute-start | bytes 1769480 | tf_op jit(solution)/shard_map/ppermute | solution.py:809
  65.7 3.1 collective-permute-start.10
  65.7 3.1 collective-permute-start.11
  68.8 8.7 %copy-start.12 = (bf16[4,96,768]{2,1,0:T(8,128)(2,1)}, bf16[4,96,768]{2,1,0:T(8,128)(2,1)S(1)}, u32[]{:S(2)}) copy-start(bf16[4,96,768]{2,1,0:T(8,128)(2,1)S(1)} %collective-permute-done.11.refs_7_) | copy-start | bytes 1769476
  77.5 1.0 copy-start.11
  191.2 9.6 %collective-permute-start.12 = (bf16[4,3,96,768]{3,2,1,0:T(8,128)(2,1)}, bf16[4,3,96,768]{3,2,1,0:T(8,128)(2,1)S(1)}, u32[]{:S(2)}, u32[]{:S(2)}) collective-permute-start(bf16[4,3,96,768]{3,2,1,0:T(8,128)(2,1)} %get-tuple-element.111), channel_id=1, source_target_pairs={{0,4},{1,5},{2,6},{3,7},{4,0},{5,1},{6,2},{7,3},{8,12},{9,13},{10,... | collective-permute-start | bytes 5308424 | tf_op jit(solution)/shard_map/ppermute | solution.py:857
  191.5 9.3 %copy-start.2 = (bf16[4,3,96,768]{3,2,1,0:T(8,128)(2,1)S(1)}, bf16[4,3,96,768]{3,2,1,0:T(8,128)(2,1)}, u32[]{:S(2)}) copy-start(bf16[4,3,96,768]{3,2,1,0:T(8,128)(2,1)} %get-tuple-element.110) | copy-start | bytes 5308420
  201.3 8.0 %copy-start.5 = (f32[6,768]{1,0:T(8,128)S(1)}, f32[6,768]{1,0:T(8,128)}, u32[]{:S(2)}) copy-start(f32[6,768]{1,0:T(8,128)} %get-tuple-element.119) | copy-start | bytes 55300
  201.3 8.0 %copy-start.6 = (f32[4,768]{1,0:T(4,128)S(1)}, f32[4,768]{1,0:T(4,128)}, u32[]{:S(2)}) copy-start(f32[4,768]{1,0:T(4,128)} %get-tuple-element.120) | copy-start | bytes 36868
  201.3 8.0 %copy-start.7 = (f32[2,768]{1,0:T(2,128)S(1)}, f32[2,768]{1,0:T(2,128)}, u32[]{:S(2)}) copy-start(f32[2,768]{1,0:T(2,128)} %get-tuple-element.118) | copy-start | bytes 18436
  201.3 38.8 %collective-permute-start.13 = (bf16[768,768]{1,0:T(8,128)(2,1)}, bf16[768,768]{1,0:T(8,128)(2,1)S(1)}, u32[]{:S(2)}, u32[]{:S(2)}) collective-permute-start(bf16[768,768]{1,0:T(8,128)(2,1)} %get-tuple-element.126), channel_id=1, source_target_pairs={{0,1},{1,0},{2,3},{3,2},{4,5},{5,4},{6,7},{7,6},{8,9},{9,8},{10,11... | collective-permute-start | bytes 3538952 | tf_op jit(solution)/shard_map/ppermute | solution.py:864
  203.0 37.1 %collective-permute-start.14 = (bf16[512,768]{1,0:T(8,128)(2,1)}, bf16[512,768]{1,0:T(8,128)(2,1)S(1)}, u32[]{:S(2)}, u32[]{:S(2)}) collective-permute-start(bf16[512,768]{1,0:T(8,128)(2,1)} %get-tuple-element.127), channel_id=1, source_target_pairs={{0,0},{1,2},{2,1},{3,3},{4,4},{5,6},{6,5},{7,7},{8,8},{9,10},{10,9... | collective-permute-start | bytes 2359304 | tf_op jit(solution)/shard_map/ppermute | solution.py:865
  205.8 34.2 %collective-permute-start.15 = (bf16[3,96,768]{2,1,0:T(8,128)(2,1)}, bf16[3,96,768]{2,1,0:T(8,128)(2,1)}, u32[]{:S(2)}, u32[]{:S(2)}) collective-permute-start(bf16[3,96,768]{2,1,0:T(8,128)(2,1)} %get-tuple-element.170), channel_id=1, source_target_pairs={{0,8},{1,9},{2,10},{3,11},{4,12},{5,13},{6,14},{7,15},{8,0},{9,1},... | collective-permute-start | bytes 1327112 | tf_op jit(solution)/shard_map/ppermute | solution.py:863
  207.1 32.9 %collective-permute-start.16 = (bf16[3,96,768]{2,1,0:T(8,128)(2,1)S(1)}, bf16[3,96,768]{2,1,0:T(8,128)(2,1)}, u32[]{:S(2)}, u32[]{:S(2)}) collective-permute-start(bf16[3,96,768]{2,1,0:T(8,128)(2,1)S(1)} %get-tuple-element.169), channel_id=1, source_target_pairs={{0,16},{1,17},{2,18},{3,19},{4,20},{5,21},{6,22},{7,23},{8,24},{9,... | collective-permute-start | bytes 1327112 | tf_op jit(solution)/shard_map/ppermute | solution.py:863
  208.3 31.7 %collective-permute-start.17 = (bf16[3,96,768]{2,1,0:T(8,128)(2,1)S(1)}, bf16[3,96,768]{2,1,0:T(8,128)(2,1)}, u32[]{:S(2)}, u32[]{:S(2)}) collective-permute-start(bf16[3,96,768]{2,1,0:T(8,128)(2,1)S(1)} %get-tuple-element.168), channel_id=1, source_target_pairs={{0,24},{1,25},{2,26},{3,27},{4,28},{5,29},{6,30},{7,31},{8,16},{9,... | collective-permute-start | bytes 1327112 | tf_op jit(solution)/shard_map/ppermute | solution.py:863
  210.4 27.6 %all-to-all-start = ((f32[32,1,288]{2,1,0:T(1,128)}), f32[32,1,288]{2,1,0:T(1,128)S(1)}, u32[]{:S(2)}, u32[]{:S(2)}) async-start(f32[32,1,288]{2,1,0:T(1,128)} %reshape.247), calls=%async_computation | async-start | bytes 98304 | tf_op jit(solution)/shard_map/all_to_all | solution.py:870
  240.1 11.9 %copy-start.3 = (bf16[512,768]{1,0:T(8,128)(2,1)}, bf16[512,768]{1,0:T(8,128)(2,1)S(1)}, u32[]{:S(2)}) copy-start(bf16[512,768]{1,0:T(8,128)(2,1)S(1)} %collective-permute-done.14) | copy-start | bytes 2359300
  252.0 53.3 %copy-start.1 = (f32[768,768]{1,0:T(8,128)S(1)}, f32[768,768]{1,0:T(8,128)}, u32[]{:S(2)}) copy-start(f32[768,768]{1,0:T(8,128)} %input_own.1) | copy-start | bytes 7077892
  256.1 21.2 %collective-permute-start.18 = (bf16[96,2304]{1,0:T(8,128)(2,1)}, bf16[96,2304]{1,0:T(8,128)(2,1)}, u32[]{:S(2)}, u32[]{:S(2)}) collective-permute-start(bf16[96,2304]{1,0:T(8,128)(2,1)} %get-tuple-element.138), channel_id=1, source_target_pairs={{0,1},{1,0},{2,3},{3,2},{4,5},{5,4},{6,7},{7,6},{8,9},{9,8},{10,11... | collective-permute-start | bytes 1327112 | tf_op jit(solution)/shard_map/ppermute | solution.py:875
  257.6 33.2 %collective-permute-start.19 = (bf16[96,2304]{1,0:T(8,128)(2,1)}, bf16[96,2304]{1,0:T(8,128)(2,1)}, u32[]{:S(2)}, u32[]{:S(2)}) collective-permute-start(bf16[96,2304]{1,0:T(8,128)(2,1)} %get-tuple-element.139), channel_id=1, source_target_pairs={{0,2},{1,3},{2,0},{3,1},{4,6},{5,7},{6,4},{7,5},{8,10},{9,11},{10,... | collective-permute-start | bytes 1327112 | tf_op jit(solution)/shard_map/ppermute | solution.py:875
  260.0 30.8 %collective-permute-start.20 = (bf16[96,2304]{1,0:T(8,128)(2,1)}, bf16[96,2304]{1,0:T(8,128)(2,1)}, u32[]{:S(2)}, u32[]{:S(2)}) collective-permute-start(bf16[96,2304]{1,0:T(8,128)(2,1)} %get-tuple-element.140), channel_id=1, source_target_pairs={{0,3},{1,2},{2,1},{3,0},{4,7},{5,6},{6,5},{7,4},{8,11},{9,10},{10,... | collective-permute-start | bytes 1327112 | tf_op jit(solution)/shard_map/ppermute | solution.py:875
  294.9 17.5 %all-to-all-start.1 = ((f32[32,1,1]{2,1,0:T(1,128)}), f32[32,1,1]{2,1,0:T(1,128)S(1)}, u32[]{:S(2)}, u32[]{:S(2)}) async-start(f32[32,1,1]{2,1,0:T(1,128)} %broadcast_in_dim.5), calls=%async_computation.2 | async-start | bytes 32768 | tf_op jit(solution)/shard_map/all_to_all | solution.py:883
Sparse Core Ops, SparseCore 0:
  11.4 97.8 all-gather.2
  153.6 98.3 reduce-scatter.1

commit v4 on v3

--- a/solution.py
+++ b/solution.py
@@ -360,8 +360,8 @@
             z2_s[rows, :] += dot_nt(ep, w1)
             now = later
         db1_ref[pl.ds(m, 1), :] = db1
-        dw_ref[:, 0, 0] = dot_nn(h1t_s[...], ep_s[...]).astype(BF).reshape(RB, RP, D)
-        dw_ref[:, 0, 1] = dot_nn(e2t_s[...], u_s[m]).astype(BF).reshape(RB, RP, D)
+        dw_ref[:, :RP] = dot_nn(h1t_s[...], ep_s[...]).astype(BF).reshape(RB, RP, D)
+        dw_ref[:, RP:] = dot_nn(e2t_s[...], u_s[m]).astype(BF).reshape(RB, RP, D)
 
     @pl.when(step == 8)
     def _():
@@ -379,8 +379,7 @@
             sums[2] += jnp.sum(dh, 0, keepdims=True)
         for n in range(3):
             sums_ref[n : n + 1, :] = sums[n]
-        dw_ref[:, 0, 0] = dot_nn(e2t_s[...], o_ref[...]).astype(BF).reshape(RB, RP, D)
-        dw_ref[:, 0, 1] = jnp.zeros((RB, RP, D), BF)
+        dw_ref[:, :RP] = dot_nn(e2t_s[...], o_ref[...]).astype(BF).reshape(RB, RP, D)
 
 
 def pack_kernel(tab, own_ref, *rest):
@@ -427,25 +426,34 @@
     own_ref[...] = back + dot_nt(dq_ref[...], w_s[:, :D]) + dz1_ref[...]
 
 
-def line_kernel(tab, own_ref, *refs):
-    chips, (feed_ref, *outs) = refs[:-5], refs[-5:]
+def head_line_kernel(z_ref, own_ref, *refs):
+    others, outs = refs[:-4], refs[-4:]
     total = own_ref[...].astype(F32)
-    for ref in chips:
+    for ref in others:
         total = total + ref[...].astype(F32)
     total = total.astype(BF)
-    width = total.shape[-1] // 4
-    for n in range(4):
-        m = n ^ tab[0]
-        outs[n][:, :D] = feed_ref[m, 0]
-        outs[n][:, D : 2 * D] = feed_ref[m, 1]
-        for other in range(4):
-
-            @pl.when(m == other)
+    width = D // 4
+    for m in range(4):
+        at = slice(m * width, (m + 1) * width)
+        mine = jnp.concatenate([total[kind, :, at] for kind in range(3)], 1)
+        for n, ref in enumerate(outs):
+
+            @pl.when((m ^ z_ref[0]) == n)
             def _():
-                at = slice(other * width, (other + 1) * width)
-                for kind in range(3):
-                    outs[n][:, 2 * D + kind * width : 2 * D + (kind + 1) * width] = total[kind, :, at]
-                outs[n][:, 2 * D + 3 * width :] = feed_ref[4, 0, :, at]
+                ref[...] = mine
+
+
+def feed_line_kernel(z_ref, feed_ref, *outs):
+    width = D // 4
+    rows = outs[0].shape[0]
+    for m in range(4):
+        for n, ref in enumerate(outs):
+
+            @pl.when((m ^ z_ref[0]) == n)
+            def _():
+                ref[:, :D] = feed_ref[2 * m * rows : (2 * m + 1) * rows, :]
+                ref[:, D : 2 * D] = feed_ref[(2 * m + 1) * rows : (2 * m + 2) * rows, :]
+                ref[:, 2 * D :] = feed_ref[8 * rows :, m * width : (m + 1) * width]
 
 
 def call(kernel, grid, in_specs, out_specs, out_shape, scratch, flops, bytes_accessed, name):
@@ -545,7 +553,7 @@
         ],
         [
             whole(ROWS, D),
-            pl.BlockSpec((RB, 1, 2, RP, D), lambda s, t: (0, jnp.maximum(s - 4, 0), 0, 0, 0)),
+            pl.BlockSpec((RB, 2 * RP, D), lambda s, t: (0, jnp.maximum(s - 4, 0), 0)),
             whole(ROWS, D),
             whole(ROWS, D),
             whole(6, D),
@@ -553,7 +561,7 @@
         ],
         [
             shape_of((ROWS, D), BF),
-            shape_of((RB, 5, 2, RP, D), BF),
+            shape_of((RB, 9 * RP, D), BF),
             shape_of((ROWS, D), F32),
             shape_of((ROWS, D), BF),
             shape_of((6, D), F32),
@@ -649,19 +657,16 @@
     )(tab, dq, dk, dv, *pieces, dz1)
 
 
-def line_parts(z, own, others, fed):
-    rows = own.shape[1]
-    return call(
-        line_kernel,
-        1,
-        [whole(3, rows, D)] * (1 + len(others)) + [whole(5, 2, rows, D)],
-        [whole(rows, 3 * D)] * 4,
-        [shape_of((rows, 3 * D), BF)] * 4,
-        [],
-        2_000_000,
-        4_000_000,
-        "line_parts",
-    )(z.reshape(1).astype(jnp.int32), own, *others, fed)
+def in_line(kernel, name, rows, width, z, *parts):
+    return pl.pallas_call(
+        kernel,
+        in_specs=[pl.BlockSpec(memory_space=pltpu.SMEM)] + [pl.BlockSpec(memory_space=pltpu.VMEM)] * len(parts),
+        out_specs=[pl.BlockSpec(memory_space=pltpu.VMEM)] * 4,
+        out_shape=[shape_of((rows, width), BF)] * 4,
+        compiler_params=pltpu.CompilerParams(vmem_limit_bytes=VMEM_LIMIT),
+        cost_estimate=pl.CostEstimate(flops=2_000_000, bytes_accessed=4_000_000, transcendentals=0),
+        name=name,
+    )(z.reshape(1).astype(jnp.int32), *parts)
 
 
 def adamw(weight, clipped, first, second, rate, decay):
@@ -673,16 +678,19 @@
     return (clipped, first_new, second_new, updated)
 
 
-def update_kernel(clip_ref, sum_ref, vec_ref, *refs):
-    ins, outs = refs[:15], refs[15:]
-    clip = clip_ref[0, 0]
-    sums = sum_ref[...]
+def update_kernel(squares_ref, head_ref, feed_ref, vec_ref, *refs):
+    ins, norm_ref, outs = refs[:15], refs[15], refs[16:]
+    norm = jnp.sqrt(jnp.sum(squares_ref[...], keepdims=True))
+    norm_ref[...] = norm
+    clip = jnp.minimum(1.0, CLIP_NORM / (norm + 1e-06))
+    head = head_ref[...]
+    fed = feed_ref[...]
     width = D // 4
     grads = (
-        [sums[:, 2 * D + n * width : 2 * D + (n + 1) * width] for n in range(3)],
-        [sums[:, 2 * D + 3 * width :].T],
-        [sums[:, :D]],
-        [sums[:, D : 2 * D]],
+        [head[:, n * width : (n + 1) * width] for n in range(3)],
+        [fed[:, 2 * D :].T],
+        [fed[:, :D]],
+        [fed[:, D : 2 * D]],
         [vec_ref[...]],
     )
     for kind, parts in enumerate(grads):
@@ -694,40 +702,43 @@
                 outs[4 * kind + m][at] = result
 
 
-def update(clip, sums, vec, weights, firsts, seconds):
-    shapes = [shape_of(one.shape, F32) for one in weights for _ in range(4)]
+def update(squares, sums, vec, weights, firsts, seconds):
+    vmem = pl.BlockSpec(memory_space=pltpu.VMEM)
     return pl.pallas_call(
         update_kernel,
-        in_specs=[pl.BlockSpec(memory_space=pltpu.SMEM)] + [pl.BlockSpec(memory_space=pltpu.VMEM)] * 17,
-        out_specs=[pl.BlockSpec(memory_space=pltpu.VMEM)] * 20,
-        out_shape=shapes,
+        in_specs=[vmem] * 19,
+        out_specs=[vmem] * 21,
+        out_shape=[shape_of((1, 1), F32)] + [shape_of(one.shape, F32) for one in weights for _ in range(4)],
         compiler_params=pltpu.CompilerParams(vmem_limit_bytes=VMEM_LIMIT),
         cost_estimate=pl.CostEstimate(flops=10_000_000, bytes_accessed=8_000_000, transcendentals=0),
         name="update",
-    )(clip, sums, vec, *weights, *firsts, *seconds)
+    )(squares, *sums, vec, *weights, *firsts, *seconds)
 
 
 def total_kernel(vec_ref, *refs):
-    parts, (sum_out, square_out) = refs[:4], refs[4:]
-    sums = parts[0][...].astype(F32)
-    for ref in parts[1:]:
-        sums = sums + ref[...].astype(F32)
-    sum_out[...] = sums
     vec = vec_ref[...]
-    square_out[0, 0] = jnp.sum(sums * sums) + jnp.sum(vec * vec)
-
-
-def total(vec, parts):
+    square = jnp.sum(vec * vec, keepdims=True)
+    for n in range(2):
+        sums = refs[4 * n][...].astype(F32)
+        for ref in refs[4 * n + 1 : 4 * n + 4]:
+            sums = sums + ref[...].astype(F32)
+        refs[8 + n][...] = sums
+        square = square + jnp.sum(sums * sums, keepdims=True)
+    refs[10][...] = jnp.broadcast_to(square, refs[10].shape)
+
+
+def total(vec, groups, devices):
     vmem = pl.BlockSpec(memory_space=pltpu.VMEM)
-    return pl.pallas_call(
+    *sums, square = pl.pallas_call(
         total_kernel,
-        in_specs=[vmem] * 5,
-        out_specs=[vmem, pl.BlockSpec(memory_space=pltpu.SMEM)],
-        out_shape=[shape_of(parts[0].shape, F32), shape_of((1, 1), F32)],
+        in_specs=[vmem] * 9,
+        out_specs=[vmem] * 3,
+        out_shape=[shape_of(group[0].shape, F32) for group in groups] + [shape_of((devices, 1), F32)],
         compiler_params=pltpu.CompilerParams(vmem_limit_bytes=VMEM_LIMIT),
         cost_estimate=pl.CostEstimate(flops=2_000_000, bytes_accessed=4_000_000, transcendentals=0),
         name="total",
-    )(vec, *parts)
+    )(vec, *[one for group in groups for one in group])
+    return sums, square
 
 
 def shards(
@@ -845,7 +856,9 @@
         moved = jnp.moveaxis(grad, 0, -3).reshape(*lead, dp_count, part, D)
         return jnp.moveaxis(moved, -3, 0)
 
-    feed_part = lax.psum_scatter(to_parts(feed_dw), "dp", scatter_dimension=0, tiled=False)
+    if part != RP:
+        feed_dw = to_parts(feed_dw.reshape(RB, 9, RP, D)).reshape(dp_count, 9 * part, D)
+    feed_part = lax.psum_scatter(feed_dw, "dp", scatter_dimension=0, tiled=False)
 
     dq, dk, dv, keep, give, sums_head = attend_back(tab, qe, qo, k, v, d_o, o, xt)
     if part != RP:
@@ -868,25 +881,28 @@
     vec_columns = D // devices
     vector_part = vector_part.reshape(12, devices, vec_columns).transpose(1, 0, 2)
     vector_grad = jnp.sum(lax.all_to_all(vector_part, AXES, 0, 0, tiled=True), 0)
-    vector_grad, feed_part, dx_own, from_nb, from_mid, *from_chips = lax.optimization_barrier(
-        (vector_grad, feed_part, dx_own, from_nb, from_mid, *from_chips)
+    vector_grad, dx_own, from_nb, from_mid, *from_chips = lax.optimization_barrier(
+        (vector_grad, dx_own, from_nb, from_mid, *from_chips)
     )
-    line_own, *line_rest = line_parts(z, chip_sum[0], from_chips, feed_part)
-    line_rest = [lax.ppermute(one, AXES, swap_z[n + 1]) for n, one in enumerate(line_rest)]
+
+    def along_line(parts):
+        return [parts[0]] + [lax.ppermute(parts[n], AXES, swap_z[n]) for n in range(1, mp_count)]
+
+    head_line = along_line(in_line(head_line_kernel, "head_line", part, 3 * D // 4, z, chip_sum[0], *from_chips))
+    feed_part, *head_line = lax.optimization_barrier((feed_part, *head_line))
+    feed_line = along_line(in_line(feed_line_kernel, "feed_line", part, 2 * D + D // 4, z, feed_part))
     zero_block = jnp.zeros((BLK, D), BF)
     from_mid = jnp.where(
         z == 1, jnp.concatenate([zero_block, from_mid], 0), jnp.concatenate([from_mid, zero_block], 0)
     )
     input_grad = dx_own + from_nb.astype(F32) + from_mid.astype(F32)
 
-    sums, local_squares = total(vector_grad, [line_own] + line_rest)
-    squares = lax.all_to_all(jnp.broadcast_to(local_squares.reshape(1), (devices,)), AXES, 0, 0, tiled=True)
-    grad_norm = jnp.sqrt(jnp.sum(squares))
-    clip_factor = jnp.minimum(1.0, CLIP_NORM / (grad_norm + 1e-06))
+    sums, square = total(vector_grad, (head_line, feed_line), devices)
+    squares = lax.all_to_all(square, AXES, 0, 0, tiled=True)
     vec_index = dp_index * mp_count + z
     vector_shard = lax.dynamic_slice_in_dim(vectors, vec_index * vec_columns, vec_columns, 1)
-    results = update(
-        clip_factor.reshape(1, 1),
+    grad_norm, *results = update(
+        squares,
         sums,
         vector_grad,
         (qkv_master, proj_master, up_master, down_master.T, vector_shard),
@@ -894,7 +910,7 @@
         (qkv_second, proj_second, up_second, down_second.T, vector_second),
     )
     down_set = [one.T for one in results[12:16]]
-    return (block_out, input_grad, grad_norm, *results[:12], *down_set, *results[16:])
+    return (block_out, input_grad, grad_norm.reshape(()), *results[:12], *down_set, *results[16:])
 
 
 def solution(mesh):

time: 327 us -> 319 us (0.976)
  waiting for transfers between devices: 101 us -> 92.7 us
    reduce_scatter x1, waiting for transfers between devices: 11.9 us -> 0.01 us  [shards(): lax.psum_scatter(feed_dw, 'dp', scatter_dimension=0, tiled=False)]
    ppermute x3 -> x6, starting transfers between devices: 4.39 us -> 8.77 us  [along_line(): lax.ppermute(parts[n], AXES, swap_z[n])]
    ppermute x3 -> x6, waiting for transfers between devices: 28.9 us -> 33.1 us  [along_line(): lax.ppermute(parts[n], AXES, swap_z[n])]
    pallas_call x3 -> x4, Pallas kernels: 11.2 us -> 12.8 us  [the longest x2 5.58 us: in_line(): pl.pallas_call(kernel, in_specs=[pl.BlockSpec(memory_space=pltpu.SMEM)] +...]
  transfers between devices with their start and end apart: 25 -> 28, of which waited for: 13 -> 14; matrix products, arithmetic and copies ran while one was open for 4% -> 4% of each run, Pallas kernels for 27% -> 29%
where the time goes in v4:
time: 319 us; the launch traced here: 318 us
  Pallas kernels  147 us (46%)
  waiting for transfers between devices  92.7 us (29%)
  starting transfers between devices  47.1 us (15%)
  between operations  14.4 us (5%)
  other arithmetic  8.58 us (3%)
  local copies, waits for them, and re-layouts  8.18 us (3%)
    pallas_call x1, Pallas kernels, feed(): call(feed_kernel, 9, [whole(ROWS, D), whole(ROWS, D), *[wo_spec] * 8, who...  43.7 us
    pallas_call x1, Pallas kernels, attend_back(): call(attend_back_kernel, PAIRS, [columns(ROWS), columns(ROWS), columns(8...  37.8 us
    ppermute x6, waiting for transfers between devices, along_line(): lax.ppermute(parts[n], AXES, swap_z[n])  33.1 us
    pallas_call x1, Pallas kernels, attend(): call(attend_kernel, PAIRS, [whole(ROWS, D), whole(ROWS, D), whole(2 * BLK...  30.2 us
    ppermute x3, waiting for transfers between devices, shards(): lax.ppermute(along_z, AXES, swap_chip[n])  19.6 us
    all_to_all x1, waiting for transfers between devices, shards(): lax.all_to_all(vector_part, AXES, 0, 0, tiled=True)  14.7 us
    ppermute x3, waiting for transfers between devices, shards(): line = [lax.ppermute(mine, AXES, swap_z[n]) for n in range(1, mp_count)]  11.7 us
    pallas_call x1, Pallas kernels, input_rest(): call(input_rest_kernel, 5, [each, each] + [w_spec] * 8, [pl.BlockSpec((BL...  9.41 us
  transfers between devices with their start and end apart: 28, of which 14 were waited for; matrix products, arithmetic and copies ran while one was open for 4% of the time, Pallas kernels for 29%

profile of v4, /device:TPU:0, one launch (start us, length us, event | category | flops | bytes accessed | tf_op | source)
XLA Modules:
  0.0 318.3 jit_solution(15330448342525198007)
XLA Ops:
  7.2 2.1 round_shards.1
  9.5 3.1 collective-permute-start
  12.5 2.6 collective-permute-start.1
  15.1 3.5 %collective-permute-done.rest_0_ = bf16[96,768]{1,0:T(8,128)(2,1)S(1)} collective-permute-done((bf16[96,768]{1,0:T(8,128)(2,1)}, bf16[96,768]{1,0:T(8,128)(2,1)S(1)}, u32[]{:S(2)}, u32[]{:S(2)}) %collective-permute-start) | collective-permute-done | bytes 147488 | tf_op jit(solution)/shard_map/ppermute | solution.py:812
  18.6 8.2 %collective-permute-done.1.rest_1_ = bf16[96,768]{1,0:T(8,128)(2,1)S(1)} collective-permute-done((bf16[96,768]{1,0:T(8,128)(2,1)}, bf16[96,768]{1,0:T(8,128)(2,1)S(1)}, u32[]{:S(2)}, u32[]{:S(2)}) %collective-permute-start.1) | collective-permute-done | bytes 147488 | tf_op jit(solution)/shard_map/ppermute | solution.py:812
  26.9 1.5 collective-permute-start.4
  28.5 2.3 pack_line.1.refs_0_
  30.9 1.5 collective-permute-start.5
  32.3 1.5 collective-permute-start.6
  34.3 8.9 %collective-permute-start.3 = (bf16[768,768]{1,0:T(8,128)(2,1)S(1)}, bf16[768,768]{1,0:T(8,128)(2,1)S(1)}, u32[]{:S(2)}, u32[]{:S(2)}) collective-permute-start(bf16[768,768]{1,0:T(8,128)(2,1)S(1)} %copy-done.4), channel_id=1, source_target_pairs={{0,1},{1,0},{2,3},{3,2},{4,5},{5,4},{6,7},{7,6},{8,9},{9,8},{10,11... | collective-permute-start | bytes 3538952 | tf_op jit(solution)/shard_map/ppermute | solution.py:816
  46.0 4.9 %collective-permute-done.5.refs_1_ = bf16[4,96,768]{2,1,0:T(8,128)(2,1)} collective-permute-done((bf16[4,96,768]{2,1,0:T(8,128)(2,1)}, bf16[4,96,768]{2,1,0:T(8,128)(2,1)}, u32[]{:S(2)}, u32[]{:S(2)}) %collective-permute-start.5) | collective-permute-done | bytes 589856 | tf_op jit(solution)/shard_map/ppermute | solution.py:818
  51.0 3.0 collective-permute-done.6.refs_2_
  53.9 11.7 %collective-permute-done.7.refs_3_ = bf16[4,96,768]{2,1,0:T(8,128)(2,1)} collective-permute-done((bf16[4,96,768]{2,1,0:T(8,128)(2,1)}, bf16[4,96,768]{2,1,0:T(8,128)(2,1)}, u32[]{:S(2)}, u32[]{:S(2)}) %collective-permute-start.7) | collective-permute-done | bytes 589856 | tf_op jit(solution)/shard_map/ppermute | solution.py:818
  66.9 1.4 fusion.2.refs_11_
  68.8 8.7 %collective-permute-done.3.nb_ref = bf16[768,768]{1,0:T(8,128)(2,1)S(1)} collective-permute-done((bf16[768,768]{1,0:T(8,128)(2,1)S(1)}, bf16[768,768]{1,0:T(8,128)(2,1)S(1)}, u32[]{:S(2)}, u32[]{:S(2)}) %collective-permute-start.3) | collective-permute-done | bytes 1179680 | tf_op jit(solution)/shard_map/ppermute | solution.py:816
  77.5 1.0 copy-done.12
  78.5 30.2 %attend.1 = (bf16[768,768]{1,0:T(8,128)(2,1)}, bf16[768,768]{1,0:T(8,128)(2,1)}, bf16[768,768]{1,0:T(8,128)(2,1)}, bf16[2048,768]{1,0:T(8,128)(2,1)}, bf16[2048,...) custom-call(s32[22]{0:T(128)} %pad_add_fusion.tab, bf16[768,768]{1,0:T(8,128)(2,1)} %x_ref.1, bf16[768,768]{1,0:T(8,128)(2,1)} %copy-done.12, ...), custom_call_target="tpu_custom_call" | custom-call | flops 5000000000 | bytes 16000000 | tf_op jit(solution)/shard_map/attend/pallas_call | solution.py:492
  109.2 43.7 %feed.1 = (bf16[768,768]{1,0:T(8,128)(2,1)}, bf16[8,864,768]{2,1,0:T(8,128)(2,1)}, f32[768,768]{1,0:T(8,128)}, bf16[768,768]{1,0:T(8,128)(2,1)}, f32[6,768]{1,0:T(8,128)}, /*index=5*/f32[4,768]{1,0:T(4,128)}) custom-call(s32[22]{0:T(128)} %pad_add_fusion.tab, bf16[768,768]{1,0:T(8,128)(2,1)} %get-tuple-element.111.o_ref, bf16[768,768]{1,0:T(8,128)(2,1)} %x_ref.1, ...), custom_call_target="tpu_custom_call" | custom-call | flops 40000000000 | bytes 48000000 | tf_op jit(solution)/shard_map/feed/pallas_call | solution.py:542
  153.0 37.8 %attend_back.1 = (bf16[768,768]{1,0:T(8,128)(2,1)}, bf16[2048,768]{1,0:T(8,128)(2,1)}, bf16[2048,768]{1,0:T(8,128)(2,1)}, bf16[4,3,96,768]{3,2,1,0:T(8,128)(2,1)...) custom-call(s32[22]{0:T(128)} %pad_add_fusion.tab, bf16[768,768]{1,0:T(8,128)(2,1)} %get-tuple-element.114.qe_ref, ...), custom_call_target="tpu_custom_call" | custom-call | flops 49999998976 | bytes 24000000 | tf_op jit(solution)/shard_map/attend_back/pallas_call | solution.py:507
  191.1 9.4 %input_rest.1 = (bf16[768,768]{1,0:T(8,128)(2,1)}, bf16[512,768]{1,0:T(8,128)(2,1)}) custom-call(s32[22]{0:T(128)} %pad_add_fusion.tab, bf16[2048,768]{1,0:T(8,128)(2,1)} %get-tuple-element.132.dk_ref, bf16[2048,768]{1,0:T(8,128)(2,1)} %get-tuple-element.133.dv_ref, bf16[4,96,768]{2,1,0:T(8,128)(2,1)} %pack_line.1.refs_0_, ...), custom_call_target="tpu_custom_call" | custom-call | flops 8000000000 | bytes 12000000 | tf_op jit(solution)/shard_map/input_rest/pallas_call | solution.py:628
  201.0 1.7 collective-permute-start.13
  202.7 1.8 collective-permute-start.14
  204.5 1.1 slice_bitcast_fusion
  205.6 1.2 collective-permute-start.15
  206.8 1.5 collective-permute-start.16
  208.3 0.8 collective-permute-start.17
  209.4 0.8 reshape.246
  210.2 3.6 %all-to-all-start = ((f32[32,1,288]{2,1,0:T(1,128)}), f32[32,1,288]{2,1,0:T(1,128)S(1)}, u32[]{:S(2)}, u32[]{:S(2)}) async-start(f32[32,1,288]{2,1,0:T(1,128)} %reshape.246), calls=%async_computation | async-start | bytes 98304 | tf_op jit(solution)/shard_map/all_to_all | solution.py:883
  213.8 9.0 %input_own.1 = f32[768,768]{1,0:T(8,128)} custom-call(s32[22]{0:T(128)} %pad_add_fusion.tab, bf16[768,768]{1,0:T(8,128)(2,1)} %get-tuple-element.131.dq_ref, bf16[2048,768]{1,0:T(8,128)(2,1)} %get-tuple-element.132.dk_ref, bf16[2048,768]{1,0:T(8,128)(2,1)} %get-tuple-element.133.dv_ref, bf16[4,96,768]{2,1,0:T(8,128)(2,1)} %pack_line.1.refs_0_, ...), custom_call_target="tpu_custom_call" | custom-call | flops 5000000000 | bytes 12000000 | tf_op jit(solution)/shard_map/input_own/pallas_call | solution.py:647
  222.8 14.7 %all-to-all-done = f32[32,1,288]{2,1,0:T(1,128)S(1)} async-done(((f32[32,1,288]{2,1,0:T(1,128)}), f32[32,1,288]{2,1,0:T(1,128)S(1)}, u32[]{:S(2)}, u32[]{:S(2)}) %all-to-all-start) | async-done | bytes 36896 | tf_op jit(solution)/shard_map/all_to_all | solution.py:883
  239.6 0.8 copy-done.3
  240.5 2.9 head_line.1
  243.4 1.6 collective-permute-start.18
  245.0 2.3 collective-permute-start.19
  247.8 2.7 collective-permute-done.18.refs_1_
  250.5 7.2 %collective-permute-done.19.refs_2_ = bf16[96,576]{1,0:T(8,128)(2,1)} collective-permute-done((bf16[96,576]{1,0:T(8,128)(2,1)}, bf16[96,576]{1,0:T(8,128)(2,1)}, u32[]{:S(2)}, u32[]{:S(2)}) %collective-permute-start.19) | collective-permute-done | bytes 110624 | tf_op jit(solution)/shard_map/ppermute | solution.py:889
  257.7 2.7 feed_line.1
  260.4 2.0 collective-permute-start.21
  262.3 0.9 collective-permute-start.22
  263.2 1.6 collective-permute-start.23
  264.7 1.4 constant_dynamic-slice_fusion.refs_4_
  266.1 9.8 %collective-permute-done.21.refs_5_ = bf16[96,1728]{1,0:T(8,128)(2,1)} collective-permute-done((bf16[96,1728]{1,0:T(8,128)(2,1)}, bf16[96,1728]{1,0:T(8,128)(2,1)}, u32[]{:S(2)}, u32[]{:S(2)}) %collective-permute-start.21) | collective-permute-done | bytes 331808 | tf_op jit(solution)/shard_map/ppermute | solution.py:889
  275.9 13.4 %collective-permute-done.22.refs_6_ = bf16[96,1728]{1,0:T(8,128)(2,1)} collective-permute-done((bf16[96,1728]{1,0:T(8,128)(2,1)}, bf16[96,1728]{1,0:T(8,128)(2,1)}, u32[]{:S(2)}, u32[]{:S(2)}) %collective-permute-start.22) | collective-permute-done | bytes 331808 | tf_op jit(solution)/shard_map/ppermute | solution.py:889
  289.3 2.8 total.1
  292.1 7.3 %all-to-all-start.1 = ((f32[32,1,1]{2,1,0:T(1,128)}), f32[32,1,1]{2,1,0:T(1,128)S(1)}, u32[]{:S(2)}, u32[]{:S(2)}) async-start(f32[32,1,1]{2,1,0:T(1,128)} %bitcast.45), calls=%async_computation.2 | async-start | bytes 32768 | tf_op jit(solution)/shard_map/all_to_all | solution.py:901
  299.3 3.2 %convert_add_fusion = f32[768,768]{1,0:T(8,128)} fusion(f32[768,768]{1,0:T(8,128)S(1)} %copy-done.1, bf16[768,768]{1,0:T(8,128)(2,1)S(1)} %collective-permute-done.13, bf16[512,768]{1,0:T(8,128)(2,1)} %copy-done.3, pred[]{:T(512)S(6)} %eq.52), kind=kLoop, calls=%fused_computation.2 | loop fusion | flops 2949120 | bytes 6684673 | tf_op jit(solution)/shard_map/add | solution.py:898
  302.5 3.9 %all-to-all-done.1 = f32[32,1,1]{2,1,0:T(1,128)S(1)} async-done(((f32[32,1,1]{2,1,0:T(1,128)}), f32[32,1,1]{2,1,0:T(1,128)S(1)}, u32[]{:S(2)}, u32[]{:S(2)}) %all-to-all-start.1) | async-done | bytes 160 | tf_op jit(solution)/shard_map/all_to_all | solution.py:901
  307.0 4.5 %update.1 = (f32[1,1]{1,0:T(1,128)}, f32[3,96,192]{2,1,0:T(8,128)}, f32[3,96,192]{2,1,0:T(8,128)}, f32[3,96,192]{2,1,0:T(8,128)}, f32[3,96,192]{2,1,0:T(8,128)},...) custom-call(f32[32,1]{1,0:T(8,128)} %bitcast.44, ...), custom_call_target="tpu_custom_call" | custom-call | flops 10000000 | bytes 8000000 | tf_op jit(solution)/shard_map/update/pallas_call | solution.py:707
  (79 shorter events, 10.0 us)
Async XLA Ops:
  7.2 19.7 %copy-start.4 = (bf16[768,768]{1,0:T(8,128)(2,1)S(1)}, bf16[768,768]{1,0:T(8,128)(2,1)}, u32[]{:S(2)}) copy-start(bf16[768,768]{1,0:T(8,128)(2,1)} %x_ref.1) | copy-start | bytes 3538948
  7.2 102.0 %all-gather.3.cloned.1.call-start = ((), (), s32[]{:S(2)}) async-start(), calls=%async_computation.4 | async-start | bytes 9732096 | tf_op jit(solution)/shard_map/all_gather | solution.py:811
  9.4 248.3 %reduce-scatter.2.cloned.1.call-start = ((), (), s32[]{:S(2)}) async-start(), calls=%async_computation.3 | async-start | bytes 11943936 | tf_op jit(solution)/shard_map/reduce_scatter | solution.py:861
  9.5 9.2 %collective-permute-start = (bf16[96,768]{1,0:T(8,128)(2,1)}, bf16[96,768]{1,0:T(8,128)(2,1)S(1)}, u32[]{:S(2)}, u32[]{:S(2)}) collective-permute-start(bf16[96,768]{1,0:T(8,128)(2,1)} %get-tuple-element.105.own_ref), channel_id=1, source_target_pairs={{0,1},{1,0},{2,3},{3,2},{4,5},{5,4},{6,7},{7,6},{8,9},{9,8},{10,11... | collective-permute-start | bytes 442376 | tf_op jit(solution)/shard_map/ppermute | solution.py:812
  12.5 14.3 %collective-permute-start.1 = (bf16[96,768]{1,0:T(8,128)(2,1)}, bf16[96,768]{1,0:T(8,128)(2,1)S(1)}, u32[]{:S(2)}, u32[]{:S(2)}) collective-permute-start(bf16[96,768]{1,0:T(8,128)(2,1)} %get-tuple-element.105.own_ref), channel_id=1, source_target_pairs={{0,2},{1,3},{2,0},{3,1},{4,6},{5,7},{6,4},{7,5},{8,10},{9,11},{10,... | collective-permute-start | bytes 442376 | tf_op jit(solution)/shard_map/ppermute | solution.py:812
  15.1 11.7 %collective-permute-start.2 = (bf16[96,768]{1,0:T(8,128)(2,1)}, bf16[96,768]{1,0:T(8,128)(2,1)S(1)}, u32[]{:S(2)}, u32[]{:S(2)}) collective-permute-start(bf16[96,768]{1,0:T(8,128)(2,1)} %get-tuple-element.105.own_ref), channel_id=1, source_target_pairs={{0,3},{1,2},{2,1},{3,0},{4,7},{5,6},{6,5},{7,4},{8,11},{9,10},{10,... | collective-permute-start | bytes 442376 | tf_op jit(solution)/shard_map/ppermute | solution.py:812
  18.6 9.9 %copy-start.14 = (bf16[96,768]{1,0:T(8,128)(2,1)}, bf16[96,768]{1,0:T(8,128)(2,1)S(1)}, u32[]{:S(2)}) copy-start(bf16[96,768]{1,0:T(8,128)(2,1)S(1)} %collective-permute-done.rest_0_) | copy-start | bytes 442372
  26.9 1.6 copy-start.15
  26.9 1.6 copy-start.16
  26.9 38.7 %collective-permute-start.4 = (bf16[512,768]{1,0:T(8,128)(2,1)S(1)}, bf16[512,768]{1,0:T(8,128)(2,1)}, u32[]{:S(2)}, u32[]{:S(2)}) collective-permute-start(bf16[512,768]{1,0:T(8,128)(2,1)S(1)} %constant_dynamic-slice_fusion.1), channel_id=1, source_target_pairs={{0,0},{1,2},{2,1},{3,3},{4,4},{5,6},{6,5},{7,7},{8,8},{9,10},{10,9... | collective-permute-start | bytes 2359304 | tf_op jit(solution)/shard_map/ppermute | solution.py:817
  28.5 16.2 %copy-start = (s32[3]{0:T(128)S(1)}, s32[3]{0:T(128)}, u32[]{:S(2)}) copy-start(s32[3]{0:T(128)} %param.26) | copy-start | bytes 40
  28.5 38.3 %copy-start.9 = (s32[3]{0:T(128)S(1)}, s32[3]{0:T(128)}, u32[]{:S(2)}) copy-start(s32[3]{0:T(128)} %param.28) | copy-start | bytes 40
  28.5 38.3 %copy-start.10 = (s32[3]{0:T(128)S(1)}, s32[3]{0:T(128)}, u32[]{:S(2)}) copy-start(s32[3]{0:T(128)} %param.27) | copy-start | bytes 40
  28.5 38.3 %copy-start.11 = (s32[3]{0:T(128)S(1)}, s32[3]{0:T(128)}, u32[]{:S(2)}) copy-start(s32[3]{0:T(128)} %param.29) | copy-start | bytes 40
  30.9 20.1 %collective-permute-start.5 = (bf16[4,96,768]{2,1,0:T(8,128)(2,1)}, bf16[4,96,768]{2,1,0:T(8,128)(2,1)}, u32[]{:S(2)}, u32[]{:S(2)}) collective-permute-start(bf16[4,96,768]{2,1,0:T(8,128)(2,1)} %pack_line.1.refs_0_), channel_id=1, source_target_pairs={{0,8},{1,9},{2,10},{3,11},{4,12},{5,13},{6,14},{7,15},{8,0},{9,1},... | collective-permute-start | bytes 1769480 | tf_op jit(solution)/shard_map/ppermute | solution.py:818
  32.3 21.6 %collective-permute-start.6 = (bf16[4,96,768]{2,1,0:T(8,128)(2,1)}, bf16[4,96,768]{2,1,0:T(8,128)(2,1)}, u32[]{:S(2)}, u32[]{:S(2)}) collective-permute-start(bf16[4,96,768]{2,1,0:T(8,128)(2,1)} %pack_line.1.refs_0_), channel_id=1, source_target_pairs={{0,16},{1,17},{2,18},{3,19},{4,20},{5,21},{6,22},{7,23},{8,24},{9,... | collective-permute-start | bytes 1769480 | tf_op jit(solution)/shard_map/ppermute | solution.py:818
  33.9 31.8 %collective-permute-start.7 = (bf16[4,96,768]{2,1,0:T(8,128)(2,1)}, bf16[4,96,768]{2,1,0:T(8,128)(2,1)}, u32[]{:S(2)}, u32[]{:S(2)}) collective-permute-start(bf16[4,96,768]{2,1,0:T(8,128)(2,1)} %pack_line.1.refs_0_), channel_id=1, source_target_pairs={{0,24},{1,25},{2,26},{3,27},{4,28},{5,29},{6,30},{7,31},{8,16},{9,... | collective-permute-start | bytes 1769480 | tf_op jit(solution)/shard_map/ppermute | solution.py:818
  34.3 43.1 %collective-permute-start.3 = (bf16[768,768]{1,0:T(8,128)(2,1)S(1)}, bf16[768,768]{1,0:T(8,128)(2,1)S(1)}, u32[]{:S(2)}, u32[]{:S(2)}) collective-permute-start(bf16[768,768]{1,0:T(8,128)(2,1)S(1)} %copy-done.4), channel_id=1, source_target_pairs={{0,1},{1,0},{2,3},{3,2},{4,5},{5,4},{6,7},{7,6},{8,9},{9,8},{10,11... | collective-permute-start | bytes 3538952 | tf_op jit(solution)/shard_map/ppermute | solution.py:816
  51.0 17.4 %collective-permute-start.9 = (bf16[4,96,768]{2,1,0:T(8,128)(2,1)}, bf16[4,96,768]{2,1,0:T(8,128)(2,1)}, u32[]{:S(2)}, u32[]{:S(2)}) collective-permute-start(bf16[4,96,768]{2,1,0:T(8,128)(2,1)} %collective-permute-done.5.refs_1_), channel_id=1, source_target_pairs={{0,4},{1,5},{2,6},{3,7},{4,0},{5,1},{6,2},{7,3},{8,12},{9,13},{10,... | collective-permute-start | bytes 1769480 | tf_op jit(solution)/shard_map/ppermute | solution.py:820
  53.9 14.4 %collective-permute-start.8 = (bf16[4,96,768]{2,1,0:T(8,128)(2,1)}, bf16[4,96,768]{2,1,0:T(8,128)(2,1)}, u32[]{:S(2)}, u32[]{:S(2)}) collective-permute-start(bf16[4,96,768]{2,1,0:T(8,128)(2,1)} %pack_line.1.refs_0_), channel_id=1, source_target_pairs={{0,4},{1,5},{2,6},{3,7},{4,0},{5,1},{6,2},{7,3},{8,12},{9,13},{10,... | collective-permute-start | bytes 1769480 | tf_op jit(solution)/shard_map/ppermute | solution.py:820
  65.7 3.1 collective-permute-start.10
  65.7 3.1 collective-permute-start.11
  68.8 8.7 %copy-start.13 = (bf16[4,96,768]{2,1,0:T(8,128)(2,1)}, bf16[4,96,768]{2,1,0:T(8,128)(2,1)S(1)}, u32[]{:S(2)}) copy-start(bf16[4,96,768]{2,1,0:T(8,128)(2,1)S(1)} %collective-permute-done.11.refs_7_) | copy-start | bytes 1769476
  77.5 1.0 copy-start.12
  190.7 9.8 %collective-permute-start.12 = (bf16[4,3,96,768]{3,2,1,0:T(8,128)(2,1)}, bf16[4,3,96,768]{3,2,1,0:T(8,128)(2,1)S(1)}, u32[]{:S(2)}, u32[]{:S(2)}) collective-permute-start(bf16[4,3,96,768]{3,2,1,0:T(8,128)(2,1)} %get-tuple-element.121), channel_id=1, source_target_pairs={{0,4},{1,5},{2,6},{3,7},{4,0},{5,1},{6,2},{7,3},{8,12},{9,13},{10,... | collective-permute-start | bytes 5308424 | tf_op jit(solution)/shard_map/ppermute | solution.py:870
  191.1 9.4 %copy-start.2 = (bf16[4,3,96,768]{3,2,1,0:T(8,128)(2,1)S(1)}, bf16[4,3,96,768]{3,2,1,0:T(8,128)(2,1)}, u32[]{:S(2)}) copy-start(bf16[4,3,96,768]{3,2,1,0:T(8,128)(2,1)} %get-tuple-element.120) | copy-start | bytes 5308420
  201.0 8.1 %copy-start.6 = (f32[6,768]{1,0:T(8,128)S(1)}, f32[6,768]{1,0:T(8,128)}, u32[]{:S(2)}) copy-start(f32[6,768]{1,0:T(8,128)} %get-tuple-element.129) | copy-start | bytes 55300
  201.0 8.1 %copy-start.7 = (f32[4,768]{1,0:T(4,128)S(1)}, f32[4,768]{1,0:T(4,128)}, u32[]{:S(2)}) copy-start(f32[4,768]{1,0:T(4,128)} %get-tuple-element.130) | copy-start | bytes 36868
  201.0 8.1 %copy-start.8 = (f32[2,768]{1,0:T(2,128)S(1)}, f32[2,768]{1,0:T(2,128)}, u32[]{:S(2)}) copy-start(f32[2,768]{1,0:T(2,128)} %get-tuple-element.128) | copy-start | bytes 18436
  201.0 38.6 %collective-permute-start.13 = (bf16[768,768]{1,0:T(8,128)(2,1)}, bf16[768,768]{1,0:T(8,128)(2,1)S(1)}, u32[]{:S(2)}, u32[]{:S(2)}) collective-permute-start(bf16[768,768]{1,0:T(8,128)(2,1)} %get-tuple-element.135), channel_id=1, source_target_pairs={{0,1},{1,0},{2,3},{3,2},{4,5},{5,4},{6,7},{7,6},{8,9},{9,8},{10,11... | collective-permute-start | bytes 3538952 | tf_op jit(solution)/shard_map/ppermute | solution.py:877
  202.7 36.9 %collective-permute-start.14 = (bf16[512,768]{1,0:T(8,128)(2,1)}, bf16[512,768]{1,0:T(8,128)(2,1)S(1)}, u32[]{:S(2)}, u32[]{:S(2)}) collective-permute-start(bf16[512,768]{1,0:T(8,128)(2,1)} %get-tuple-element.136), channel_id=1, source_target_pairs={{0,0},{1,2},{2,1},{3,3},{4,4},{5,6},{6,5},{7,7},{8,8},{9,10},{10,9... | collective-permute-start | bytes 2359304 | tf_op jit(solution)/shard_map/ppermute | solution.py:878
  205.6 34.0 %collective-permute-start.15 = (bf16[3,96,768]{2,1,0:T(8,128)(2,1)}, bf16[3,96,768]{2,1,0:T(8,128)(2,1)}, u32[]{:S(2)}, u32[]{:S(2)}) collective-permute-start(bf16[3,96,768]{2,1,0:T(8,128)(2,1)} %get-tuple-element.190), channel_id=1, source_target_pairs={{0,8},{1,9},{2,10},{3,11},{4,12},{5,13},{6,14},{7,15},{8,0},{9,1},... | collective-permute-start | bytes 1327112 | tf_op jit(solution)/shard_map/ppermute | solution.py:876
  206.8 32.7 %collective-permute-start.16 = (bf16[3,96,768]{2,1,0:T(8,128)(2,1)S(1)}, bf16[3,96,768]{2,1,0:T(8,128)(2,1)}, u32[]{:S(2)}, u32[]{:S(2)}) collective-permute-start(bf16[3,96,768]{2,1,0:T(8,128)(2,1)S(1)} %get-tuple-element.189), channel_id=1, source_target_pairs={{0,16},{1,17},{2,18},{3,19},{4,20},{5,21},{6,22},{7,23},{8,24},{9,... | collective-permute-start | bytes 1327112 | tf_op jit(solution)/shard_map/ppermute | solution.py:876
  208.3 31.3 %collective-permute-start.17 = (bf16[3,96,768]{2,1,0:T(8,128)(2,1)S(1)}, bf16[3,96,768]{2,1,0:T(8,128)(2,1)}, u32[]{:S(2)}, u32[]{:S(2)}) collective-permute-start(bf16[3,96,768]{2,1,0:T(8,128)(2,1)S(1)} %get-tuple-element.188), channel_id=1, source_target_pairs={{0,24},{1,25},{2,26},{3,27},{4,28},{5,29},{6,30},{7,31},{8,16},{9,... | collective-permute-start | bytes 1327112 | tf_op jit(solution)/shard_map/ppermute | solution.py:876
  210.2 27.3 %all-to-all-start = ((f32[32,1,288]{2,1,0:T(1,128)}), f32[32,1,288]{2,1,0:T(1,128)S(1)}, u32[]{:S(2)}, u32[]{:S(2)}) async-start(f32[32,1,288]{2,1,0:T(1,128)} %reshape.246), calls=%async_computation | async-start | bytes 98304 | tf_op jit(solution)/shard_map/all_to_all | solution.py:883
  239.6 0.9 copy-start.3
  243.4 55.9 %copy-start.1 = (f32[768,768]{1,0:T(8,128)S(1)}, f32[768,768]{1,0:T(8,128)}, u32[]{:S(2)}) copy-start(f32[768,768]{1,0:T(8,128)} %input_own.1) | copy-start | bytes 7077892
  243.4 7.1 %collective-permute-start.18 = (bf16[96,576]{1,0:T(8,128)(2,1)}, bf16[96,576]{1,0:T(8,128)(2,1)}, u32[]{:S(2)}, u32[]{:S(2)}) collective-permute-start(bf16[96,576]{1,0:T(8,128)(2,1)} %get-tuple-element.147), channel_id=1, source_target_pairs={{0,1},{1,0},{2,3},{3,2},{4,5},{5,4},{6,7},{7,6},{8,9},{9,8},{10,11... | collective-permute-start | bytes 331784 | tf_op jit(solution)/shard_map/ppermute | solution.py:889
  245.0 12.7 %collective-permute-start.19 = (bf16[96,576]{1,0:T(8,128)(2,1)}, bf16[96,576]{1,0:T(8,128)(2,1)}, u32[]{:S(2)}, u32[]{:S(2)}) collective-permute-start(bf16[96,576]{1,0:T(8,128)(2,1)} %get-tuple-element.148), channel_id=1, source_target_pairs={{0,2},{1,3},{2,0},{3,1},{4,6},{5,7},{6,4},{7,5},{8,10},{9,11},{10,... | collective-permute-start | bytes 331784 | tf_op jit(solution)/shard_map/ppermute | solution.py:889
  247.2 10.4 %collective-permute-start.20 = (bf16[96,576]{1,0:T(8,128)(2,1)}, bf16[96,576]{1,0:T(8,128)(2,1)}, u32[]{:S(2)}, u32[]{:S(2)}) collective-permute-start(bf16[96,576]{1,0:T(8,128)(2,1)} %get-tuple-element.149), channel_id=1, source_target_pairs={{0,3},{1,2},{2,1},{3,0},{4,7},{5,6},{6,5},{7,4},{8,11},{9,10},{10,... | collective-permute-start | bytes 331784 | tf_op jit(solution)/shard_map/ppermute | solution.py:889
  260.4 15.5 %collective-permute-start.21 = (bf16[96,1728]{1,0:T(8,128)(2,1)}, bf16[96,1728]{1,0:T(8,128)(2,1)}, u32[]{:S(2)}, u32[]{:S(2)}) collective-permute-start(bf16[96,1728]{1,0:T(8,128)(2,1)} %get-tuple-element.156), channel_id=1, source_target_pairs={{0,1},{1,0},{2,3},{3,2},{4,5},{5,4},{6,7},{7,6},{8,9},{9,8},{10,11... | collective-permute-start | bytes 995336 | tf_op jit(solution)/shard_map/ppermute | solution.py:889
  262.3 27.0 %collective-permute-start.22 = (bf16[96,1728]{1,0:T(8,128)(2,1)}, bf16[96,1728]{1,0:T(8,128)(2,1)}, u32[]{:S(2)}, u32[]{:S(2)}) collective-permute-start(bf16[96,1728]{1,0:T(8,128)(2,1)} %get-tuple-element.157), channel_id=1, source_target_pairs={{0,2},{1,3},{2,0},{3,1},{4,6},{5,7},{6,4},{7,5},{8,10},{9,11},{10,... | collective-permute-start | bytes 995336 | tf_op jit(solution)/shard_map/ppermute | solution.py:889
  263.2 26.1 %collective-permute-start.23 = (bf16[96,1728]{1,0:T(8,128)(2,1)}, bf16[96,1728]{1,0:T(8,128)(2,1)}, u32[]{:S(2)}, u32[]{:S(2)}) collective-permute-start(bf16[96,1728]{1,0:T(8,128)(2,1)} %get-tuple-element.158), channel_id=1, source_target_pairs={{0,3},{1,2},{2,1},{3,0},{4,7},{5,6},{6,5},{7,4},{8,11},{9,10},{10,... | collective-permute-start | bytes 995336 | tf_op jit(solution)/shard_map/ppermute | solution.py:889
  292.1 14.4 %all-to-all-start.1 = ((f32[32,1,1]{2,1,0:T(1,128)}), f32[32,1,1]{2,1,0:T(1,128)S(1)}, u32[]{:S(2)}, u32[]{:S(2)}) async-start(f32[32,1,1]{2,1,0:T(1,128)} %bitcast.45), calls=%async_computation.2 | async-start | bytes 32768 | tf_op jit(solution)/shard_map/all_to_all | solution.py:901
  306.4 0.6 copy-start.5
Sparse Core Ops, SparseCore 0:
  11.4 97.7 all-gather.2
  153.1 92.5 reduce-scatter.1

commit v5 on v4

--- a/solution.py
+++ b/solution.py
@@ -31,6 +31,7 @@
 AXES = ("dp", "mp")
 BLK = 256
 ROWS = 768
+HALF = ROWS // 2
 PAIRS = HEADS // 2
 RB = 8
 RP = D // RB
@@ -296,7 +297,7 @@
     vec_ref, w_ref, cot_ref, weight_ref, out_ref, dw_ref, dz1_ref, do_ref, sums_ref, db1_ref = refs[8:18]
     wo_s, h1b_s, h1t_s, hat1_s, root1_s, z2_s, u_s, gp_s, e2_s, e2t_s, ep_s = refs[18:]
     step = pl.program_id(0)
-    blocks = [slice(i * BLK, (i + 1) * BLK) for i in range(3)]
+    blocks = [slice(i * HALF, (i + 1) * HALF) for i in range(2)]
 
     @pl.when(step == 0)
     def _():
@@ -317,15 +318,15 @@
         w1 = w_ref[:, 0, 0].reshape(D, D)
         w2t = w_ref[:, 0, 1].reshape(D, D)
         bias = vec_ref[pl.ds(8 + step, 1), :]
-        now = dot_nn(h1b_s[:BLK, :], w1)
+        now = dot_nn(h1b_s[:HALF, :], w1)
         for i, rows in enumerate(blocks):
-            later = dot_nn(h1b_s[blocks[i + 1], :], w1) if i < 2 else None
+            later = dot_nn(h1b_s[blocks[1], :], w1) if i == 0 else None
             act, slope = gelu_both(now + bias)
             act = act.astype(BF)
             u_s[step, rows, :] = act
             gp_s[step, rows, :] = slope.astype(BF)
-            z2_s[rows, :] += dot_nt(act, w2t)
             now = later
+        z2_s[...] += dot_nt(u_s[step], w2t)
 
     @pl.when(step == 3)
     def _():
@@ -351,9 +352,9 @@
         w1 = w_ref[:, 0, 0].reshape(D, D)
         w2t = w_ref[:, 0, 1].reshape(D, D)
         db1 = jnp.zeros((1, D), F32)
-        now = dot_nn(e2_s[:BLK, :], w2t)
+        now = dot_nn(e2_s[:HALF, :], w2t)
         for i, rows in enumerate(blocks):
-            later = dot_nn(e2_s[blocks[i + 1], :], w2t) if i < 2 else None
+            later = dot_nn(e2_s[blocks[1], :], w2t) if i == 0 else None
             ep = (gp_s[m, rows, :].astype(F32) * now).astype(BF)
             ep_s[rows, :] = ep
             db1 += jnp.sum(ep.astype(F32), 0, keepdims=True)
@@ -716,7 +717,8 @@
 
 
 def total_kernel(vec_ref, *refs):
-    vec = vec_ref[...]
+    vec = jnp.sum(vec_ref[...], 0, keepdims=True)
+    refs[10][...] = vec
     square = jnp.sum(vec * vec, keepdims=True)
     for n in range(2):
         sums = refs[4 * n][...].astype(F32)
@@ -724,21 +726,22 @@
             sums = sums + ref[...].astype(F32)
         refs[8 + n][...] = sums
         square = square + jnp.sum(sums * sums, keepdims=True)
-    refs[10][...] = jnp.broadcast_to(square, refs[10].shape)
+    refs[11][...] = jnp.broadcast_to(square, refs[11].shape)
 
 
 def total(vec, groups, devices):
     vmem = pl.BlockSpec(memory_space=pltpu.VMEM)
-    *sums, square = pl.pallas_call(
+    *sums, vec_sum, square = pl.pallas_call(
         total_kernel,
         in_specs=[vmem] * 9,
-        out_specs=[vmem] * 3,
-        out_shape=[shape_of(group[0].shape, F32) for group in groups] + [shape_of((devices, 1), F32)],
+        out_specs=[vmem] * 4,
+        out_shape=[shape_of(group[0].shape, F32) for group in groups]
+        + [shape_of((1, vec.shape[1]), F32), shape_of((devices, 1), F32)],
         compiler_params=pltpu.CompilerParams(vmem_limit_bytes=VMEM_LIMIT),
         cost_estimate=pl.CostEstimate(flops=2_000_000, bytes_accessed=4_000_000, transcendentals=0),
         name="total",
     )(vec, *[one for group in groups for one in group])
-    return sums, square
+    return sums, vec_sum, square
 
 
 def shards(
@@ -816,7 +819,7 @@
     nb = lax.ppermute(tokens_late, AXES, swap_z[1])
     mid = lax.ppermute(lax.dynamic_slice_in_dim(tokens_late, mid_at, 2 * BLK, 0), AXES, swap_mid)
     same = [along_z] + [lax.ppermute(along_z, AXES, swap_chip[n]) for n in range(1, chips)]
-    first, same[1] = lax.optimization_barrier((along_z, same[1]))
+    first, same[1], nb = lax.optimization_barrier((along_z, same[1], nb))
     other = [lax.ppermute(one, AXES, swap_core) for one in [first] + same[1:]]
     pieces = same + other
     kernel_core, kernel_chip = core, chip_index
@@ -879,10 +882,10 @@
     dx_own = input_own(tab, dq, dk, dv, pieces, dz1)
     vector_part = jnp.concatenate([sums_head, sums_norm, bias_up_grad], 0)
     vec_columns = D // devices
-    vector_part = vector_part.reshape(12, devices, vec_columns).transpose(1, 0, 2)
-    vector_grad = jnp.sum(lax.all_to_all(vector_part, AXES, 0, 0, tiled=True), 0)
-    vector_grad, dx_own, from_nb, from_mid, *from_chips = lax.optimization_barrier(
-        (vector_grad, dx_own, from_nb, from_mid, *from_chips)
+    vector_part = vector_part.reshape(12, devices, vec_columns).transpose(1, 0, 2).reshape(devices, 12 * vec_columns)
+    vector_parts = lax.all_to_all(vector_part, AXES, 0, 0, tiled=True)
+    vector_parts, dx_own, from_nb, from_mid, *from_chips = lax.optimization_barrier(
+        (vector_parts, dx_own, from_nb, from_mid, *from_chips)
     )
 
     def along_line(parts):
@@ -897,7 +900,8 @@
     )
     input_grad = dx_own + from_nb.astype(F32) + from_mid.astype(F32)
 
-    sums, square = total(vector_grad, (head_line, feed_line), devices)
+    sums, vector_grad, square = total(vector_parts, (head_line, feed_line), devices)
+    vector_grad = vector_grad.reshape(12, vec_columns)
     squares = lax.all_to_all(square, AXES, 0, 0, tiled=True)
     vec_index = dp_index * mp_count + z
     vector_shard = lax.dynamic_slice_in_dim(vectors, vec_index * vec_columns, vec_columns, 1)

time: 319 us -> 317 us (level)
  starting transfers between devices: 47.1 us -> 43.4 us
  waiting for transfers between devices: 92.7 us -> 95.9 us
    ppermute x3, waiting for transfers between devices: 19.6 us -> 26.8 us  [shards(): lax.ppermute(along_z, AXES, swap_chip[n])]
    ppermute x1, waiting for transfers between devices: 8.68 us -> 3 us  [shards(): nb = lax.ppermute(tokens_late, AXES, swap_z[1])]
  transfers between devices with their start and end apart: 28 -> 28, of which waited for: 14 -> 13; matrix products, arithmetic and copies ran while one was open for 4% -> 4% of each run, Pallas kernels for 29% -> 29%
where the time goes in v5:
time: 317 us; the launch traced here: 316 us
  Pallas kernels  147 us (46%)
  waiting for transfers between devices  95.9 us (30%)
  starting transfers between devices  43.4 us (14%)
  between operations  14.3 us (5%)
  local copies, waits for them, and re-layouts  8.06 us (3%)
  other arithmetic  7.87 us (2%)
    pallas_call x1, Pallas kernels, feed(): call(feed_kernel, 9, [whole(ROWS, D), whole(ROWS, D), *[wo_spec] * 8, who...  42.9 us
    pallas_call x1, Pallas kernels, attend_back(): call(attend_back_kernel, PAIRS, [columns(ROWS), columns(ROWS), columns(8...  37.8 us
    ppermute x6, waiting for transfers between devices, along_line(): lax.ppermute(parts[n], AXES, swap_z[n])  32.9 us
    pallas_call x1, Pallas kernels, attend(): call(attend_kernel, PAIRS, [whole(ROWS, D), whole(ROWS, D), whole(2 * BLK...  30.6 us
    ppermute x3, waiting for transfers between devices, shards(): lax.ppermute(along_z, AXES, swap_chip[n])  26.8 us
    all_to_all x1, waiting for transfers between devices, shards(): vector_parts = lax.all_to_all(vector_part, AXES, 0, 0, tiled=True)  15.8 us
    ppermute x3, waiting for transfers between devices, shards(): line = [lax.ppermute(mine, AXES, swap_z[n]) for n in range(1, mp_count)]  11.6 us
    pallas_call x1, Pallas kernels, input_rest(): call(input_rest_kernel, 5, [each, each] + [w_spec] * 8, [pl.BlockSpec((BL...  9.48 us
  transfers between devices with their start and end apart: 28, of which 13 were waited for; matrix products, arithmetic and copies ran while one was open for 4% of the time, Pallas kernels for 29%

profile of v5, /device:TPU:0, one launch (start us, length us, event | category | flops | bytes accessed | tf_op | source)
XLA Modules:
  0.0 316.2 jit_solution(9043220720142620617)
XLA Ops:
  7.2 2.1 round_shards.1
  9.4 3.1 collective-permute-start
  12.5 2.6 collective-permute-start.1
  15.1 3.5 %collective-permute-done.rest_0_ = bf16[96,768]{1,0:T(8,128)(2,1)S(1)} collective-permute-done((bf16[96,768]{1,0:T(8,128)(2,1)}, bf16[96,768]{1,0:T(8,128)(2,1)S(1)}, u32[]{:S(2)}, u32[]{:S(2)}) %collective-permute-start) | collective-permute-done | bytes 147488 | tf_op jit(solution)/shard_map/ppermute | solution.py:815
  18.5 8.1 %collective-permute-done.1.rest_1_ = bf16[96,768]{1,0:T(8,128)(2,1)S(1)} collective-permute-done((bf16[96,768]{1,0:T(8,128)(2,1)}, bf16[96,768]{1,0:T(8,128)(2,1)S(1)}, u32[]{:S(2)}, u32[]{:S(2)}) %collective-permute-start.1) | collective-permute-done | bytes 147488 | tf_op jit(solution)/shard_map/ppermute | solution.py:815
  26.7 5.8 %collective-permute-start.4 = (bf16[768,768]{1,0:T(8,128)(2,1)}, bf16[768,768]{1,0:T(8,128)(2,1)S(1)}, u32[]{:S(2)}, u32[]{:S(2)}) collective-permute-start(bf16[768,768]{1,0:T(8,128)(2,1)} %x_ref.1), channel_id=1, source_target_pairs={{0,1},{1,0},{2,3},{3,2},{4,5},{5,4},{6,7},{7,6},{8,9},{9,8},{10,11... | collective-permute-start | bytes 3538952 | tf_op jit(solution)/shard_map/ppermute | solution.py:819
  32.5 2.4 pack_line.1.refs_0_
  34.9 1.6 collective-permute-start.3
  36.5 1.6 collective-permute-start.6
  40.6 0.7 collective-permute-start.5
  41.3 0.7 constant_dynamic-slice_fusion.4
  42.1 13.9 %collective-permute-done.6.refs_2_ = bf16[4,96,768]{2,1,0:T(8,128)(2,1)} collective-permute-done((bf16[4,96,768]{2,1,0:T(8,128)(2,1)}, bf16[4,96,768]{2,1,0:T(8,128)(2,1)}, u32[]{:S(2)}, u32[]{:S(2)}) %collective-permute-start.6) | collective-permute-done | bytes 589856 | tf_op jit(solution)/shard_map/ppermute | solution.py:821
  56.1 12.9 %collective-permute-done.7.refs_3_ = bf16[4,96,768]{2,1,0:T(8,128)(2,1)} collective-permute-done((bf16[4,96,768]{2,1,0:T(8,128)(2,1)}, bf16[4,96,768]{2,1,0:T(8,128)(2,1)}, u32[]{:S(2)}, u32[]{:S(2)}) %collective-permute-start.7) | collective-permute-done | bytes 589856 | tf_op jit(solution)/shard_map/ppermute | solution.py:821
  68.9 3.0 collective-permute-done.4.nb_ref
  73.2 1.4 fusion.2.refs_11_
  75.5 30.6 %attend.1 = (bf16[768,768]{1,0:T(8,128)(2,1)}, bf16[768,768]{1,0:T(8,128)(2,1)}, bf16[768,768]{1,0:T(8,128)(2,1)}, bf16[2048,768]{1,0:T(8,128)(2,1)}, bf16[2048,...) custom-call(s32[22]{0:T(128)} %pad_add_fusion.tab, bf16[768,768]{1,0:T(8,128)(2,1)} %x_ref.1, bf16[768,768]{1,0:T(8,128)(2,1)} %copy-done.12, ...), custom_call_target="tpu_custom_call" | custom-call | flops 5000000000 | bytes 16000000 | tf_op jit(solution)/shard_map/attend/pallas_call | solution.py:493
  106.1 2.7 all-gather.3.cloned.1.call-done
  108.8 42.9 %feed.1 = (bf16[768,768]{1,0:T(8,128)(2,1)}, bf16[8,864,768]{2,1,0:T(8,128)(2,1)}, f32[768,768]{1,0:T(8,128)}, bf16[768,768]{1,0:T(8,128)(2,1)}, f32[6,768]{1,0:T(8,128)}, /*index=5*/f32[4,768]{1,0:T(4,128)}) custom-call(s32[22]{0:T(128)} %pad_add_fusion.tab, bf16[768,768]{1,0:T(8,128)(2,1)} %get-tuple-element.114.o_ref, bf16[768,768]{1,0:T(8,128)(2,1)} %x_ref.1, ...), custom_call_target="tpu_custom_call" | custom-call | flops 40000000000 | bytes 48000000 | tf_op jit(solution)/shard_map/feed/pallas_call | solution.py:543
  151.7 37.8 %attend_back.1 = (bf16[768,768]{1,0:T(8,128)(2,1)}, bf16[2048,768]{1,0:T(8,128)(2,1)}, bf16[2048,768]{1,0:T(8,128)(2,1)}, bf16[4,3,96,768]{3,2,1,0:T(8,128)(2,1)...) custom-call(s32[22]{0:T(128)} %pad_add_fusion.tab, bf16[768,768]{1,0:T(8,128)(2,1)} %get-tuple-element.117.qe_ref, ...), custom_call_target="tpu_custom_call" | custom-call | flops 49999998976 | bytes 24000000 | tf_op jit(solution)/shard_map/attend_back/pallas_call | solution.py:508
  189.8 9.5 %input_rest.1 = (bf16[768,768]{1,0:T(8,128)(2,1)}, bf16[512,768]{1,0:T(8,128)(2,1)}) custom-call(s32[22]{0:T(128)} %pad_add_fusion.tab, bf16[2048,768]{1,0:T(8,128)(2,1)} %get-tuple-element.135.dk_ref, bf16[2048,768]{1,0:T(8,128)(2,1)} %get-tuple-element.136.dv_ref, bf16[4,96,768]{2,1,0:T(8,128)(2,1)} %pack_line.1.refs_0_, ...), custom_call_target="tpu_custom_call" | custom-call | flops 8000000000 | bytes 12000000 | tf_op jit(solution)/shard_map/input_rest/pallas_call | solution.py:629
  199.8 1.6 collective-permute-start.13
  201.4 1.8 collective-permute-start.14
  203.2 1.1 slice_bitcast_fusion
  204.3 1.4 collective-permute-start.15
  206.3 1.5 collective-permute-start.17
  208.0 0.7 copy.90
  208.8 3.4 %all-to-all-start = ((f32[32,1,288]{2,1,0:T(1,128)}), f32[32,1,288]{2,1,0:T(1,128)S(1)}, u32[]{:S(2)}, u32[]{:S(2)}) async-start(f32[32,1,288]{2,1,0:T(1,128)} %copy.90), calls=%async_computation | async-start | bytes 98304 | tf_op jit(solution)/shard_map/all_to_all | solution.py:886
  212.2 8.5 %input_own.1 = f32[768,768]{1,0:T(8,128)} custom-call(s32[22]{0:T(128)} %pad_add_fusion.tab, bf16[768,768]{1,0:T(8,128)(2,1)} %get-tuple-element.134.dq_ref, bf16[2048,768]{1,0:T(8,128)(2,1)} %get-tuple-element.135.dk_ref, bf16[2048,768]{1,0:T(8,128)(2,1)} %get-tuple-element.136.dv_ref, bf16[4,96,768]{2,1,0:T(8,128)(2,1)} %pack_line.1.refs_0_, ...), custom_call_target="tpu_custom_call" | custom-call | flops 5000000000 | bytes 12000000 | tf_op jit(solution)/shard_map/input_own/pallas_call | solution.py:648
  220.7 15.8 %all-to-all-done = f32[32,1,288]{2,1,0:T(1,128)S(1)} async-done(((f32[32,1,288]{2,1,0:T(1,128)}), f32[32,1,288]{2,1,0:T(1,128)S(1)}, u32[]{:S(2)}, u32[]{:S(2)}) %all-to-all-start) | async-done | bytes 36896 | tf_op jit(solution)/shard_map/all_to_all | solution.py:886
  237.2 0.8 copy-done.3
  238.1 2.9 head_line.1
  241.0 1.4 collective-permute-start.18
  242.4 2.3 collective-permute-start.19
  245.4 2.8 collective-permute-done.18.refs_1_
  248.1 7.0 %collective-permute-done.19.refs_2_ = bf16[96,576]{1,0:T(8,128)(2,1)} collective-permute-done((bf16[96,576]{1,0:T(8,128)(2,1)}, bf16[96,576]{1,0:T(8,128)(2,1)}, u32[]{:S(2)}, u32[]{:S(2)}) %collective-permute-start.19) | collective-permute-done | bytes 110624 | tf_op jit(solution)/shard_map/ppermute | solution.py:892
  255.1 2.7 feed_line.1
  257.8 2.0 collective-permute-start.21
  259.8 0.9 collective-permute-start.22
  260.7 1.5 collective-permute-start.23
  262.2 1.4 constant_dynamic-slice_fusion.refs_4_
  263.6 9.8 %collective-permute-done.21.refs_5_ = bf16[96,1728]{1,0:T(8,128)(2,1)} collective-permute-done((bf16[96,1728]{1,0:T(8,128)(2,1)}, bf16[96,1728]{1,0:T(8,128)(2,1)}, u32[]{:S(2)}, u32[]{:S(2)}) %collective-permute-start.21) | collective-permute-done | bytes 331808 | tf_op jit(solution)/shard_map/ppermute | solution.py:892
  273.4 13.3 %collective-permute-done.22.refs_6_ = bf16[96,1728]{1,0:T(8,128)(2,1)} collective-permute-done((bf16[96,1728]{1,0:T(8,128)(2,1)}, bf16[96,1728]{1,0:T(8,128)(2,1)}, u32[]{:S(2)}, u32[]{:S(2)}) %collective-permute-start.22) | collective-permute-done | bytes 331808 | tf_op jit(solution)/shard_map/ppermute | solution.py:892
  286.7 2.8 total.1
  289.5 7.6 %all-to-all-start.1 = ((f32[32,1,1]{2,1,0:T(1,128)}), f32[32,1,1]{2,1,0:T(1,128)S(1)}, u32[]{:S(2)}, u32[]{:S(2)}) async-start(f32[32,1,1]{2,1,0:T(1,128)} %bitcast.51), calls=%async_computation.2 | async-start | bytes 32768 | tf_op jit(solution)/shard_map/all_to_all | solution.py:905
  297.2 3.2 %convert_add_fusion = f32[768,768]{1,0:T(8,128)} fusion(f32[768,768]{1,0:T(8,128)S(1)} %copy-done.1, bf16[768,768]{1,0:T(8,128)(2,1)S(1)} %collective-permute-done.13, bf16[512,768]{1,0:T(8,128)(2,1)} %copy-done.3, pred[]{:T(512)S(6)} %eq.52), kind=kLoop, calls=%fused_computation.2 | loop fusion | flops 2949120 | bytes 6684673 | tf_op jit(solution)/shard_map/add | solution.py:901
  300.4 0.7 reduce
  301.7 2.5 all-to-all-done.1
  304.9 4.5 %update.1 = (f32[1,1]{1,0:T(1,128)}, f32[3,96,192]{2,1,0:T(8,128)}, f32[3,96,192]{2,1,0:T(8,128)}, f32[3,96,192]{2,1,0:T(8,128)}, f32[3,96,192]{2,1,0:T(8,128)},...) custom-call(f32[32,1]{1,0:T(8,128)} %bitcast.50, ...), custom_call_target="tpu_custom_call" | custom-call | flops 10000000 | bytes 8000000 | tf_op jit(solution)/shard_map/update/pallas_call | solution.py:708
  (78 shorter events, 9.0 us)
Async XLA Ops:
  7.2 101.6 %all-gather.3.cloned.1.call-start = ((), (), s32[]{:S(2)}) async-start(), calls=%async_computation.4 | async-start | bytes 9732096 | tf_op jit(solution)/shard_map/all_gather | solution.py:814
  9.3 245.8 %reduce-scatter.2.cloned.1.call-start = ((), (), s32[]{:S(2)}) async-start(), calls=%async_computation.3 | async-start | bytes 11943936 | tf_op jit(solution)/shard_map/reduce_scatter | solution.py:864
  9.4 9.2 %collective-permute-start = (bf16[96,768]{1,0:T(8,128)(2,1)}, bf16[96,768]{1,0:T(8,128)(2,1)S(1)}, u32[]{:S(2)}, u32[]{:S(2)}) collective-permute-start(bf16[96,768]{1,0:T(8,128)(2,1)} %get-tuple-element.106.own_ref), channel_id=1, source_target_pairs={{0,1},{1,0},{2,3},{3,2},{4,5},{5,4},{6,7},{7,6},{8,9},{9,8},{10,11... | collective-permute-start | bytes 442376 | tf_op jit(solution)/shard_map/ppermute | solution.py:815
  12.5 14.2 %collective-permute-start.1 = (bf16[96,768]{1,0:T(8,128)(2,1)}, bf16[96,768]{1,0:T(8,128)(2,1)S(1)}, u32[]{:S(2)}, u32[]{:S(2)}) collective-permute-start(bf16[96,768]{1,0:T(8,128)(2,1)} %get-tuple-element.106.own_ref), channel_id=1, source_target_pairs={{0,2},{1,3},{2,0},{3,1},{4,6},{5,7},{6,4},{7,5},{8,10},{9,11},{10,... | collective-permute-start | bytes 442376 | tf_op jit(solution)/shard_map/ppermute | solution.py:815
  15.0 11.6 %collective-permute-start.2 = (bf16[96,768]{1,0:T(8,128)(2,1)}, bf16[96,768]{1,0:T(8,128)(2,1)S(1)}, u32[]{:S(2)}, u32[]{:S(2)}) collective-permute-start(bf16[96,768]{1,0:T(8,128)(2,1)} %get-tuple-element.106.own_ref), channel_id=1, source_target_pairs={{0,3},{1,2},{2,1},{3,0},{4,7},{5,6},{6,5},{7,4},{8,11},{9,10},{10,... | collective-permute-start | bytes 442376 | tf_op jit(solution)/shard_map/ppermute | solution.py:815
  18.5 14.0 %copy-start.14 = (bf16[96,768]{1,0:T(8,128)(2,1)}, bf16[96,768]{1,0:T(8,128)(2,1)S(1)}, u32[]{:S(2)}) copy-start(bf16[96,768]{1,0:T(8,128)(2,1)S(1)} %collective-permute-done.rest_0_) | copy-start | bytes 442372
  26.7 5.8 %copy-start.15 = (bf16[96,768]{1,0:T(8,128)(2,1)}, bf16[96,768]{1,0:T(8,128)(2,1)S(1)}, u32[]{:S(2)}) copy-start(bf16[96,768]{1,0:T(8,128)(2,1)S(1)} %collective-permute-done.1.rest_1_) | copy-start | bytes 442372
  26.7 5.8 %copy-start.16 = (bf16[96,768]{1,0:T(8,128)(2,1)}, bf16[96,768]{1,0:T(8,128)(2,1)S(1)}, u32[]{:S(2)}) copy-start(bf16[96,768]{1,0:T(8,128)(2,1)S(1)} %collective-permute-done.2.rest_2_) | copy-start | bytes 442372
  26.7 45.3 %collective-permute-start.4 = (bf16[768,768]{1,0:T(8,128)(2,1)}, bf16[768,768]{1,0:T(8,128)(2,1)S(1)}, u32[]{:S(2)}, u32[]{:S(2)}) collective-permute-start(bf16[768,768]{1,0:T(8,128)(2,1)} %x_ref.1), channel_id=1, source_target_pairs={{0,1},{1,0},{2,3},{3,2},{4,5},{5,4},{6,7},{7,6},{8,9},{9,8},{10,11... | collective-permute-start | bytes 3538952 | tf_op jit(solution)/shard_map/ppermute | solution.py:819
  32.5 6.7 %copy-start = (s32[3]{0:T(128)S(1)}, s32[3]{0:T(128)}, u32[]{:S(2)}) copy-start(s32[3]{0:T(128)} %param.26) | copy-start | bytes 40
  32.5 8.0 %copy-start.4 = (bf16[768,768]{1,0:T(8,128)(2,1)S(1)}, bf16[768,768]{1,0:T(8,128)(2,1)}, u32[]{:S(2)}) copy-start(bf16[768,768]{1,0:T(8,128)(2,1)} %x_ref.1) | copy-start | bytes 3538948
  34.9 38.1 %copy-start.9 = (s32[3]{0:T(128)S(1)}, s32[3]{0:T(128)}, u32[]{:S(2)}) copy-start(s32[3]{0:T(128)} %param.28) | copy-start | bytes 40
  34.9 38.1 %copy-start.10 = (s32[3]{0:T(128)S(1)}, s32[3]{0:T(128)}, u32[]{:S(2)}) copy-start(s32[3]{0:T(128)} %param.27) | copy-start | bytes 40
  34.9 38.1 %copy-start.11 = (s32[3]{0:T(128)S(1)}, s32[3]{0:T(128)}, u32[]{:S(2)}) copy-start(s32[3]{0:T(128)} %param.29) | copy-start | bytes 40
  34.9 34.0 %collective-permute-start.3 = (bf16[4,96,768]{2,1,0:T(8,128)(2,1)}, bf16[4,96,768]{2,1,0:T(8,128)(2,1)}, u32[]{:S(2)}, u32[]{:S(2)}) collective-permute-start(bf16[4,96,768]{2,1,0:T(8,128)(2,1)} %pack_line.1.refs_0_), channel_id=1, source_target_pairs={{0,8},{1,9},{2,10},{3,11},{4,12},{5,13},{6,14},{7,15},{8,0},{9,1},... | collective-permute-start | bytes 1769480 | tf_op jit(solution)/shard_map/ppermute | solution.py:821
  36.5 19.5 %collective-permute-start.6 = (bf16[4,96,768]{2,1,0:T(8,128)(2,1)}, bf16[4,96,768]{2,1,0:T(8,128)(2,1)}, u32[]{:S(2)}, u32[]{:S(2)}) collective-permute-start(bf16[4,96,768]{2,1,0:T(8,128)(2,1)} %pack_line.1.refs_0_), channel_id=1, source_target_pairs={{0,16},{1,17},{2,18},{3,19},{4,20},{5,21},{6,22},{7,23},{8,24},{9,... | collective-permute-start | bytes 1769480 | tf_op jit(solution)/shard_map/ppermute | solution.py:821
  38.1 30.8 %collective-permute-start.7 = (bf16[4,96,768]{2,1,0:T(8,128)(2,1)}, bf16[4,96,768]{2,1,0:T(8,128)(2,1)}, u32[]{:S(2)}, u32[]{:S(2)}) collective-permute-start(bf16[4,96,768]{2,1,0:T(8,128)(2,1)} %pack_line.1.refs_0_), channel_id=1, source_target_pairs={{0,24},{1,25},{2,26},{3,27},{4,28},{5,29},{6,30},{7,31},{8,16},{9,... | collective-permute-start | bytes 1769480 | tf_op jit(solution)/shard_map/ppermute | solution.py:821
  40.6 34.0 %collective-permute-start.5 = (bf16[512,768]{1,0:T(8,128)(2,1)S(1)}, bf16[512,768]{1,0:T(8,128)(2,1)S(1)}, u32[]{:S(2)}, u32[]{:S(2)}) collective-permute-start(bf16[512,768]{1,0:T(8,128)(2,1)S(1)} %constant_dynamic-slice_fusion.1), channel_id=1, source_target_pairs={{0,0},{1,2},{2,1},{3,3},{4,4},{5,6},{6,5},{7,7},{8,8},{9,10},{10,9... | collective-permute-start | bytes 2359304 | tf_op jit(solution)/shard_map/ppermute | solution.py:820
  56.1 18.6 %collective-permute-start.10 = (bf16[4,96,768]{2,1,0:T(8,128)(2,1)}, bf16[4,96,768]{2,1,0:T(8,128)(2,1)}, u32[]{:S(2)}, u32[]{:S(2)}) collective-permute-start(bf16[4,96,768]{2,1,0:T(8,128)(2,1)} %collective-permute-done.6.refs_2_), channel_id=1, source_target_pairs={{0,4},{1,5},{2,6},{3,7},{4,0},{5,1},{6,2},{7,3},{8,12},{9,13},{10,... | collective-permute-start | bytes 1769480 | tf_op jit(solution)/shard_map/ppermute | solution.py:823
  68.9 5.7 %collective-permute-start.11 = (bf16[4,96,768]{2,1,0:T(8,128)(2,1)}, bf16[4,96,768]{2,1,0:T(8,128)(2,1)}, u32[]{:S(2)}, u32[]{:S(2)}) collective-permute-start(bf16[4,96,768]{2,1,0:T(8,128)(2,1)} %collective-permute-done.7.refs_3_), channel_id=1, source_target_pairs={{0,4},{1,5},{2,6},{3,7},{4,0},{5,1},{6,2},{7,3},{8,12},{9,13},{10,... | collective-permute-start | bytes 1769480 | tf_op jit(solution)/shard_map/ppermute | solution.py:823
  71.9 3.2 %copy-start.12 = (bf16[768,768]{1,0:T(8,128)(2,1)}, bf16[768,768]{1,0:T(8,128)(2,1)S(1)}, u32[]{:S(2)}) copy-start(bf16[768,768]{1,0:T(8,128)(2,1)S(1)} %collective-permute-done.4.nb_ref) | copy-start | bytes 3538948
  71.9 2.7 collective-permute-start.9
  71.9 3.2 %collective-permute-start.8 = (bf16[4,96,768]{2,1,0:T(8,128)(2,1)}, bf16[4,96,768]{2,1,0:T(8,128)(2,1)}, u32[]{:S(2)}, u32[]{:S(2)}) collective-permute-start(bf16[4,96,768]{2,1,0:T(8,128)(2,1)} %pack_line.1.refs_0_), channel_id=1, source_target_pairs={{0,4},{1,5},{2,6},{3,7},{4,0},{5,1},{6,2},{7,3},{8,12},{9,13},{10,... | collective-permute-start | bytes 1769480 | tf_op jit(solution)/shard_map/ppermute | solution.py:823
  74.6 0.9 copy-start.13
  189.5 9.8 %collective-permute-start.12 = (bf16[4,3,96,768]{3,2,1,0:T(8,128)(2,1)}, bf16[4,3,96,768]{3,2,1,0:T(8,128)(2,1)S(1)}, u32[]{:S(2)}, u32[]{:S(2)}) collective-permute-start(bf16[4,3,96,768]{3,2,1,0:T(8,128)(2,1)} %get-tuple-element.124), channel_id=1, source_target_pairs={{0,4},{1,5},{2,6},{3,7},{4,0},{5,1},{6,2},{7,3},{8,12},{9,13},{10,... | collective-permute-start | bytes 5308424 | tf_op jit(solution)/shard_map/ppermute | solution.py:873
  189.8 9.5 %copy-start.2 = (bf16[4,3,96,768]{3,2,1,0:T(8,128)(2,1)S(1)}, bf16[4,3,96,768]{3,2,1,0:T(8,128)(2,1)}, u32[]{:S(2)}) copy-start(bf16[4,3,96,768]{3,2,1,0:T(8,128)(2,1)} %get-tuple-element.123) | copy-start | bytes 5308420
  199.8 7.9 %copy-start.6 = (f32[6,768]{1,0:T(8,128)S(1)}, f32[6,768]{1,0:T(8,128)}, u32[]{:S(2)}) copy-start(f32[6,768]{1,0:T(8,128)} %get-tuple-element.132) | copy-start | bytes 55300
  199.8 7.9 %copy-start.7 = (f32[4,768]{1,0:T(4,128)S(1)}, f32[4,768]{1,0:T(4,128)}, u32[]{:S(2)}) copy-start(f32[4,768]{1,0:T(4,128)} %get-tuple-element.133) | copy-start | bytes 36868
  199.8 7.9 %copy-start.8 = (f32[2,768]{1,0:T(2,128)S(1)}, f32[2,768]{1,0:T(2,128)}, u32[]{:S(2)}) copy-start(f32[2,768]{1,0:T(2,128)} %get-tuple-element.131) | copy-start | bytes 18436
  199.8 37.4 %collective-permute-start.13 = (bf16[768,768]{1,0:T(8,128)(2,1)}, bf16[768,768]{1,0:T(8,128)(2,1)S(1)}, u32[]{:S(2)}, u32[]{:S(2)}) collective-permute-start(bf16[768,768]{1,0:T(8,128)(2,1)} %get-tuple-element.138), channel_id=1, source_target_pairs={{0,1},{1,0},{2,3},{3,2},{4,5},{5,4},{6,7},{7,6},{8,9},{9,8},{10,11... | collective-permute-start | bytes 3538952 | tf_op jit(solution)/shard_map/ppermute | solution.py:880
  201.4 35.8 %collective-permute-start.14 = (bf16[512,768]{1,0:T(8,128)(2,1)}, bf16[512,768]{1,0:T(8,128)(2,1)S(1)}, u32[]{:S(2)}, u32[]{:S(2)}) collective-permute-start(bf16[512,768]{1,0:T(8,128)(2,1)} %get-tuple-element.139), channel_id=1, source_target_pairs={{0,0},{1,2},{2,1},{3,3},{4,4},{5,6},{6,5},{7,7},{8,8},{9,10},{10,9... | collective-permute-start | bytes 2359304 | tf_op jit(solution)/shard_map/ppermute | solution.py:881
  204.3 32.9 %collective-permute-start.15 = (bf16[3,96,768]{2,1,0:T(8,128)(2,1)}, bf16[3,96,768]{2,1,0:T(8,128)(2,1)}, u32[]{:S(2)}, u32[]{:S(2)}) collective-permute-start(bf16[3,96,768]{2,1,0:T(8,128)(2,1)} %get-tuple-element.194), channel_id=1, source_target_pairs={{0,8},{1,9},{2,10},{3,11},{4,12},{5,13},{6,14},{7,15},{8,0},{9,1},... | collective-permute-start | bytes 1327112 | tf_op jit(solution)/shard_map/ppermute | solution.py:879
  205.7 31.5 %collective-permute-start.16 = (bf16[3,96,768]{2,1,0:T(8,128)(2,1)S(1)}, bf16[3,96,768]{2,1,0:T(8,128)(2,1)}, u32[]{:S(2)}, u32[]{:S(2)}) collective-permute-start(bf16[3,96,768]{2,1,0:T(8,128)(2,1)S(1)} %get-tuple-element.193), channel_id=1, source_target_pairs={{0,16},{1,17},{2,18},{3,19},{4,20},{5,21},{6,22},{7,23},{8,24},{9,... | collective-permute-start | bytes 1327112 | tf_op jit(solution)/shard_map/ppermute | solution.py:879
  206.3 30.9 %collective-permute-start.17 = (bf16[3,96,768]{2,1,0:T(8,128)(2,1)S(1)}, bf16[3,96,768]{2,1,0:T(8,128)(2,1)}, u32[]{:S(2)}, u32[]{:S(2)}) collective-permute-start(bf16[3,96,768]{2,1,0:T(8,128)(2,1)S(1)} %get-tuple-element.192), channel_id=1, source_target_pairs={{0,24},{1,25},{2,26},{3,27},{4,28},{5,29},{6,30},{7,31},{8,16},{9,... | collective-permute-start | bytes 1327112 | tf_op jit(solution)/shard_map/ppermute | solution.py:879
  208.8 27.8 %all-to-all-start = ((f32[32,1,288]{2,1,0:T(1,128)}), f32[32,1,288]{2,1,0:T(1,128)S(1)}, u32[]{:S(2)}, u32[]{:S(2)}) async-start(f32[32,1,288]{2,1,0:T(1,128)} %copy.90), calls=%async_computation | async-start | bytes 98304 | tf_op jit(solution)/shard_map/all_to_all | solution.py:886
  237.2 0.9 copy-start.3
  241.0 56.2 %copy-start.1 = (f32[768,768]{1,0:T(8,128)S(1)}, f32[768,768]{1,0:T(8,128)}, u32[]{:S(2)}) copy-start(f32[768,768]{1,0:T(8,128)} %input_own.1) | copy-start | bytes 7077892
  241.0 7.2 %collective-permute-start.18 = (bf16[96,576]{1,0:T(8,128)(2,1)}, bf16[96,576]{1,0:T(8,128)(2,1)}, u32[]{:S(2)}, u32[]{:S(2)}) collective-permute-start(bf16[96,576]{1,0:T(8,128)(2,1)} %get-tuple-element.150), channel_id=1, source_target_pairs={{0,1},{1,0},{2,3},{3,2},{4,5},{5,4},{6,7},{7,6},{8,9},{9,8},{10,11... | collective-permute-start | bytes 331784 | tf_op jit(solution)/shard_map/ppermute | solution.py:892
  242.4 12.7 %collective-permute-start.19 = (bf16[96,576]{1,0:T(8,128)(2,1)}, bf16[96,576]{1,0:T(8,128)(2,1)}, u32[]{:S(2)}, u32[]{:S(2)}) collective-permute-start(bf16[96,576]{1,0:T(8,128)(2,1)} %get-tuple-element.151), channel_id=1, source_target_pairs={{0,2},{1,3},{2,0},{3,1},{4,6},{5,7},{6,4},{7,5},{8,10},{9,11},{10,... | collective-permute-start | bytes 331784 | tf_op jit(solution)/shard_map/ppermute | solution.py:892
  244.7 10.4 %collective-permute-start.20 = (bf16[96,576]{1,0:T(8,128)(2,1)}, bf16[96,576]{1,0:T(8,128)(2,1)}, u32[]{:S(2)}, u32[]{:S(2)}) collective-permute-start(bf16[96,576]{1,0:T(8,128)(2,1)} %get-tuple-element.152), channel_id=1, source_target_pairs={{0,3},{1,2},{2,1},{3,0},{4,7},{5,6},{6,5},{7,4},{8,11},{9,10},{10,... | collective-permute-start | bytes 331784 | tf_op jit(solution)/shard_map/ppermute | solution.py:892
  257.8 15.6 %collective-permute-start.21 = (bf16[96,1728]{1,0:T(8,128)(2,1)}, bf16[96,1728]{1,0:T(8,128)(2,1)}, u32[]{:S(2)}, u32[]{:S(2)}) collective-permute-start(bf16[96,1728]{1,0:T(8,128)(2,1)} %get-tuple-element.159), channel_id=1, source_target_pairs={{0,1},{1,0},{2,3},{3,2},{4,5},{5,4},{6,7},{7,6},{8,9},{9,8},{10,11... | collective-permute-start | bytes 995336 | tf_op jit(solution)/shard_map/ppermute | solution.py:892
  259.8 27.0 %collective-permute-start.22 = (bf16[96,1728]{1,0:T(8,128)(2,1)}, bf16[96,1728]{1,0:T(8,128)(2,1)}, u32[]{:S(2)}, u32[]{:S(2)}) collective-permute-start(bf16[96,1728]{1,0:T(8,128)(2,1)} %get-tuple-element.160), channel_id=1, source_target_pairs={{0,2},{1,3},{2,0},{3,1},{4,6},{5,7},{6,4},{7,5},{8,10},{9,11},{10,... | collective-permute-start | bytes 995336 | tf_op jit(solution)/shard_map/ppermute | solution.py:892
  260.7 26.0 %collective-permute-start.23 = (bf16[96,1728]{1,0:T(8,128)(2,1)}, bf16[96,1728]{1,0:T(8,128)(2,1)}, u32[]{:S(2)}, u32[]{:S(2)}) collective-permute-start(bf16[96,1728]{1,0:T(8,128)(2,1)} %get-tuple-element.161), channel_id=1, source_target_pairs={{0,3},{1,2},{2,1},{3,0},{4,7},{5,6},{6,5},{7,4},{8,11},{9,10},{10,... | collective-permute-start | bytes 995336 | tf_op jit(solution)/shard_map/ppermute | solution.py:892
  289.5 14.7 %all-to-all-start.1 = ((f32[32,1,1]{2,1,0:T(1,128)}), f32[32,1,1]{2,1,0:T(1,128)S(1)}, u32[]{:S(2)}, u32[]{:S(2)}) async-start(f32[32,1,1]{2,1,0:T(1,128)} %bitcast.51), calls=%async_computation.2 | async-start | bytes 32768 | tf_op jit(solution)/shard_map/all_to_all | solution.py:905
  304.3 0.6 copy-start.5
Sparse Core Ops, SparseCore 0:
  11.4 97.3 all-gather.2
  151.8 91.9 reduce-scatter.1

commit v6 on v5

--- a/solution.py
+++ b/solution.py
@@ -381,6 +381,7 @@
         for n in range(3):
             sums_ref[n : n + 1, :] = sums[n]
         dw_ref[:, :RP] = dot_nn(e2t_s[...], o_ref[...]).astype(BF).reshape(RB, RP, D)
+        dw_ref[:, RP:] = jnp.zeros((RB, RP, D), BF)
 
 
 def pack_kernel(tab, own_ref, *rest):
@@ -454,7 +455,7 @@
             def _():
                 ref[:, :D] = feed_ref[2 * m * rows : (2 * m + 1) * rows, :]
                 ref[:, D : 2 * D] = feed_ref[(2 * m + 1) * rows : (2 * m + 2) * rows, :]
-                ref[:, 2 * D :] = feed_ref[8 * rows :, m * width : (m + 1) * width]
+                ref[:, 2 * D :] = feed_ref[8 * rows : 9 * rows, m * width : (m + 1) * width]
 
 
 def call(kernel, grid, in_specs, out_specs, out_shape, scratch, flops, bytes_accessed, name):
@@ -562,7 +563,7 @@
         ],
         [
             shape_of((ROWS, D), BF),
-            shape_of((RB, 9 * RP, D), BF),
+            shape_of((RB, 10 * RP, D), BF),
             shape_of((ROWS, D), F32),
             shape_of((ROWS, D), BF),
             shape_of((6, D), F32),
@@ -860,7 +861,7 @@
         return jnp.moveaxis(moved, -3, 0)
 
     if part != RP:
-        feed_dw = to_parts(feed_dw.reshape(RB, 9, RP, D)).reshape(dp_count, 9 * part, D)
+        feed_dw = to_parts(feed_dw.reshape(RB, 10, RP, D)).reshape(dp_count, 10 * part, D)
     feed_part = lax.psum_scatter(feed_dw, "dp", scatter_dimension=0, tiled=False)
 
     dq, dk, dv, keep, give, sums_head = attend_back(tab, qe, qo, k, v, d_o, o, xt)

time: 317 us -> 317 us (level)
  no operation moved by 1% of the time
where the time goes in v6:
time: 317 us; the launch traced here: 316 us
  Pallas kernels  147 us (46%)
  waiting for transfers between devices  96.1 us (30%)
  starting transfers between devices  43 us (14%)
  between operations  14.3 us (5%)
  local copies, waits for them, and re-layouts  8.16 us (3%)
  other arithmetic  7.88 us (2%)
    pallas_call x1, Pallas kernels, feed(): call(feed_kernel, 9, [whole(ROWS, D), whole(ROWS, D), *[wo_spec] * 8, who...  43.3 us
    pallas_call x1, Pallas kernels, attend_back(): call(attend_back_kernel, PAIRS, [columns(ROWS), columns(ROWS), columns(8...  37.8 us
    ppermute x6, waiting for transfers between devices, along_line(): lax.ppermute(parts[n], AXES, swap_z[n])  33.1 us
    pallas_call x1, Pallas kernels, attend(): call(attend_kernel, PAIRS, [whole(ROWS, D), whole(ROWS, D), whole(2 * BLK...  30.6 us
    ppermute x3, waiting for transfers between devices, shards(): lax.ppermute(along_z, AXES, swap_chip[n])  26.8 us
    all_to_all x1, waiting for transfers between devices, shards(): vector_parts = lax.all_to_all(vector_part, AXES, 0, 0, tiled=True)  15.9 us
    ppermute x3, waiting for transfers between devices, shards(): line = [lax.ppermute(mine, AXES, swap_z[n]) for n in range(1, mp_count)]  11.6 us
    pallas_call x1, Pallas kernels, input_rest(): call(input_rest_kernel, 5, [each, each] + [w_spec] * 8, [pl.BlockSpec((BL...  9.1 us
  transfers between devices with their start and end apart: 28, of which 13 were waited for; matrix products, arithmetic and copies ran while one was open for 4% of the time, Pallas kernels for 29%

profile of v6, /device:TPU:0, one launch (start us, length us, event | category | flops | bytes accessed | tf_op | source)
XLA Modules:
  0.0 316.1 jit_solution(17218048607415355139)
XLA Ops:
  7.2 2.1 round_shards.1
  9.4 3.1 collective-permute-start
  12.5 2.6 collective-permute-start.1
  15.1 3.5 %collective-permute-done.rest_0_ = bf16[96,768]{1,0:T(8,128)(2,1)S(1)} collective-permute-done((bf16[96,768]{1,0:T(8,128)(2,1)}, bf16[96,768]{1,0:T(8,128)(2,1)S(1)}, u32[]{:S(2)}, u32[]{:S(2)}) %collective-permute-start) | collective-permute-done | bytes 147488 | tf_op jit(solution)/shard_map/ppermute | solution.py:816
  18.5 8.1 %collective-permute-done.1.rest_1_ = bf16[96,768]{1,0:T(8,128)(2,1)S(1)} collective-permute-done((bf16[96,768]{1,0:T(8,128)(2,1)}, bf16[96,768]{1,0:T(8,128)(2,1)S(1)}, u32[]{:S(2)}, u32[]{:S(2)}) %collective-permute-start.1) | collective-permute-done | bytes 147488 | tf_op jit(solution)/shard_map/ppermute | solution.py:816
  26.7 5.8 %collective-permute-start.4 = (bf16[768,768]{1,0:T(8,128)(2,1)}, bf16[768,768]{1,0:T(8,128)(2,1)S(1)}, u32[]{:S(2)}, u32[]{:S(2)}) collective-permute-start(bf16[768,768]{1,0:T(8,128)(2,1)} %x_ref.1), channel_id=1, source_target_pairs={{0,1},{1,0},{2,3},{3,2},{4,5},{5,4},{6,7},{7,6},{8,9},{9,8},{10,11... | collective-permute-start | bytes 3538952 | tf_op jit(solution)/shard_map/ppermute | solution.py:820
  32.5 2.4 pack_line.1.refs_0_
  35.0 1.6 collective-permute-start.3
  36.5 1.6 collective-permute-start.6
  40.6 0.7 collective-permute-start.5
  41.3 0.7 constant_dynamic-slice_fusion.4
  42.1 13.9 %collective-permute-done.6.refs_2_ = bf16[4,96,768]{2,1,0:T(8,128)(2,1)} collective-permute-done((bf16[4,96,768]{2,1,0:T(8,128)(2,1)}, bf16[4,96,768]{2,1,0:T(8,128)(2,1)}, u32[]{:S(2)}, u32[]{:S(2)}) %collective-permute-start.6) | collective-permute-done | bytes 589856 | tf_op jit(solution)/shard_map/ppermute | solution.py:822
  56.1 12.9 %collective-permute-done.7.refs_3_ = bf16[4,96,768]{2,1,0:T(8,128)(2,1)} collective-permute-done((bf16[4,96,768]{2,1,0:T(8,128)(2,1)}, bf16[4,96,768]{2,1,0:T(8,128)(2,1)}, u32[]{:S(2)}, u32[]{:S(2)}) %collective-permute-start.7) | collective-permute-done | bytes 589856 | tf_op jit(solution)/shard_map/ppermute | solution.py:822
  68.9 3.0 collective-permute-done.4.nb_ref
  73.2 1.4 fusion.2.refs_11_
  75.5 30.6 %attend.1 = (bf16[768,768]{1,0:T(8,128)(2,1)}, bf16[768,768]{1,0:T(8,128)(2,1)}, bf16[768,768]{1,0:T(8,128)(2,1)}, bf16[2048,768]{1,0:T(8,128)(2,1)}, bf16[2048,...) custom-call(s32[22]{0:T(128)} %pad_add_fusion.tab, bf16[768,768]{1,0:T(8,128)(2,1)} %x_ref.1, bf16[768,768]{1,0:T(8,128)(2,1)} %copy-done.12, ...), custom_call_target="tpu_custom_call" | custom-call | flops 5000000000 | bytes 16000000 | tf_op jit(solution)/shard_map/attend/pallas_call | solution.py:494
  106.2 2.7 all-gather.3.cloned.1.call-done
  108.8 43.3 %feed.1 = (bf16[768,768]{1,0:T(8,128)(2,1)}, bf16[8,960,768]{2,1,0:T(8,128)(2,1)}, f32[768,768]{1,0:T(8,128)}, bf16[768,768]{1,0:T(8,128)(2,1)}, f32[6,768]{1,0:T(8,128)}, /*index=5*/f32[4,768]{1,0:T(4,128)}) custom-call(s32[22]{0:T(128)} %pad_add_fusion.tab, bf16[768,768]{1,0:T(8,128)(2,1)} %get-tuple-element.114.o_ref, bf16[768,768]{1,0:T(8,128)(2,1)} %x_ref.1, ...), custom_call_target="tpu_custom_call" | custom-call | flops 40000000000 | bytes 48000000 | tf_op jit(solution)/shard_map/feed/pallas_call | solution.py:544
  152.1 37.8 %attend_back.1 = (bf16[768,768]{1,0:T(8,128)(2,1)}, bf16[2048,768]{1,0:T(8,128)(2,1)}, bf16[2048,768]{1,0:T(8,128)(2,1)}, bf16[4,3,96,768]{3,2,1,0:T(8,128)(2,1)...) custom-call(s32[22]{0:T(128)} %pad_add_fusion.tab, bf16[768,768]{1,0:T(8,128)(2,1)} %get-tuple-element.117.qe_ref, ...), custom_call_target="tpu_custom_call" | custom-call | flops 49999998976 | bytes 24000000 | tf_op jit(solution)/shard_map/attend_back/pallas_call | solution.py:509
  190.2 9.1 %input_rest.1 = (bf16[768,768]{1,0:T(8,128)(2,1)}, bf16[512,768]{1,0:T(8,128)(2,1)}) custom-call(s32[22]{0:T(128)} %pad_add_fusion.tab, bf16[2048,768]{1,0:T(8,128)(2,1)} %get-tuple-element.135.dk_ref, bf16[2048,768]{1,0:T(8,128)(2,1)} %get-tuple-element.136.dv_ref, bf16[4,96,768]{2,1,0:T(8,128)(2,1)} %pack_line.1.refs_0_, ...), custom_call_target="tpu_custom_call" | custom-call | flops 8000000000 | bytes 12000000 | tf_op jit(solution)/shard_map/input_rest/pallas_call | solution.py:630
  199.9 1.5 collective-permute-start.13
  201.4 1.8 collective-permute-start.14
  203.2 1.1 slice_bitcast_fusion
  204.3 1.4 collective-permute-start.15
  206.3 1.4 collective-permute-start.17
  208.0 0.7 copy.90
  208.8 3.4 %all-to-all-start = ((f32[32,1,288]{2,1,0:T(1,128)}), f32[32,1,288]{2,1,0:T(1,128)S(1)}, u32[]{:S(2)}, u32[]{:S(2)}) async-start(f32[32,1,288]{2,1,0:T(1,128)} %copy.90), calls=%async_computation | async-start | bytes 98304 | tf_op jit(solution)/shard_map/all_to_all | solution.py:887
  212.2 8.5 %input_own.1 = f32[768,768]{1,0:T(8,128)} custom-call(s32[22]{0:T(128)} %pad_add_fusion.tab, bf16[768,768]{1,0:T(8,128)(2,1)} %get-tuple-element.134.dq_ref, bf16[2048,768]{1,0:T(8,128)(2,1)} %get-tuple-element.135.dk_ref, bf16[2048,768]{1,0:T(8,128)(2,1)} %get-tuple-element.136.dv_ref, bf16[4,96,768]{2,1,0:T(8,128)(2,1)} %pack_line.1.refs_0_, ...), custom_call_target="tpu_custom_call" | custom-call | flops 5000000000 | bytes 12000000 | tf_op jit(solution)/shard_map/input_own/pallas_call | solution.py:649
  220.7 15.9 %all-to-all-done = f32[32,1,288]{2,1,0:T(1,128)S(1)} async-done(((f32[32,1,288]{2,1,0:T(1,128)}), f32[32,1,288]{2,1,0:T(1,128)S(1)}, u32[]{:S(2)}, u32[]{:S(2)}) %all-to-all-start) | async-done | bytes 36896 | tf_op jit(solution)/shard_map/all_to_all | solution.py:887
  237.2 0.9 copy-done.3
  238.1 2.9 head_line.1
  241.0 1.6 collective-permute-start.18
  242.6 2.5 collective-permute-start.19
  245.4 2.7 collective-permute-done.18.refs_1_
  248.1 7.2 %collective-permute-done.19.refs_2_ = bf16[96,576]{1,0:T(8,128)(2,1)} collective-permute-done((bf16[96,576]{1,0:T(8,128)(2,1)}, bf16[96,576]{1,0:T(8,128)(2,1)}, u32[]{:S(2)}, u32[]{:S(2)}) %collective-permute-start.19) | collective-permute-done | bytes 110624 | tf_op jit(solution)/shard_map/ppermute | solution.py:893
  255.3 2.7 feed_line.1
  258.1 2.0 collective-permute-start.21
  260.0 0.9 collective-permute-start.22
  261.0 1.5 collective-permute-start.23
  262.5 1.4 constant_dynamic-slice_fusion.refs_4_
  263.9 9.8 %collective-permute-done.21.refs_5_ = bf16[96,1728]{1,0:T(8,128)(2,1)} collective-permute-done((bf16[96,1728]{1,0:T(8,128)(2,1)}, bf16[96,1728]{1,0:T(8,128)(2,1)}, u32[]{:S(2)}, u32[]{:S(2)}) %collective-permute-start.21) | collective-permute-done | bytes 331808 | tf_op jit(solution)/shard_map/ppermute | solution.py:893
  273.6 13.4 %collective-permute-done.22.refs_6_ = bf16[96,1728]{1,0:T(8,128)(2,1)} collective-permute-done((bf16[96,1728]{1,0:T(8,128)(2,1)}, bf16[96,1728]{1,0:T(8,128)(2,1)}, u32[]{:S(2)}, u32[]{:S(2)}) %collective-permute-start.22) | collective-permute-done | bytes 331808 | tf_op jit(solution)/shard_map/ppermute | solution.py:893
  287.0 2.8 total.1
  289.8 7.3 %all-to-all-start.1 = ((f32[32,1,1]{2,1,0:T(1,128)}), f32[32,1,1]{2,1,0:T(1,128)S(1)}, u32[]{:S(2)}, u32[]{:S(2)}) async-start(f32[32,1,1]{2,1,0:T(1,128)} %bitcast.51), calls=%async_computation.2 | async-start | bytes 32768 | tf_op jit(solution)/shard_map/all_to_all | solution.py:906
  297.1 3.2 %convert_add_fusion = f32[768,768]{1,0:T(8,128)} fusion(f32[768,768]{1,0:T(8,128)S(1)} %copy-done.1, bf16[768,768]{1,0:T(8,128)(2,1)S(1)} %collective-permute-done.13, bf16[512,768]{1,0:T(8,128)(2,1)} %copy-done.3, pred[]{:T(512)S(6)} %eq.52), kind=kLoop, calls=%fused_computation.2 | loop fusion | flops 2949120 | bytes 6684673 | tf_op jit(solution)/shard_map/add | solution.py:902
  300.3 0.7 reduce
  301.7 2.5 all-to-all-done.1
  304.8 4.5 %update.1 = (f32[1,1]{1,0:T(1,128)}, f32[3,96,192]{2,1,0:T(8,128)}, f32[3,96,192]{2,1,0:T(8,128)}, f32[3,96,192]{2,1,0:T(8,128)}, f32[3,96,192]{2,1,0:T(8,128)},...) custom-call(f32[32,1]{1,0:T(8,128)} %bitcast.50, ...), custom_call_target="tpu_custom_call" | custom-call | flops 10000000 | bytes 8000000 | tf_op jit(solution)/shard_map/update/pallas_call | solution.py:709
  (78 shorter events, 8.8 us)
Async XLA Ops:
  7.2 101.6 %all-gather.3.cloned.1.call-start = ((), (), s32[]{:S(2)}) async-start(), calls=%async_computation.4 | async-start | bytes 9732096 | tf_op jit(solution)/shard_map/all_gather | solution.py:815
  9.3 246.0 %reduce-scatter.2.cloned.1.call-start = ((), (), s32[]{:S(2)}) async-start(), calls=%async_computation.3 | async-start | bytes 13271040 | tf_op jit(solution)/shard_map/reduce_scatter | solution.py:865
  9.4 9.2 %collective-permute-start = (bf16[96,768]{1,0:T(8,128)(2,1)}, bf16[96,768]{1,0:T(8,128)(2,1)S(1)}, u32[]{:S(2)}, u32[]{:S(2)}) collective-permute-start(bf16[96,768]{1,0:T(8,128)(2,1)} %get-tuple-element.106.own_ref), channel_id=1, source_target_pairs={{0,1},{1,0},{2,3},{3,2},{4,5},{5,4},{6,7},{7,6},{8,9},{9,8},{10,11... | collective-permute-start | bytes 442376 | tf_op jit(solution)/shard_map/ppermute | solution.py:816
  12.5 14.2 %collective-permute-start.1 = (bf16[96,768]{1,0:T(8,128)(2,1)}, bf16[96,768]{1,0:T(8,128)(2,1)S(1)}, u32[]{:S(2)}, u32[]{:S(2)}) collective-permute-start(bf16[96,768]{1,0:T(8,128)(2,1)} %get-tuple-element.106.own_ref), channel_id=1, source_target_pairs={{0,2},{1,3},{2,0},{3,1},{4,6},{5,7},{6,4},{7,5},{8,10},{9,11},{10,... | collective-permute-start | bytes 442376 | tf_op jit(solution)/shard_map/ppermute | solution.py:816
  15.0 11.6 %collective-permute-start.2 = (bf16[96,768]{1,0:T(8,128)(2,1)}, bf16[96,768]{1,0:T(8,128)(2,1)S(1)}, u32[]{:S(2)}, u32[]{:S(2)}) collective-permute-start(bf16[96,768]{1,0:T(8,128)(2,1)} %get-tuple-element.106.own_ref), channel_id=1, source_target_pairs={{0,3},{1,2},{2,1},{3,0},{4,7},{5,6},{6,5},{7,4},{8,11},{9,10},{10,... | collective-permute-start | bytes 442376 | tf_op jit(solution)/shard_map/ppermute | solution.py:816
  18.5 14.0 %copy-start.14 = (bf16[96,768]{1,0:T(8,128)(2,1)}, bf16[96,768]{1,0:T(8,128)(2,1)S(1)}, u32[]{:S(2)}) copy-start(bf16[96,768]{1,0:T(8,128)(2,1)S(1)} %collective-permute-done.rest_0_) | copy-start | bytes 442372
  26.7 5.8 %copy-start.15 = (bf16[96,768]{1,0:T(8,128)(2,1)}, bf16[96,768]{1,0:T(8,128)(2,1)S(1)}, u32[]{:S(2)}) copy-start(bf16[96,768]{1,0:T(8,128)(2,1)S(1)} %collective-permute-done.1.rest_1_) | copy-start | bytes 442372
  26.7 5.8 %copy-start.16 = (bf16[96,768]{1,0:T(8,128)(2,1)}, bf16[96,768]{1,0:T(8,128)(2,1)S(1)}, u32[]{:S(2)}) copy-start(bf16[96,768]{1,0:T(8,128)(2,1)S(1)} %collective-permute-done.2.rest_2_) | copy-start | bytes 442372
  26.7 45.3 %collective-permute-start.4 = (bf16[768,768]{1,0:T(8,128)(2,1)}, bf16[768,768]{1,0:T(8,128)(2,1)S(1)}, u32[]{:S(2)}, u32[]{:S(2)}) collective-permute-start(bf16[768,768]{1,0:T(8,128)(2,1)} %x_ref.1), channel_id=1, source_target_pairs={{0,1},{1,0},{2,3},{3,2},{4,5},{5,4},{6,7},{7,6},{8,9},{9,8},{10,11... | collective-permute-start | bytes 3538952 | tf_op jit(solution)/shard_map/ppermute | solution.py:820
  32.5 6.7 %copy-start = (s32[3]{0:T(128)S(1)}, s32[3]{0:T(128)}, u32[]{:S(2)}) copy-start(s32[3]{0:T(128)} %param.26) | copy-start | bytes 40
  32.5 8.0 %copy-start.4 = (bf16[768,768]{1,0:T(8,128)(2,1)S(1)}, bf16[768,768]{1,0:T(8,128)(2,1)}, u32[]{:S(2)}) copy-start(bf16[768,768]{1,0:T(8,128)(2,1)} %x_ref.1) | copy-start | bytes 3538948
  35.0 38.1 %copy-start.9 = (s32[3]{0:T(128)S(1)}, s32[3]{0:T(128)}, u32[]{:S(2)}) copy-start(s32[3]{0:T(128)} %param.28) | copy-start | bytes 40
  35.0 38.1 %copy-start.10 = (s32[3]{0:T(128)S(1)}, s32[3]{0:T(128)}, u32[]{:S(2)}) copy-start(s32[3]{0:T(128)} %param.27) | copy-start | bytes 40
  35.0 38.1 %copy-start.11 = (s32[3]{0:T(128)S(1)}, s32[3]{0:T(128)}, u32[]{:S(2)}) copy-start(s32[3]{0:T(128)} %param.29) | copy-start | bytes 40
  35.0 34.0 %collective-permute-start.3 = (bf16[4,96,768]{2,1,0:T(8,128)(2,1)}, bf16[4,96,768]{2,1,0:T(8,128)(2,1)}, u32[]{:S(2)}, u32[]{:S(2)}) collective-permute-start(bf16[4,96,768]{2,1,0:T(8,128)(2,1)} %pack_line.1.refs_0_), channel_id=1, source_target_pairs={{0,8},{1,9},{2,10},{3,11},{4,12},{5,13},{6,14},{7,15},{8,0},{9,1},... | collective-permute-start | bytes 1769480 | tf_op jit(solution)/shard_map/ppermute | solution.py:822
  36.5 19.5 %collective-permute-start.6 = (bf16[4,96,768]{2,1,0:T(8,128)(2,1)}, bf16[4,96,768]{2,1,0:T(8,128)(2,1)}, u32[]{:S(2)}, u32[]{:S(2)}) collective-permute-start(bf16[4,96,768]{2,1,0:T(8,128)(2,1)} %pack_line.1.refs_0_), channel_id=1, source_target_pairs={{0,16},{1,17},{2,18},{3,19},{4,20},{5,21},{6,22},{7,23},{8,24},{9,... | collective-permute-start | bytes 1769480 | tf_op jit(solution)/shard_map/ppermute | solution.py:822
  38.1 30.8 %collective-permute-start.7 = (bf16[4,96,768]{2,1,0:T(8,128)(2,1)}, bf16[4,96,768]{2,1,0:T(8,128)(2,1)}, u32[]{:S(2)}, u32[]{:S(2)}) collective-permute-start(bf16[4,96,768]{2,1,0:T(8,128)(2,1)} %pack_line.1.refs_0_), channel_id=1, source_target_pairs={{0,24},{1,25},{2,26},{3,27},{4,28},{5,29},{6,30},{7,31},{8,16},{9,... | collective-permute-start | bytes 1769480 | tf_op jit(solution)/shard_map/ppermute | solution.py:822
  40.6 34.0 %collective-permute-start.5 = (bf16[512,768]{1,0:T(8,128)(2,1)S(1)}, bf16[512,768]{1,0:T(8,128)(2,1)S(1)}, u32[]{:S(2)}, u32[]{:S(2)}) collective-permute-start(bf16[512,768]{1,0:T(8,128)(2,1)S(1)} %constant_dynamic-slice_fusion.1), channel_id=1, source_target_pairs={{0,0},{1,2},{2,1},{3,3},{4,4},{5,6},{6,5},{7,7},{8,8},{9,10},{10,9... | collective-permute-start | bytes 2359304 | tf_op jit(solution)/shard_map/ppermute | solution.py:821
  56.1 18.6 %collective-permute-start.10 = (bf16[4,96,768]{2,1,0:T(8,128)(2,1)}, bf16[4,96,768]{2,1,0:T(8,128)(2,1)}, u32[]{:S(2)}, u32[]{:S(2)}) collective-permute-start(bf16[4,96,768]{2,1,0:T(8,128)(2,1)} %collective-permute-done.6.refs_2_), channel_id=1, source_target_pairs={{0,4},{1,5},{2,6},{3,7},{4,0},{5,1},{6,2},{7,3},{8,12},{9,13},{10,... | collective-permute-start | bytes 1769480 | tf_op jit(solution)/shard_map/ppermute | solution.py:824
  68.9 5.7 %collective-permute-start.11 = (bf16[4,96,768]{2,1,0:T(8,128)(2,1)}, bf16[4,96,768]{2,1,0:T(8,128)(2,1)}, u32[]{:S(2)}, u32[]{:S(2)}) collective-permute-start(bf16[4,96,768]{2,1,0:T(8,128)(2,1)} %collective-permute-done.7.refs_3_), channel_id=1, source_target_pairs={{0,4},{1,5},{2,6},{3,7},{4,0},{5,1},{6,2},{7,3},{8,12},{9,13},{10,... | collective-permute-start | bytes 1769480 | tf_op jit(solution)/shard_map/ppermute | solution.py:824
  71.9 3.2 %copy-start.12 = (bf16[768,768]{1,0:T(8,128)(2,1)}, bf16[768,768]{1,0:T(8,128)(2,1)S(1)}, u32[]{:S(2)}) copy-start(bf16[768,768]{1,0:T(8,128)(2,1)S(1)} %collective-permute-done.4.nb_ref) | copy-start | bytes 3538948
  71.9 2.7 collective-permute-start.9
  71.9 3.2 %collective-permute-start.8 = (bf16[4,96,768]{2,1,0:T(8,128)(2,1)}, bf16[4,96,768]{2,1,0:T(8,128)(2,1)}, u32[]{:S(2)}, u32[]{:S(2)}) collective-permute-start(bf16[4,96,768]{2,1,0:T(8,128)(2,1)} %pack_line.1.refs_0_), channel_id=1, source_target_pairs={{0,4},{1,5},{2,6},{3,7},{4,0},{5,1},{6,2},{7,3},{8,12},{9,13},{10,... | collective-permute-start | bytes 1769480 | tf_op jit(solution)/shard_map/ppermute | solution.py:824
  74.6 0.9 copy-start.13
  189.9 9.4 %collective-permute-start.12 = (bf16[4,3,96,768]{3,2,1,0:T(8,128)(2,1)}, bf16[4,3,96,768]{3,2,1,0:T(8,128)(2,1)S(1)}, u32[]{:S(2)}, u32[]{:S(2)}) collective-permute-start(bf16[4,3,96,768]{3,2,1,0:T(8,128)(2,1)} %get-tuple-element.124), channel_id=1, source_target_pairs={{0,4},{1,5},{2,6},{3,7},{4,0},{5,1},{6,2},{7,3},{8,12},{9,13},{10,... | collective-permute-start | bytes 5308424 | tf_op jit(solution)/shard_map/ppermute | solution.py:874
  190.2 9.1 %copy-start.2 = (bf16[4,3,96,768]{3,2,1,0:T(8,128)(2,1)S(1)}, bf16[4,3,96,768]{3,2,1,0:T(8,128)(2,1)}, u32[]{:S(2)}) copy-start(bf16[4,3,96,768]{3,2,1,0:T(8,128)(2,1)} %get-tuple-element.123) | copy-start | bytes 5308420
  199.8 7.9 %copy-start.6 = (f32[6,768]{1,0:T(8,128)S(1)}, f32[6,768]{1,0:T(8,128)}, u32[]{:S(2)}) copy-start(f32[6,768]{1,0:T(8,128)} %get-tuple-element.132) | copy-start | bytes 55300
  199.8 7.9 %copy-start.7 = (f32[4,768]{1,0:T(4,128)S(1)}, f32[4,768]{1,0:T(4,128)}, u32[]{:S(2)}) copy-start(f32[4,768]{1,0:T(4,128)} %get-tuple-element.133) | copy-start | bytes 36868
  199.8 7.9 %copy-start.8 = (f32[2,768]{1,0:T(2,128)S(1)}, f32[2,768]{1,0:T(2,128)}, u32[]{:S(2)}) copy-start(f32[2,768]{1,0:T(2,128)} %get-tuple-element.131) | copy-start | bytes 18436
  199.9 37.3 %collective-permute-start.13 = (bf16[768,768]{1,0:T(8,128)(2,1)}, bf16[768,768]{1,0:T(8,128)(2,1)S(1)}, u32[]{:S(2)}, u32[]{:S(2)}) collective-permute-start(bf16[768,768]{1,0:T(8,128)(2,1)} %get-tuple-element.138), channel_id=1, source_target_pairs={{0,1},{1,0},{2,3},{3,2},{4,5},{5,4},{6,7},{7,6},{8,9},{9,8},{10,11... | collective-permute-start | bytes 3538952 | tf_op jit(solution)/shard_map/ppermute | solution.py:881
  201.4 35.8 %collective-permute-start.14 = (bf16[512,768]{1,0:T(8,128)(2,1)}, bf16[512,768]{1,0:T(8,128)(2,1)S(1)}, u32[]{:S(2)}, u32[]{:S(2)}) collective-permute-start(bf16[512,768]{1,0:T(8,128)(2,1)} %get-tuple-element.139), channel_id=1, source_target_pairs={{0,0},{1,2},{2,1},{3,3},{4,4},{5,6},{6,5},{7,7},{8,8},{9,10},{10,9... | collective-permute-start | bytes 2359304 | tf_op jit(solution)/shard_map/ppermute | solution.py:882
  204.3 32.9 %collective-permute-start.15 = (bf16[3,96,768]{2,1,0:T(8,128)(2,1)}, bf16[3,96,768]{2,1,0:T(8,128)(2,1)}, u32[]{:S(2)}, u32[]{:S(2)}) collective-permute-start(bf16[3,96,768]{2,1,0:T(8,128)(2,1)} %get-tuple-element.194), channel_id=1, source_target_pairs={{0,8},{1,9},{2,10},{3,11},{4,12},{5,13},{6,14},{7,15},{8,0},{9,1},... | collective-permute-start | bytes 1327112 | tf_op jit(solution)/shard_map/ppermute | solution.py:880
  205.7 31.5 %collective-permute-start.16 = (bf16[3,96,768]{2,1,0:T(8,128)(2,1)S(1)}, bf16[3,96,768]{2,1,0:T(8,128)(2,1)}, u32[]{:S(2)}, u32[]{:S(2)}) collective-permute-start(bf16[3,96,768]{2,1,0:T(8,128)(2,1)S(1)} %get-tuple-element.193), channel_id=1, source_target_pairs={{0,16},{1,17},{2,18},{3,19},{4,20},{5,21},{6,22},{7,23},{8,24},{9,... | collective-permute-start | bytes 1327112 | tf_op jit(solution)/shard_map/ppermute | solution.py:880
  206.3 30.9 %collective-permute-start.17 = (bf16[3,96,768]{2,1,0:T(8,128)(2,1)S(1)}, bf16[3,96,768]{2,1,0:T(8,128)(2,1)}, u32[]{:S(2)}, u32[]{:S(2)}) collective-permute-start(bf16[3,96,768]{2,1,0:T(8,128)(2,1)S(1)} %get-tuple-element.192), channel_id=1, source_target_pairs={{0,24},{1,25},{2,26},{3,27},{4,28},{5,29},{6,30},{7,31},{8,16},{9,... | collective-permute-start | bytes 1327112 | tf_op jit(solution)/shard_map/ppermute | solution.py:880
  208.8 27.8 %all-to-all-start = ((f32[32,1,288]{2,1,0:T(1,128)}), f32[32,1,288]{2,1,0:T(1,128)S(1)}, u32[]{:S(2)}, u32[]{:S(2)}) async-start(f32[32,1,288]{2,1,0:T(1,128)} %copy.90), calls=%async_computation | async-start | bytes 98304 | tf_op jit(solution)/shard_map/all_to_all | solution.py:887
  237.2 0.9 copy-start.3
  241.0 56.1 %copy-start.1 = (f32[768,768]{1,0:T(8,128)S(1)}, f32[768,768]{1,0:T(8,128)}, u32[]{:S(2)}) copy-start(f32[768,768]{1,0:T(8,128)} %input_own.1) | copy-start | bytes 7077892
  241.0 7.1 %collective-permute-start.18 = (bf16[96,576]{1,0:T(8,128)(2,1)}, bf16[96,576]{1,0:T(8,128)(2,1)}, u32[]{:S(2)}, u32[]{:S(2)}) collective-permute-start(bf16[96,576]{1,0:T(8,128)(2,1)} %get-tuple-element.150), channel_id=1, source_target_pairs={{0,1},{1,0},{2,3},{3,2},{4,5},{5,4},{6,7},{7,6},{8,9},{9,8},{10,11... | collective-permute-start | bytes 331784 | tf_op jit(solution)/shard_map/ppermute | solution.py:893
  242.6 12.7 %collective-permute-start.19 = (bf16[96,576]{1,0:T(8,128)(2,1)}, bf16[96,576]{1,0:T(8,128)(2,1)}, u32[]{:S(2)}, u32[]{:S(2)}) collective-permute-start(bf16[96,576]{1,0:T(8,128)(2,1)} %get-tuple-element.151), channel_id=1, source_target_pairs={{0,2},{1,3},{2,0},{3,1},{4,6},{5,7},{6,4},{7,5},{8,10},{9,11},{10,... | collective-permute-start | bytes 331784 | tf_op jit(solution)/shard_map/ppermute | solution.py:893
  245.1 10.3 %collective-permute-start.20 = (bf16[96,576]{1,0:T(8,128)(2,1)}, bf16[96,576]{1,0:T(8,128)(2,1)}, u32[]{:S(2)}, u32[]{:S(2)}) collective-permute-start(bf16[96,576]{1,0:T(8,128)(2,1)} %get-tuple-element.152), channel_id=1, source_target_pairs={{0,3},{1,2},{2,1},{3,0},{4,7},{5,6},{6,5},{7,4},{8,11},{9,10},{10,... | collective-permute-start | bytes 331784 | tf_op jit(solution)/shard_map/ppermute | solution.py:893
  258.1 15.5 %collective-permute-start.21 = (bf16[96,1728]{1,0:T(8,128)(2,1)}, bf16[96,1728]{1,0:T(8,128)(2,1)}, u32[]{:S(2)}, u32[]{:S(2)}) collective-permute-start(bf16[96,1728]{1,0:T(8,128)(2,1)} %get-tuple-element.159), channel_id=1, source_target_pairs={{0,1},{1,0},{2,3},{3,2},{4,5},{5,4},{6,7},{7,6},{8,9},{9,8},{10,11... | collective-permute-start | bytes 995336 | tf_op jit(solution)/shard_map/ppermute | solution.py:893
  260.0 27.0 %collective-permute-start.22 = (bf16[96,1728]{1,0:T(8,128)(2,1)}, bf16[96,1728]{1,0:T(8,128)(2,1)}, u32[]{:S(2)}, u32[]{:S(2)}) collective-permute-start(bf16[96,1728]{1,0:T(8,128)(2,1)} %get-tuple-element.160), channel_id=1, source_target_pairs={{0,2},{1,3},{2,0},{3,1},{4,6},{5,7},{6,4},{7,5},{8,10},{9,11},{10,... | collective-permute-start | bytes 995336 | tf_op jit(solution)/shard_map/ppermute | solution.py:893
  261.0 26.0 %collective-permute-start.23 = (bf16[96,1728]{1,0:T(8,128)(2,1)}, bf16[96,1728]{1,0:T(8,128)(2,1)}, u32[]{:S(2)}, u32[]{:S(2)}) collective-permute-start(bf16[96,1728]{1,0:T(8,128)(2,1)} %get-tuple-element.161), channel_id=1, source_target_pairs={{0,3},{1,2},{2,1},{3,0},{4,7},{5,6},{6,5},{7,4},{8,11},{9,10},{10,... | collective-permute-start | bytes 995336 | tf_op jit(solution)/shard_map/ppermute | solution.py:893
  289.8 14.4 %all-to-all-start.1 = ((f32[32,1,1]{2,1,0:T(1,128)}), f32[32,1,1]{2,1,0:T(1,128)S(1)}, u32[]{:S(2)}, u32[]{:S(2)}) async-start(f32[32,1,1]{2,1,0:T(1,128)} %bitcast.51), calls=%async_computation.2 | async-start | bytes 32768 | tf_op jit(solution)/shard_map/all_to_all | solution.py:906
  304.2 0.6 copy-start.5
Sparse Core Ops, SparseCore 0:
  11.4 97.3 all-gather.2
  152.3 97.8 reduce-scatter.1
